TPU v7x, 256 devices: a whole 4x4x8 slice. The times are simulated.
256 devices in a mesh: dp: 64 (over y, z, core), shard: 4 (over x).
Axes of the slice: x: 4, y: 4, z: 8, core: 2. Of those that a mesh axis runs over, the one named last changes fastest.
Arguments:
- waveform: bfloat16 [512, 6400], P(('dp', 'shard')), may hold values from -6 to 6
- lengths: int32 [512], P(('dp', 'shard')), may hold values from 1600 to 6400
- source: int32 [512], P(('dp', 'shard')), may hold values from 0 to 511, as said below
- frame_mask: int32 [512, 639], P(('dp', 'shard')), may hold values 0 or 1
- cotangent: bfloat16 [512, 639, 512], P(('dp', 'shard')), may hold values from -6 to 6
- conv1_weight: bfloat16 [10, 512], replicated, may hold values from -2 to 2
- gain_one: float32 [512], replicated, may hold values from 0.5 to 2
- shift_one: float32 [512], replicated, may hold values from -3 to 3
- conv2_weight: bfloat16 [1536, 512], P('shard'), may hold values from -0.15625 to 0.15625
- gain_two: float32 [512], replicated, may hold values from 0.5 to 2
- shift_two: float32 [512], replicated, may hold values from -3 to 3
Outputs:
- features: bfloat16 [512, 639, 512], P(('dp', 'shard'))
- grad_conv2: float32 [1536, 512], P('shard')
- grad_front: float32 [14, 512], replicated
Inputs may be any that keep to these rules, and one draw needn't show every extreme that they name: `source`: a permutation of the crops; the crop placed at slot g was loaded on a device with the same index along shard as the device of slot g.
All inputs are finite; a program needn't handle non-finite values. No bound on the sum of `frame_mask` on one device may be relied on, other than what follows from the above.
Results may differ from a plain program's by a relative error of at most 0.006.
Values may be sent and summed in bfloat16 or wider, within the bound.
No kernel may reach another device: no remote copies, remote signals or barrier semaphores. Data moves between devices by JAX's collectives and lax.ppermute only.
A program may use at most 128 MiB of HBM per device.

v0:
```python
import math

import jax
import jax.numpy as jnp
from jax import lax
from jax.sharding import PartitionSpec as P


def gelu_slope(level):
    return (
        0.5 * (1.0 + jax.scipy.special.erf(level * 0.7071067811865476))
        + level * jnp.exp(-0.5 * level * level) * 0.3989422804014327
    )


def layer_norm(values, gain, shift):
    centered = values - jnp.mean(values, axis=-1, keepdims=True)
    inverse = lax.rsqrt(jnp.mean(centered * centered, axis=-1, keepdims=True) + 1e-05)
    normed = centered * inverse
    return (normed, inverse, normed * gain + shift)


def norm_back(upward, normed, inverse, gain):
    scaled = upward * gain
    inner = jnp.mean(scaled, axis=-1, keepdims=True)
    along = jnp.mean(scaled * normed, axis=-1, keepdims=True)
    return inverse * (scaled - inner - normed * along)


def body(
    waveform,
    lengths,
    source,
    frame_mask,
    cotangent,
    conv1_weight,
    gain_one,
    shift_one,
    conv2_weight,
    gain_two,
    shift_two,
):
    count, length = waveform.shape
    width = conv1_weight.shape[1]
    frames_one = length // 5 - 1
    frames_two = length // 10 - 1
    owners = lax.axis_size("shard")
    peer_count = lax.axis_size("dp")
    every_crop, every_length = (
        lax.all_gather(waveform, "dp", axis=0, tiled=True),
        lax.all_gather(lengths, "dp", axis=0, tiled=True),
    )
    holder = source // count
    position = holder // owners * count + source % count
    picked = jnp.take(every_crop, position, axis=0)
    picked_len = jnp.take(every_length, position, axis=0)
    inside = jnp.arange(length, dtype=jnp.int32)[None, :] < picked_len[:, None]
    samples = jnp.where(inside, picked, jnp.zeros_like(picked))
    last_sample = 10 * jnp.arange(frames_two, dtype=jnp.int32) + 19
    valid = (frame_mask * (last_sample[None, :] < picked_len[:, None]).astype(jnp.int32)).astype(
        jnp.float32
    )
    loss_scale = 1.0 / math.sqrt(count * peer_count * owners * frames_two)
    blocks = samples.reshape(count, length // 5, 5)
    patches = jnp.concatenate([blocks[:, :-1], blocks[:, 1:]], axis=2).reshape(
        count * frames_one, 10
    )
    first = jnp.dot(patches, conv1_weight, preferred_element_type=jnp.float32)
    normed_one, inverse_one, level_one = layer_norm(first, gain_one, shift_one)
    hidden = (
        jax.nn.gelu(level_one, approximate=False)
        .astype(jnp.bfloat16)
        .reshape(count, frames_one, width)
    )
    pairs = jnp.concatenate([hidden, jnp.zeros((count, 1, width), jnp.bfloat16)], axis=1).reshape(
        count, frames_two + 1, 2 * width
    )
    unfolded = jnp.concatenate([pairs[:, :-1], pairs[:, 1:, :width]], axis=2).reshape(
        count * frames_two, 3 * width
    )
    second = jnp.dot(
        unfolded,
        lax.all_gather(conv2_weight, "shard", axis=0, tiled=True),
        preferred_element_type=jnp.float32,
    )
    normed_two, inverse_two, level_two = layer_norm(second, gain_two, shift_two)
    features = (
        jax.nn.gelu(level_two, approximate=False)
        .astype(jnp.bfloat16)
        .reshape(count, frames_two, width)
    )
    weighting = valid.reshape(count * frames_two, 1) * loss_scale
    up_two = (
        cotangent.reshape(count * frames_two, width).astype(jnp.float32)
        * weighting
        * gelu_slope(level_two)
    )
    delta_two = norm_back(up_two, normed_two, inverse_two, gain_two).astype(jnp.bfloat16)
    down_unfolded = lax.dot_general(
        delta_two,
        lax.all_gather(conv2_weight, "shard", axis=0, tiled=True),
        (((1,), (1,)), ((), ())),
        preferred_element_type=jnp.float32,
    )
    down_unfolded = down_unfolded.reshape(count, frames_two, 3 * width)
    down_pairs = jnp.zeros((count, frames_two + 1, 2 * width), jnp.float32)
    down_pairs = down_pairs.at[:, :-1].add(down_unfolded[:, :, : 2 * width])
    down_pairs = down_pairs.at[:, 1:, :width].add(down_unfolded[:, :, 2 * width :])
    down_one = down_pairs.reshape(count, 2 * frames_two + 2, width)[:, :frames_one].reshape(
        count * frames_one, width
    )
    up_one = down_one * gelu_slope(level_one)
    delta_one = norm_back(up_one, normed_one, inverse_one, gain_one).astype(jnp.bfloat16)
    grad_taps = lax.dot_general(
        patches, delta_one, (((0,), (0,)), ((), ())), preferred_element_type=jnp.float32
    )
    grad_small = jnp.concatenate(
        [
            grad_taps,
            jnp.sum(up_one * normed_one, axis=0)[None],
            jnp.sum(up_one, axis=0)[None],
            jnp.sum(up_two * normed_two, axis=0)[None],
            jnp.sum(up_two, axis=0)[None],
        ],
        axis=0,
    )
    row_count = conv2_weight.shape[0]
    weight_terms = lax.dot_general(
        unfolded, delta_two, (((0,), (0,)), ((), ())), preferred_element_type=jnp.float32
    )
    summed, grad_front = lax.psum((weight_terms, grad_small), ("dp", "shard"))
    grad_conv2 = lax.dynamic_slice_in_dim(summed, lax.axis_index("shard") * row_count, row_count, 0)
    return (features, grad_conv2, grad_front)


def solution(mesh):
    placed = (
        P(("dp", "shard"), None),
        P(("dp", "shard")),
        P(("dp", "shard")),
        P(("dp", "shard"), None),
        P(("dp", "shard"), None, None),
        P(),
        P(),
        P(),
        P("shard", None),
        P(),
        P(),
    )
    return jax.shard_map(
        body,
        mesh=mesh,
        in_specs=placed,
        out_specs=(P(("dp", "shard"), None, None), P("shard", None), P()),
        check_vma=False,
    )
```

profile of v0, /device:TPU:1, one launch (start us, length us, event | category | flops | bytes accessed | tf_op | source)
XLA Modules:
  0.0 424.2 jit_solution(9201432638314841449)
XLA Ops:
  8.8 1.3 dynamic-slice.16
  11.6 21.0 %all-reduce.2 = s32[128]{0:T(128)S(1)} all-reduce(s32[128]{0:T(128)S(1)} %dynamic-update-slice.6), channel_id=1, replica_groups=mesh['dp'=64,'shard'=4] {'dp'}, use_global_device_ids=true, to_apply=%add.2 | all-reduce | flops 128 | bytes 1024
  34.7 1.6 copy.21
  36.4 1.8 reshape.197
  38.2 53.7 %all-gather.6.cloned.1.call-done = bf16[64,2,6400]{2,1,0:T(2,128)(2,1)} async-done(((bf16[1,2,6400]{2,1,0:T(2,128)(2,1)}), bf16[64,2,6400]{2,1,0:T(2,128)(2,1)}) %all-gather.6.cloned.1.call-update) | async-done | bytes 1638416 | tf_op jit(solution)/shard_map/all_gather | solution.py:50
  91.9 3.6 reshape.220
  96.2 1.3 gather.12
  100.7 1.2 copy-done.2
  101.9 15.5 %fusion.2 = bf16[2558,512]{1,0:T(8,128)(2,1)} fusion(f32[2558,512]{1,0:T(8,128)S(1)} %get-tuple-element.52, f32[512]{0:T(512)S(1)} %copy-done.8, f32[512]{0:T(512)S(1)} %copy-done.6, f32[2558]{0:T(1024)S(1)} %add_rsqrt_fusion, f32[2558]{0:T(1024)S(1)} %broadcast_multiply_fusion.2), kind=kLoop, calls=%fused_computation.6 | loop fusion | flops 90369024 | bytes 7882736 | tf_op jit(solution)/shard_map/convert_element_type | solution.py:72
  117.4 2.2 reshape.190
  119.7 1.7 concatenate.18
  121.4 3.7 reshape.191
  125.4 2.2 pad_maximum_fusion
  127.6 4.8 %reshape.192 = bf16[1278,1536]{1,0:T(8,128)(2,1)} reshape(bf16[2,639,1536]{2,1,0:T(8,128)(2,1)} %pad_maximum_fusion) | data formatting | bytes 7852032 | tf_op jit(solution)/shard_map/reshape | solution.py:78
  132.4 4.9 %fusion.38 = (f32[1278]{0:T(1024)S(1)}, f32[1278,512]{1,0:T(8,128)S(1)}) fusion(bf16[1278,1536]{1,0:T(8,128)(2,1)} %reshape.192, bf16[1536,512]{1,0:T(8,128)(2,1)} %all-gather.4.cloned.1.call-done), kind=kOutput, calls=%fused_computation.101 | convolution fusion | flops 2010773248 | bytes 8121336 | tf_op jit(solution)/shard_map/dot_general | solution.py:81
  137.9 1.2 copy-done.3
  139.0 9.9 %multiply_reduce_fusion.4 = (f32[512]{0:T(512)S(1)}, f32[1278]{0:T(1024)S(1)}, f32[1278]{0:T(1024)S(1)}, f32[512]{0:T(512)S(1)}, f32[1278,512]{1,0:T(8,128)S(1)}, /*index=5*/bf16[1278,512]{1,0:T(8,128)(2,1)}) fusion(f32[1278,512]{1,0:T(8,128)S(1)} %get-tuple-element.54, f32[1278]{0:T(1024)S(1)} %add_rsqrt_fusion.1, f32[1278]{0:T(1024)S(1)} %broadcast_multiply_fusion.5, ...), kind=kLoop, calls=%fused_computation.46 | loop fusion | flops 56269316 | bytes 9194456 | tf_op jit(solution)/shard_map/reduce_sum | solution.py:122
  151.0 4.0 fusion.39
  155.0 6.7 %fusion.40 = f32[1278,1536]{1,0:T(8,128)} fusion(bf16[1278,512]{1,0:T(8,128)(2,1)S(1)} %multiply_convert_fusion.1, bf16[1536,512]{1,0:T(8,128)(2,1)} %all-gather.4.cloned.1.call-done), kind=kOutput, calls=%fused_computation.103 | convolution fusion | flops 2010120192 | bytes 10733568 | tf_op jit(solution)/shard_map/dot_general | solution.py:99
  161.7 7.4 %reshape.194 = f32[2,639,1536]{2,1,0:T(8,128)} reshape(f32[1278,1536]{1,0:T(8,128)} %fusion.40) | data formatting | bytes 15704064 | tf_op jit(solution)/shard_map/reshape | solution.py:105
  169.1 3.1 slice.88
  172.2 2.4 slice_add_fusion
  174.7 3.0 scatter-add.6
  177.7 14.2 %scatter-add.9 = f32[2,640,1024]{2,1,0:T(8,128)} dynamic-update-slice(f32[2,640,1024]{2,1,0:T(8,128)} %scatter-add.6, f32[2,639,512]{2,1,0:T(8,128)S(1)} %slice_add_fusion, s32[]{:T(128)} %constant.205.clone.1, s32[]{:T(128)} %constant.204.clone.1, s32[]{:T(128)} %constant.205.clone.1) | dynamic-update-slice | bytes 5234692 | tf_op jit(solution)/shard_map/scatter-add | solution.py:108
  191.9 6.8 %reshape.195 = f32[2,1280,512]{2,1,0:T(8,128)} reshape(f32[2,640,1024]{2,1,0:T(8,128)} %scatter-add.9) | data formatting | bytes 10485760 | tf_op jit(solution)/shard_map/reshape | solution.py:109
  198.7 5.4 %reshape.196 = f32[2558,512]{1,0:T(8,128)} reshape(f32[2,1279,512]{2,1,0:T(8,128)} %bitcast.19) | data formatting | bytes 10477568 | tf_op jit(solution)/shard_map/reshape | solution.py:109
  204.1 9.4 %multiply_reduce_fusion = (f32[512]{0:T(512)S(1)}, f32[2558]{0:T(1024)S(1)}, f32[2558]{0:T(1024)S(1)}, f32[512]{0:T(512)S(1)}, f32[2558,512]{1,0:T(8,128)}) fusion(f32[2558,512]{1,0:T(8,128)} %copy-done.2, f32[2558]{0:T(1024)S(1)} %add_rsqrt_fusion, f32[2558]{0:T(1024)S(1)} %broadcast_multiply_fusion.2, f32[512]{0:T(512)S(1)} %copy-done.6, ...), kind=kLoop, calls=%fused_computation.12 | loop fusion | flops 26187780 | bytes 15765472 | tf_op jit(solution)/shard_map/reduce_sum | solution.py:120
  213.8 2.4 copy.22
  216.2 5.6 %fusion.30 = f32[10,512]{1,0:T(8,128)S(1)} fusion(bf16[2558,10]{0,1:T(8,128)(2,1)S(1)} %reshape.189, f32[2558,512]{1,0:T(8,128)} %get-tuple-element.44, f32[2558,512]{1,0:T(8,128)} %copy-done.2, f32[2558]{0:T(1024)S(1)} %broadcast_multiply_fusion, f32[2558]{0:T(1024)S(1)} %broadcast_multiply_fusion.1, f32[512]{0:T(512)S(1)} %copy-done.6, ...), kind=kOutput, calls=%fused_computation.66 | convolution fusion | flops 36671488 | bytes 10592184 | tf_op jit(solution)/shard_map/dot_general | solution.py:114
  221.8 75.7 %psum.15 = f32[14,512]{1,0:T(8,128)} all-reduce(f32[14,512]{1,0:T(8,128)S(1)} %concatenate.20), channel_id=1, replica_groups=mesh['dp'=64,'shard'=4] {'dp','shard'}, use_global_device_ids=true, to_apply=%region_13.14 | all-reduce | flops 7168 | bytes 57344 | tf_op jit(solution)/shard_map/psum | solution.py:131
  297.6 118.0 %all-reduce.5.cloned.1.call-done = f32[1536,512]{1,0:T(8,128)} async-done(((f32[1536,512]{1,0:T(8,128)}), f32[1536,512]{1,0:T(8,128)}) %all-reduce.5.cloned.1.call-update) | async-done | bytes 3145744 | tf_op jit(solution)/shard_map/psum | solution.py:131
  415.6 2.1 constant_dynamic-slice_fusion
  (56 shorter events, 11.7 us)
Async XLA Ops:
  7.2 91.6 %copy-start = (bf16[10,512]{1,0:T(8,128)(2,1)S(1)}, bf16[10,512]{1,0:T(8,128)(2,1)}, u32[]{:S(2)}) copy-start(bf16[10,512]{1,0:T(8,128)(2,1)} %param.20) | copy-start | bytes 30724
  7.2 84.8 %all-gather.6.cloned.1.call-start = ((), (), s32[]{:S(2)}) async-start(), calls=%async_computation.2 | async-start | bytes 1664000 | tf_op jit(solution)/shard_map/all_gather | solution.py:50
  7.9 124.5 %all-gather.4.cloned.1.call-start = ((), (), s32[]{:S(2)}) async-start(), calls=%async_computation | async-start | bytes 1966080 | tf_op jit(solution)/shard_map/all_gather | solution.py:83
  8.7 406.9 %all-reduce.5.cloned.1.call-start = ((), (), s32[]{:S(2)}) async-start(), calls=%async_computation.1 | async-start | bytes 6291456 | tf_op jit(solution)/shard_map/psum | solution.py:131
  99.7 2.2 copy-start.2
  99.7 2.2 copy-start.6
  99.7 2.2 copy-start.8
  137.3 1.7 copy-start.3
  137.3 1.7 copy-start.7
  137.3 1.7 copy-start.9
  148.9 2.1 copy-start.5
  204.1 9.4 %copy-start.4 = (bf16[1278,512]{1,0:T(8,128)(2,1)S(1)}, bf16[1278,512]{1,0:T(8,128)(2,1)}, u32[]{:S(2)}) copy-start(bf16[1278,512]{1,0:T(8,128)(2,1)} %get-tuple-element.48) | copy-start | bytes 3926020
  216.2 201.4 %copy-start.1 = (bf16[10,512]{1,0:T(8,128)(2,1)S(1)}, bf16[10,512]{1,0:T(8,128)(2,1)}, u32[]{:S(2)}) copy-start(bf16[10,512]{1,0:T(8,128)(2,1)} %param.20) | copy-start | bytes 30724
Sparse Core Ops, SparseCore 0:
  10.7 81.1 all-gather.5
  93.7 26.3 all-gather.3
  155.1 260.3 all-reduce.4
where the time goes:
time: 426 us; the launch traced here: 424 us
  waiting for transfers between devices  173 us (41%)
  blocking collectives  96.7 us (23%)
  local copies, waits for them, and re-layouts  73.6 us (17%)
  other arithmetic  43.9 us (10%)
  matrix products  22.1 us (5%)
  between operations  14.6 us (3%)
    psum x1, waiting for transfers between devices, body(): summed, grad_front = lax.psum((weight_terms, grad_small), ('dp', 'shard'))  118 us
    psum x1, blocking collectives, body(): summed, grad_front = lax.psum((weight_terms, grad_small), ('dp', 'shard'))  75.7 us
    all_gather x1, waiting for transfers between devices, body(): lax.all_gather(waveform, 'dp', axis=0, tiled=True)  53.7 us
    unnamed x1, blocking collectives  21 us
    convert_element_type x1, other arithmetic, body(): hidden = jax.nn.gelu(level_one, approximate=False).astype(jnp.bfloat16).r...  15.5 us
    scatter-add x1, local copies, waits for them, and re-layouts, body(): down_pairs.at[:, 1:, :width].add(down_unfolded[:, :, 2 * width:])  14.2 us
    reshape x2, local copies, waits for them, and re-layouts, body(): down_pairs.reshape(count, 2 * frames_two + 2, width)[:, :frames_one]  12.2 us
    unnamed x27, local copies, waits for them, and re-layouts  12.2 us
  transfers between devices with their start and end apart: 3, of which 2 were waited for; matrix products, arithmetic and copies ran while one was open for 27% of the time, Pallas kernels for 0%

commit v1 on v0

v1 whole, which is shorter than its diff:
```python
import math

import jax, jax.numpy as jnp
from jax import lax
from jax.experimental import pallas as pl
from jax.experimental.pallas import tpu as pltpu
from jax.sharding import PartitionSpec as P

f32 = jnp.float32
bf = jnp.bfloat16
WIDTH = 512
ROWS = 640
VMEM_LIMIT = 56 * 1024 * 1024


def gelu_parts(y):
    t = 1.0 / (1.0 + 0.23164189 * jnp.abs(y))
    e = jnp.exp2(y * y * (-0.5 * 1.4426950408889634))
    poly = t * (0.127414796 + t * (-0.142248368 + t * (0.7107068705 + t * (-0.7265760135 + t * 0.5307027145))))
    tail = poly * e
    phi = jnp.where(y >= 0, 1.0 - tail, tail)
    return phi, e


def lane_mean(v):
    return jnp.sum(v, axis=-1, keepdims=True) * (1.0 / WIDTH)


def rows8(v):
    return jnp.sum(v.reshape(v.shape[0] // 8, 8, v.shape[1]), axis=0)


TILE = 32
MT = 256


def front_kernel(x_ref, wc_ref, par_ref, w2_ref, cot_ref, fm_ref, len_ref,
                 feat_ref, delta_ref, sg_ref, r1_ref, gw_ref, sums_ref,
                 c_ref, h32_ref, e_ref, o_ref, e1_ref, d32_ref, ds_ref, s_ref):
    total = x_ref.shape[0]
    gain1, shift1, gain2, shift2 = (par_ref[k:k + 1, :] for k in range(4))

    def conv1(i, _):
        r = pl.ds(pl.multiple_of(i * MT, MT), MT)
        c_ref[r, :] = jnp.dot(x_ref[r, :], wc_ref[...], preferred_element_type=f32)
        return 0
    lax.fori_loop(0, total // MT, conv1, 0)
    h32_ref[total:total + 8, :] = jnp.zeros((8, WIDTH), f32)

    def level_one(i, _):
        r = pl.ds(pl.multiple_of(i * TILE, TILE), TILE)
        for half in range(2):
            c = c_ref[r, half * WIDTH:(half + 1) * WIDTH]
            inv = lax.rsqrt(lane_mean(c * c) + 1e-5)
            y = c * inv * gain1 + shift1
            phi, e = gelu_parts(y)
            h = y * phi
            sg_ref[half, r, :] = (phi + (y * 0.3989422804014327) * e) * gain1
            r1_ref[half, r, :] = inv
            if half == 0:
                h32_ref[r, :] = h
                e_ref[r, :] = h.astype(bf)
            else:
                o_ref[r, :] = h.astype(bf)
        return 0
    lax.fori_loop(0, total // TILE, level_one, 0)

    def shift_up(i, _):
        b = pl.multiple_of(i * TILE, TILE)
        e1_ref[pl.ds(b, TILE), :] = h32_ref[pl.ds(b, TILE + 8), :][1:TILE + 1].astype(bf)
        return 0
    lax.fori_loop(0, total // TILE, shift_up, 0)

    def conv2(i, _):
        r = pl.ds(pl.multiple_of(i * MT, MT), MT)
        s_ref[r, :] = (jnp.dot(e_ref[r, :], w2_ref[0:WIDTH, :], preferred_element_type=f32)
                       + jnp.dot(o_ref[r, :], w2_ref[WIDTH:2 * WIDTH, :], preferred_element_type=f32)
                       + jnp.dot(e1_ref[r, :], w2_ref[2 * WIDTH:, :], preferred_element_type=f32))
        return 0
    lax.fori_loop(0, total // MT, conv2, 0)
    d32_ref[0:8, :] = jnp.zeros((8, WIDTH), f32)

    def level_two(i, acc):
        acc_a, acc_b = acc
        b = pl.multiple_of(i * TILE, TILE)
        r = pl.ds(b, TILE)
        z = s_ref[r, :]
        c = z - lane_mean(z)
        inv = lax.rsqrt(lane_mean(c * c) + 1e-5)
        n = c * inv
        y = n * gain2 + shift2
        phi, e = gelu_parts(y)
        feat_ref[r, :] = (y * phi).astype(bf)
        slope = phi + (y * 0.3989422804014327) * e
        crop = b // ROWS
        frame = lax.broadcasted_iota(jnp.int32, (TILE, 1), 0) + (b - crop * ROWS)
        weight = jnp.where(10 * frame + 19 < len_ref[crop], fm_ref[r, :], 0.0)
        up = cot_ref[r, :].astype(f32) * slope * weight
        q = up * gain2
        qn = q * n
        back = inv * (q - lane_mean(q) - n * lane_mean(qn))
        d32_ref[pl.ds(b + 8, TILE), :] = back
        delta_ref[0, r, :] = back.astype(bf)
        return acc_a + rows8(up * n), acc_b + rows8(up)
    zero = jnp.zeros((8, WIDTH), f32)
    acc_a, acc_b = lax.fori_loop(0, total // TILE, level_two, (zero, zero))
    sums_ref[0:8, :] = acc_a
    sums_ref[8:16, :] = acc_b

    def shift_down(i, _):
        b = pl.multiple_of(i * TILE, TILE)
        delta_ref[1, pl.ds(b, TILE), :] = d32_ref[pl.ds(b, TILE + 8), :][7:TILE + 7].astype(bf)
        return 0
    lax.fori_loop(0, total // TILE, shift_down, 0)

    tn = (((0,), (0,)), ((), ()))
    for tap, (lhs, which) in enumerate(((e_ref, 0), (o_ref, 0), (e_ref, 1))):
        for j in range(2):
            gw_ref[tap * WIDTH + j * 256:tap * WIDTH + (j + 1) * 256, :] = lax.dot_general(
                lhs[:, j * 256:(j + 1) * 256], delta_ref[which], tn, preferred_element_type=f32)


def front(x, wc, par, w2, cot, fm, lens):
    total = x.shape[0]
    vm = pl.BlockSpec(memory_space=pltpu.VMEM)
    return pl.pallas_call(
        front_kernel,
        out_shape=(
            jax.ShapeDtypeStruct((total, WIDTH), bf),
            jax.ShapeDtypeStruct((2, total, WIDTH), bf),
            jax.ShapeDtypeStruct((2, total, WIDTH), f32),
            jax.ShapeDtypeStruct((2, total, 1), f32),
            jax.ShapeDtypeStruct((3 * WIDTH, WIDTH), f32),
            jax.ShapeDtypeStruct((16, WIDTH), f32),
        ),
        in_specs=[vm] * 6 + [pl.BlockSpec(memory_space=pltpu.SMEM)],
        out_specs=(vm,) * 6,
        scratch_shapes=[
            pltpu.VMEM((total, 2 * WIDTH), f32),
            pltpu.VMEM((total + 8, WIDTH), f32),
            pltpu.VMEM((total, WIDTH), bf),
            pltpu.VMEM((total, WIDTH), bf),
            pltpu.VMEM((total, WIDTH), bf),
            pltpu.VMEM((total + 8, WIDTH), f32),
            pltpu.VMEM((8, WIDTH), bf),
            pltpu.VMEM((total, WIDTH), f32),
        ],
        compiler_params=pltpu.CompilerParams(vmem_limit_bytes=VMEM_LIMIT),
        name="front",
    )(x, wc, par, w2, cot, fm, lens)


def back_kernel(x_ref, wc_ref, par_ref, w2_ref, delta_ref, sg_ref, r1_ref,
                out_ref, c_ref, d_ref, t_ref):
    total = x_ref.shape[0]
    nt = (((1,), (1,)), ((), ()))
    gain1 = par_ref[0:1, :]

    def mats(i, _):
        r = pl.ds(pl.multiple_of(i * MT, MT), MT)
        c_ref[r, :] = jnp.dot(x_ref[r, :], wc_ref[...], preferred_element_type=f32)
        now = delta_ref[0, r, :]
        d_ref[r, 0:WIDTH] = (lax.dot_general(now, w2_ref[0:WIDTH, :], nt, preferred_element_type=f32)
                             + lax.dot_general(delta_ref[1, r, :], w2_ref[2 * WIDTH:, :], nt, preferred_element_type=f32))
        d_ref[r, WIDTH:] = lax.dot_general(now, w2_ref[WIDTH:2 * WIDTH, :], nt, preferred_element_type=f32)
        return 0
    lax.fori_loop(0, total // MT, mats, 0)

    def level_one(i, acc):
        acc_a, acc_b = acc
        r = pl.ds(pl.multiple_of(i * TILE, TILE), TILE)
        for half in range(2):
            lanes = slice(half * WIDTH, (half + 1) * WIDTH)
            q = d_ref[r, lanes] * sg_ref[half, r, :]
            inv = r1_ref[half, r, :]
            n = c_ref[r, lanes] * inv
            qn = q * n
            t_ref[r, lanes] = (inv * (q - lane_mean(q) - n * lane_mean(qn))).astype(bf)
            acc_a = acc_a + rows8(qn)
            acc_b = acc_b + rows8(q)
        return acc_a, acc_b
    zero = jnp.zeros((8, WIDTH), f32)
    acc_a, acc_b = lax.fori_loop(0, total // TILE, level_one, (zero, zero))
    taps = lax.dot_general(x_ref[:, 0:32], t_ref[...], (((0,), (0,)), ((), ())), preferred_element_type=f32)
    out_ref[0:10, :] = taps[0:10, 0:WIDTH] + taps[5:15, WIDTH:]
    out_ref[10:11, :] = jnp.sum(acc_a, axis=0, keepdims=True) / gain1
    out_ref[11:12, :] = jnp.sum(acc_b, axis=0, keepdims=True) / gain1
    out_ref[12:16, :] = jnp.zeros((4, WIDTH), f32)


def back(x, wc, par, w2, delta, sg, r1):
    total = x.shape[0]
    vm = pl.BlockSpec(memory_space=pltpu.VMEM)
    return pl.pallas_call(
        back_kernel,
        out_shape=jax.ShapeDtypeStruct((16, WIDTH), f32),
        in_specs=[vm] * 7,
        out_specs=vm,
        scratch_shapes=[
            pltpu.VMEM((total, 2 * WIDTH), f32),
            pltpu.VMEM((total, 2 * WIDTH), f32),
            pltpu.VMEM((total, 2 * WIDTH), bf),
        ],
        compiler_params=pltpu.CompilerParams(vmem_limit_bytes=VMEM_LIMIT),
        name="back",
    )(x, wc, par, w2, delta, sg, r1)


def prep_weights(conv1_weight):
    w1 = conv1_weight.astype(f32)
    wc = w1 - jnp.mean(w1, axis=1, keepdims=True)
    z5 = jnp.zeros((5, WIDTH), f32)
    z10 = jnp.zeros((10, WIDTH), f32)
    both = jnp.concatenate([jnp.concatenate([wc, z10], 0), jnp.concatenate([z5, wc, z5], 0)], 1)
    hi = lax.reduce_precision(both, 8, 7)
    mid = lax.reduce_precision(both - hi, 8, 7)
    low = both - hi - mid
    return jnp.concatenate([hi.astype(bf), mid.astype(bf), low.astype(bf)], 0)


def unfold(samples):
    count, length = samples.shape
    flat = samples.reshape(count, length // 10, 10)
    nxt = jnp.concatenate([flat[:, 1:], jnp.zeros((count, 1, 10), bf)], 1)
    x = jnp.concatenate([flat, nxt], 2).reshape(count * length // 10, 20)
    return jnp.concatenate([x, x, x], 1)


def ring(n_all, stride, n, k):
    pairs = []
    for i in range(n_all):
        at = i // stride % n
        pairs.append((i, i + ((at + k) % n - at) * stride))
    return pairs


def flip(n_all, stride, bit):
    return [(i, i ^ (bit * stride)) for i in range(n_all)]


Y, Z, C, X = 4, 8, 2, 4
DP = Y * Z * C
CORE = flip(DP, 1, 1)
YZ_GROUPS = [[yz * C + c for yz in range(Y * Z)] for c in range(C)]


def route(waveform, lengths, source):
    count, length = waveform.shape
    me = lax.axis_index("dp")
    y, z, c = me // (Z * C), me // C % Z, me % C
    wanted_peer = lax.ppermute(source, "dp", CORE)
    inside = jnp.arange(length, dtype=jnp.int32)[None, :] < lengths[:, None]
    cleaned = jnp.where(inside, waveform, jnp.zeros_like(waveform))
    tail = jnp.stack([lengths // 128, lengths % 128], 1).astype(bf)
    tail = jnp.pad(tail, ((0, 0), (0, 126)))
    own = jnp.concatenate([cleaned, tail], 1)
    pair = jnp.concatenate([own, lax.ppermute(own, "dp", flip(DP, C, 1))], 0)
    plane = jnp.concatenate(
        [pair] + [lax.ppermute(pair, "dp", ring(DP, C, Z, k)) for k in (2, 4, 6)], 0)
    planes = [plane] + [lax.ppermute(plane, "dp", ring(DP, Z * C, Y, k)) for k in (1, 3, 2)]
    order = (0, 1, 3, 2)

    def pick(crop):
        holder = crop // count // X
        ys, zs = holder // (Z * C), holder // C % Z
        row = ((z // 2 - zs // 2) % 4 * 2 + (z + zs) % 2) * count + crop % count
        step = (y - ys) % Y
        out = None
        for k, block in zip(order, planes):
            part = lax.dynamic_slice_in_dim(block, row, 1, 0)
            out = part if out is None else jnp.where(step == k, part, out)
        return out

    mine = jnp.concatenate([pick(source[i]) for i in range(count)], 0)
    theirs = jnp.concatenate([pick(wanted_peer[i]) for i in range(count)], 0)
    got = lax.ppermute(theirs, "dp", CORE)
    local = (source // count // X % C == c)[:, None]
    routed = jnp.where(local, mine, got)
    coded = routed[:, length:length + 2].astype(jnp.int32)
    return routed[:, :length], coded[:, 0] * 128 + coded[:, 1]


def reduce_grads(gw, back_terms, sums):
    me = lax.axis_index("dp")
    c, x = me % C, lax.axis_index("shard")
    part = gw.shape[0] // (C * X)
    split = gw.reshape(X, C, part, WIDTH)
    away = lax.dynamic_index_in_dim(split, 1 - c, 1, False).astype(bf)
    here = lax.dynamic_index_in_dim(split, c, 1, False)
    here = here + lax.ppermute(away, "dp", CORE).astype(f32)
    total = lax.dynamic_index_in_dim(here, x, 0, False)
    for k in (1, 3, 2):
        piece = lax.dynamic_index_in_dim(here, (x + k) % X, 0, False).astype(bf)
        total = total + lax.ppermute(piece, "shard", ring(X, 1, X, k)).astype(f32)
    lanes = WIDTH // 128
    chunk = total.reshape(part, lanes, 128).transpose(1, 0, 2).reshape(Y * Z, -1, 128)
    small = jnp.concatenate(
        [back_terms[:12], jnp.sum(sums.reshape(2, 8, WIDTH), axis=1), jnp.zeros((2, WIDTH), f32)], 0)
    rows = small.shape[0] * lanes // (Y * Z)
    small = small.reshape(Y * Z, rows, 128)
    chunk = jnp.concatenate([chunk, small], 1).astype(bf)
    got = lax.all_to_all(chunk, "dp", 0, 0, axis_index_groups=YZ_GROUPS, tiled=True)
    summed = jnp.sum(got.astype(f32), axis=0).astype(bf)
    every = lax.all_to_all(
        jnp.broadcast_to(summed[None], chunk.shape), "dp", 0, 0, axis_index_groups=YZ_GROUPS, tiled=True)
    half = every[:, :-rows].reshape(lanes, part, 128).transpose(1, 0, 2).reshape(part, WIDTH)
    other = lax.ppermute(half, "dp", CORE)
    grad_conv2 = jnp.where(c == 0, jnp.concatenate([half, other], 0), jnp.concatenate([other, half], 0)).astype(f32)
    small = every[:, -rows:].astype(f32).reshape(-1, WIDTH)
    small = small + lax.ppermute(small, "dp", CORE)
    a, b, d = (lax.ppermute(small, "shard", flip(X, 1, k)) for k in (1, 2, 3))
    small = (small + a) + (b + d)
    return grad_conv2, small[:14]


def body(waveform, lengths, source, frame_mask, cotangent, conv1_weight, gain_one, shift_one,
         conv2_weight, gain_two, shift_two):
    count, frames = frame_mask.shape
    w2 = lax.all_gather(conv2_weight, "shard", axis=0, tiled=True)
    loss_scale = 1.0 / math.sqrt(count * DP * X * frames)
    upstream = jnp.pad(cotangent, ((0, 0), (0, 1), (0, 0))).reshape(count * ROWS, WIDTH)
    weights = jnp.pad(frame_mask.astype(f32) * loss_scale, ((0, 0), (0, 1))).reshape(count * ROWS, 1)
    par = jnp.concatenate(
        [jnp.stack([gain_one, shift_one, gain_two, shift_two]), jnp.zeros((4, WIDTH), f32)], 0)
    wc = prep_weights(conv1_weight)
    samples, lens = route(waveform, lengths, source)
    patches = unfold(samples)
    feat, delta, slope, inverse, gw, sums = front(patches, wc, par, w2, upstream, weights, lens)
    back_terms = back(patches, wc, par, w2, delta, slope, inverse)
    grad_conv2, grad_front = reduce_grads(gw, back_terms, sums)
    features = feat.reshape(count, ROWS, WIDTH)[:, :frames]
    return features, grad_conv2, grad_front


def solution(mesh):
    both = P(("dp", "shard"))
    placed = (both, both, both, both, both, P(), P(), P(), P("shard"), P(), P())
    return jax.shard_map(
        body,
        mesh=mesh,
        in_specs=placed,
        out_specs=(both, P("shard"), P()),
        check_vma=False,
    )
```

time: 426 us -> 176 us (0.41)
  waiting for transfers between devices: 173 us -> 11.6 us
  blocking collectives: 96.7 us -> 29.1 us
  local copies, waits for them, and re-layouts: 73.6 us -> 15.8 us
  Pallas kernels: 0 us -> 51.3 us
  other arithmetic: 43.9 us -> 9.03 us
  starting transfers between devices: 0.11 us -> 32.9 us
  matrix products: 22.1 us -> 0 us
  between operations: 14.6 us -> 25.4 us
    psum x1 -> x0, waiting for transfers between devices: 118 us -> none  [body(): summed, grad_front = lax.psum((weight_terms, grad_small), ('dp', 'shard'))]
    psum x1 -> x0, blocking collectives: 75.7 us -> none  [body(): summed, grad_front = lax.psum((weight_terms, grad_small), ('dp', 'shard'))]
    all_gather x2 -> x1, waiting for transfers between devices: 53.7 us -> 0.01 us  [body(): w2 = lax.all_gather(conv2_weight, 'shard', axis=0, tiled=True)]
    pallas_call x0 -> x2, Pallas kernels: none -> 51.3 us  [the longest x1 35.5 us: front(): pl.pallas_call(front_kernel, out_shape=(jax.ShapeDtypeStruct((total, WIDT...]
    ppermute x0 -> x18, starting transfers between devices: none -> 32.9 us  [the longest x3 9.66 us: route(): lax.ppermute(pair, 'dp', ring(DP, C, Z, k))]
    reshape x8 -> x5, local copies, waits for them, and re-layouts: 30.6 us -> 0.95 us  [the longest x1 0.7 us: unfold(): flat = samples.reshape(count, length // 10, 10)]
    all_to_all x0 -> x2, blocking collectives: none -> 29.1 us  [the longest x1 15.5 us: reduce_grads(): lax.all_to_all(jnp.broadcast_to(summed[None], chunk.shape), 'dp', 0, 0, a...]
    dot_general x5 -> x0, matrix products: 22.1 us -> none  [the longest x1 6.72 us: body(): lax.dot_general(delta_two, lax.all_gather(conv2_weight, 'shard', axis=0,...]
  transfers between devices with their start and end apart: 3 -> 19, of which waited for: 2 -> 6; matrix products, arithmetic and copies ran while one was open for 27% -> 11% of each run, Pallas kernels for 0% -> 9%
where the time goes in v1:
time: 176 us; the launch traced here: 175 us
  Pallas kernels  51.3 us (29%)
  starting transfers between devices  32.9 us (19%)
  blocking collectives  29.1 us (17%)
  between operations  25.4 us (14%)
  local copies, waits for them, and re-layouts  15.8 us (9%)
  waiting for transfers between devices  11.6 us (7%)
  other arithmetic  9.03 us (5%)
    pallas_call x1, Pallas kernels, front(): pl.pallas_call(front_kernel, out_shape=(jax.ShapeDtypeStruct((total, WIDT...  35.5 us
    pallas_call x1, Pallas kernels, back(): pl.pallas_call(back_kernel, out_shape=jax.ShapeDtypeStruct((16, WIDTH), f...  15.8 us
    all_to_all x1, blocking collectives, reduce_grads(): lax.all_to_all(jnp.broadcast_to(summed[None], chunk.shape), 'dp', 0, 0, a...  15.5 us
    all_to_all x1, blocking collectives, reduce_grads(): lax.all_to_all(chunk, 'dp', 0, 0, axis_index_groups=YZ_GROUPS, tiled=True)  13.6 us
    ppermute x3, starting transfers between devices, route(): lax.ppermute(pair, 'dp', ring(DP, C, Z, k))  9.66 us
    ppermute x3, waiting for transfers between devices, reduce_grads(): total = total + lax.ppermute(piece, 'shard', ring(X, 1, X, k)).astype(f32)  7.93 us
    ppermute x3, starting transfers between devices, route(): lax.ppermute(plane, 'dp', ring(DP, Z * C, Y, k))  4.45 us
    ppermute x3, starting transfers between devices, reduce_grads(): total = total + lax.ppermute(piece, 'shard', ring(X, 1, X, k)).astype(f32)  4.28 us
  transfers between devices with their start and end apart: 19, of which 6 were waited for; matrix products, arithmetic and copies ran while one was open for 11% of the time, Pallas kernels for 9%

profile of v1, /device:TPU:1, one launch (start us, length us, event | category | flops | bytes accessed | tf_op | source)
XLA Modules:
  0.0 175.2 jit_solution(5909231857319307487)
XLA Ops:
  8.1 0.8 compare_select_fusion
  9.0 2.6 %collective-permute-start = (bf16[2,6528]{1,0:T(2,128)(2,1)S(1)}, bf16[2,6528]{1,0:T(2,128)(2,1)S(1)}, u32[]{:S(2)}, u32[]{:S(2)}) collective-permute-start(bf16[2,6528]{1,0:T(2,128)(2,1)S(1)} %pad_maximum_fusion.3), channel_id=1, source_target_pairs={{0,8},{4,12},{8,0},{12,4},{16,24},{20,28},{24,16},{28,20},{32,40},... | collective-permute-start | bytes 78344 | tf_op jit(solution)/shard_map/ppermute | solution.py:257
  11.6 1.0 collective-permute-start.7
  13.2 0.8 convert_reduce_fusion
  14.1 0.8 convert_subtract_fusion
  15.7 3.1 %collective-permute-start.1 = (bf16[4,6528]{1,0:T(4,128)(2,1)S(1)}, bf16[4,6528]{1,0:T(4,128)(2,1)S(1)}, u32[]{:S(2)}, u32[]{:S(2)}) collective-permute-start(bf16[4,6528]{1,0:T(4,128)(2,1)S(1)} %pad_maximum_fusion.2), channel_id=1, source_target_pairs={{0,16},{4,20},{8,24},{12,28},{16,32},{20,36},{24,40},{28,44},{32,4... | collective-permute-start | bytes 156680 | tf_op jit(solution)/shard_map/ppermute | solution.py:259
  18.8 4.2 %collective-permute-start.2 = (bf16[4,6528]{1,0:T(4,128)(2,1)S(1)}, bf16[4,6528]{1,0:T(4,128)(2,1)S(1)}, u32[]{:S(2)}, u32[]{:S(2)}) collective-permute-start(bf16[4,6528]{1,0:T(4,128)(2,1)S(1)} %pad_maximum_fusion.2), channel_id=1, source_target_pairs={{0,32},{4,36},{8,40},{12,44},{16,48},{20,52},{24,56},{28,60},{32,0... | collective-permute-start | bytes 156680 | tf_op jit(solution)/shard_map/ppermute | solution.py:259
  23.0 2.4 %collective-permute-start.3 = (bf16[4,6528]{1,0:T(4,128)(2,1)S(1)}, bf16[4,6528]{1,0:T(4,128)(2,1)S(1)}, u32[]{:S(2)}, u32[]{:S(2)}) collective-permute-start(bf16[4,6528]{1,0:T(4,128)(2,1)S(1)} %pad_maximum_fusion.2), channel_id=1, source_target_pairs={{0,48},{4,52},{8,56},{12,60},{16,0},{20,4},{24,8},{28,12},{32,16},... | collective-permute-start | bytes 156680 | tf_op jit(solution)/shard_map/ppermute | solution.py:259
  25.3 1.3 fusion.14
  32.5 1.2 pad.15.clone
  33.7 1.1 copy.35
  35.6 1.4 collective-permute-start.6
  37.0 1.5 collective-permute-start.5
  38.5 1.6 collective-permute-start.4
  46.9 1.6 collective-permute-done.4
  48.9 2.0 %collective-permute-start.8 = (bf16[2,6528]{1,0:T(2,128)(2,1)S(1)}, bf16[2,6528]{1,0:T(2,128)(2,1)S(1)}, u32[]{:S(2)}, u32[]{:S(2)}) collective-permute-start(bf16[2,6528]{1,0:T(2,128)(2,1)S(1)} %pad_maximum_fusion.4), channel_id=1, source_target_pairs={{0,4},{4,0},{8,12},{12,8},{16,20},{20,16},{24,28},{28,24},{32,36},... | collective-permute-start | bytes 78344 | tf_op jit(solution)/shard_map/ppermute | solution.py:276
  53.4 3.7 %concatenate.66.x_ref = bf16[1280,60]{1,0:T(8,128)(2,1)} concatenate(bf16[1280,10]{1,0:T(8,128)(2,1)S(1)} %concatenate.63, bf16[1280,10]{1,0:T(8,128)(2,1)S(1)} %bitcast.54, bf16[1280,10]{1,0:T(8,128)(2,1)S(1)} %concatenate.63, bf16[1280,10]{1,0:T(8,128)(2,1)S(1)} %bitcast.55, bf16[1280,10]{1,0:T(8,128)(2,1)S(1)} %concatenate.63, bf16[1280,10]{1,0:T(8,128)(2,1)S(1)} %bitcast.56), dimensions={1} | concatenate | bytes 307200 | tf_op jit(solution)/shard_map/concatenate | solution.py:226
  57.9 35.5 %front.1 = (bf16[1280,512]{1,0:T(8,128)(2,1)}, bf16[2,1280,512]{2,1,0:T(8,128)(2,1)}, f32[2,1280,512]{2,1,0:T(8,128)}, f32[2,1280,1]{2,1,0:T(8,128)}, f32[1536,512]{1,0:T(8,128)}, /*index=5*/f32[16,512]{1,0:T(8,128)}) custom-call(bf16[1280,60]{1,0:T(8,128)(2,1)} %concatenate.66.x_ref, bf16[60,1024]{1,0:T(8,128)(2,1)} %pad_maximum_fusion.1.wc_ref, ...), custom_call_target="tpu_custom_call" | custom-call | tf_op jit(solution)/shard_map/front/pallas_call | solution.py:126
  93.4 1.5 fusion
  95.4 15.8 %back.1 = f32[16,512]{1,0:T(8,128)} custom-call(bf16[1280,60]{1,0:T(8,128)(2,1)} %concatenate.66.x_ref, bf16[60,1024]{1,0:T(8,128)(2,1)} %pad_maximum_fusion.1.wc_ref, f32[8,512]{1,0:T(8,128)} %concatenate.71.par_ref, bf16[1536,512]{1,0:T(8,128)(2,1)} %all-gather.2.cloned.1.call-done.w2_ref, bf16[2,1280,512]{2,1,0:T(8,128)(2,1)} %get-tuple-element.11.delta_ref, ...), custom_call_target="tpu_custom_call" | custom-call | tf_op jit(solution)/shard_map/back/pallas_call | solution.py:194
  112.4 2.8 %collective-permute-start.12 = (bf16[192,512]{1,0:T(8,128)(2,1)S(1)}, bf16[192,512]{1,0:T(8,128)(2,1)S(1)}, u32[]{:S(2)}, u32[]{:S(2)}) collective-permute-start(bf16[192,512]{1,0:T(8,128)(2,1)S(1)} %get-tuple-element.16), channel_id=1, source_target_pairs={{0,2},{1,3},{2,0},{3,1},{4,6},{5,7},{6,4},{7,5},{8,10},{9,11},{10,... | collective-permute-start | bytes 589832 | tf_op jit(solution)/shard_map/ppermute | solution.py:294
  115.3 0.8 collective-permute-start.11
  116.8 3.6 %collective-permute-done.12 = bf16[192,512]{1,0:T(8,128)(2,1)S(1)} collective-permute-done((bf16[192,512]{1,0:T(8,128)(2,1)S(1)}, bf16[192,512]{1,0:T(8,128)(2,1)S(1)}, u32[]{:S(2)}, u32[]{:S(2)}) %collective-permute-start.12) | collective-permute-done | bytes 196640 | tf_op jit(solution)/shard_map/ppermute | solution.py:294
  120.4 4.3 %collective-permute-done.11 = bf16[192,512]{1,0:T(8,128)(2,1)S(1)} collective-permute-done((bf16[192,512]{1,0:T(8,128)(2,1)S(1)}, bf16[192,512]{1,0:T(8,128)(2,1)S(1)}, u32[]{:S(2)}, u32[]{:S(2)}) %collective-permute-start.11) | collective-permute-done | bytes 196640 | tf_op jit(solution)/shard_map/ppermute | solution.py:294
  125.0 13.6 %all_to_all.10 = bf16[32,26,128]{2,1,0:T(8,128)(2,1)S(1)} all-to-all(bf16[32,26,128]{2,1,0:T(8,128)(2,1)S(1)} %pad_maximum_fusion), channel_id=1, replica_groups={{0,8,16,24,32,40,48,56,64,72,80,88,96,104,112,120,128,136,144,152,160,1..., dimensions={0} | all-to-all | bytes 425984 | tf_op jit(solution)/shard_map/all_to_all | solution.py:302
  138.7 15.5 %all_to_all.11 = bf16[32,26,128]{2,1,0:T(8,128)(2,1)S(1)} all-to-all(bf16[32,26,128]{2,1,0:T(8,128)(2,1)S(1)} %broadcast_in_dim.36), channel_id=1, replica_groups={{0,8,16,24,32,40,48,56,64,72,80,88,96,104,112,120,128,136,144,152,160,1..., dimensions={0} | all-to-all | bytes 425984 | tf_op jit(solution)/shard_map/all_to_all | solution.py:304
  154.3 3.8 %collective-permute-start.14 = (f32[16,512]{1,0:T(8,128)S(1)}, f32[16,512]{1,0:T(8,128)S(1)}, u32[]{:S(2)}, u32[]{:S(2)}) collective-permute-start(f32[16,512]{1,0:T(8,128)S(1)} %reshape.80), channel_id=1, source_target_pairs={{0,4},{4,0},{8,12},{12,8},{16,20},{20,16},{24,28},{28,24},{32,36},... | collective-permute-start | bytes 98312 | tf_op jit(solution)/shard_map/ppermute | solution.py:310
  158.0 0.9 collective-permute-done.14
  158.9 3.1 %collective-permute-start.17 = (f32[16,512]{1,0:T(8,128)S(1)}, f32[16,512]{1,0:T(8,128)S(1)}, u32[]{:S(2)}, u32[]{:S(2)}) collective-permute-start(f32[16,512]{1,0:T(8,128)S(1)} %add.300), channel_id=1, source_target_pairs={{0,3},{1,2},{2,1},{3,0},{4,7},{5,6},{6,5},{7,4},{8,11},{9,10},{10,... | collective-permute-start | bytes 98312 | tf_op jit(solution)/shard_map/ppermute | solution.py:311
  162.7 2.4 %copy.30 = bf16[2,639,512]{2,0,1:T(2,128)(2,1)} copy(bf16[2,639,512]{2,1,0:T(8,128)(2,1)S(1)} %bitcast.61) | data formatting | bytes 2617344
  165.3 1.0 collective-permute-start.13
  167.4 1.0 fusion.1
  (88 shorter events, 13.3 us)
Async XLA Ops:
  7.2 25.1 %copy-start.2 = (bf16[2,639,512]{2,0,1:T(2,128)(2,1)S(1)}, bf16[2,639,512]{2,0,1:T(2,128)(2,1)}, u32[]{:S(2)}) copy-start(bf16[2,639,512]{2,0,1:T(2,128)(2,1)} %param.15) | copy-start | bytes 3926020
  7.2 50.7 %all-gather.2.cloned.1.call-start = ((), (), s32[]{:S(2)}) async-start(), calls=%async_computation.2 | async-start | bytes 1966080 | tf_op jit(solution)/shard_map/all_gather | solution.py:319
  9.0 6.6 %collective-permute-start = (bf16[2,6528]{1,0:T(2,128)(2,1)S(1)}, bf16[2,6528]{1,0:T(2,128)(2,1)S(1)}, u32[]{:S(2)}, u32[]{:S(2)}) collective-permute-start(bf16[2,6528]{1,0:T(2,128)(2,1)S(1)} %pad_maximum_fusion.3), channel_id=1, source_target_pairs={{0,8},{4,12},{8,0},{12,4},{16,24},{20,28},{24,16},{28,20},{32,40},... | collective-permute-start | bytes 78344 | tf_op jit(solution)/shard_map/ppermute | solution.py:257
  11.6 29.2 %collective-permute-start.7 = (s32[2]{0:T(128)}, s32[2]{0:T(128)S(1)}, u32[]{:S(2)}, u32[]{:S(2)}) collective-permute-start(s32[2]{0:T(128)} %param.13), channel_id=1, source_target_pairs={{0,4},{4,0},{8,12},{12,8},{16,20},{20,16},{24,28},{28,24},{32,36},... | collective-permute-start | bytes 32 | tf_op jit(solution)/shard_map/ppermute | solution.py:251
  15.7 19.7 %collective-permute-start.1 = (bf16[4,6528]{1,0:T(4,128)(2,1)S(1)}, bf16[4,6528]{1,0:T(4,128)(2,1)S(1)}, u32[]{:S(2)}, u32[]{:S(2)}) collective-permute-start(bf16[4,6528]{1,0:T(4,128)(2,1)S(1)} %pad_maximum_fusion.2), channel_id=1, source_target_pairs={{0,16},{4,20},{8,24},{12,28},{16,32},{20,36},{24,40},{28,44},{32,4... | collective-permute-start | bytes 156680 | tf_op jit(solution)/shard_map/ppermute | solution.py:259
  18.8 16.7 %collective-permute-start.2 = (bf16[4,6528]{1,0:T(4,128)(2,1)S(1)}, bf16[4,6528]{1,0:T(4,128)(2,1)S(1)}, u32[]{:S(2)}, u32[]{:S(2)}) collective-permute-start(bf16[4,6528]{1,0:T(4,128)(2,1)S(1)} %pad_maximum_fusion.2), channel_id=1, source_target_pairs={{0,32},{4,36},{8,40},{12,44},{16,48},{20,52},{24,56},{28,60},{32,0... | collective-permute-start | bytes 156680 | tf_op jit(solution)/shard_map/ppermute | solution.py:259
  23.0 12.5 %collective-permute-start.3 = (bf16[4,6528]{1,0:T(4,128)(2,1)S(1)}, bf16[4,6528]{1,0:T(4,128)(2,1)S(1)}, u32[]{:S(2)}, u32[]{:S(2)}) collective-permute-start(bf16[4,6528]{1,0:T(4,128)(2,1)S(1)} %pad_maximum_fusion.2), channel_id=1, source_target_pairs={{0,48},{4,52},{8,56},{12,60},{16,0},{20,4},{24,8},{28,12},{32,16},... | collective-permute-start | bytes 156680 | tf_op jit(solution)/shard_map/ppermute | solution.py:259
  32.4 2.3 %copy-start.4 = (f32[512]{0:T(512)S(1)}, f32[512]{0:T(512)}, u32[]{:S(2)}) copy-start(f32[512]{0:T(512)} %param.17) | copy-start | bytes 6148
  32.5 2.3 %copy-start.5 = (f32[512]{0:T(512)S(1)}, f32[512]{0:T(512)}, u32[]{:S(2)}) copy-start(f32[512]{0:T(512)} %param.18) | copy-start | bytes 6148
  32.5 2.3 %copy-start.6 = (f32[512]{0:T(512)S(1)}, f32[512]{0:T(512)}, u32[]{:S(2)}) copy-start(f32[512]{0:T(512)} %param.20) | copy-start | bytes 6148
  32.5 2.3 %copy-start.7 = (f32[512]{0:T(512)S(1)}, f32[512]{0:T(512)}, u32[]{:S(2)}) copy-start(f32[512]{0:T(512)} %param.21) | copy-start | bytes 6148
  35.6 11.2 %collective-permute-start.6 = (bf16[16,6528]{1,0:T(8,128)(2,1)S(1)}, bf16[16,6528]{1,0:T(8,128)(2,1)S(1)}, u32[]{:S(2)}, u32[]{:S(2)}) collective-permute-start(bf16[16,6528]{1,0:T(8,128)(2,1)S(1)} %concatenate.60), channel_id=1, source_target_pairs={{0,64},{4,68},{8,72},{12,76},{16,80},{20,84},{24,88},{28,92},{32,9... | collective-permute-start | bytes 626696 | tf_op jit(solution)/shard_map/ppermute | solution.py:260
  37.0 9.9 %collective-permute-start.5 = (bf16[16,6528]{1,0:T(8,128)(2,1)S(1)}, bf16[16,6528]{1,0:T(8,128)(2,1)S(1)}, u32[]{:S(2)}, u32[]{:S(2)}) collective-permute-start(bf16[16,6528]{1,0:T(8,128)(2,1)S(1)} %concatenate.60), channel_id=1, source_target_pairs={{0,192},{4,196},{8,200},{12,204},{16,208},{20,212},{24,216},{28,22... | collective-permute-start | bytes 626696 | tf_op jit(solution)/shard_map/ppermute | solution.py:260
  38.5 9.9 %collective-permute-start.4 = (bf16[16,6528]{1,0:T(8,128)(2,1)S(1)}, bf16[16,6528]{1,0:T(8,128)(2,1)S(1)}, u32[]{:S(2)}, u32[]{:S(2)}) collective-permute-start(bf16[16,6528]{1,0:T(8,128)(2,1)S(1)} %concatenate.60), channel_id=1, source_target_pairs={{0,128},{4,132},{8,136},{12,140},{16,144},{20,148},{24,152},{28,15... | collective-permute-start | bytes 626696 | tf_op jit(solution)/shard_map/ppermute | solution.py:260
  48.9 2.9 %collective-permute-start.8 = (bf16[2,6528]{1,0:T(2,128)(2,1)S(1)}, bf16[2,6528]{1,0:T(2,128)(2,1)S(1)}, u32[]{:S(2)}, u32[]{:S(2)}) collective-permute-start(bf16[2,6528]{1,0:T(2,128)(2,1)S(1)} %pad_maximum_fusion.4), channel_id=1, source_target_pairs={{0,4},{4,0},{8,12},{12,8},{16,20},{20,16},{24,28},{28,24},{32,36},... | collective-permute-start | bytes 78344 | tf_op jit(solution)/shard_map/ppermute | solution.py:276
  94.9 17.1 %collective-permute-start.9 = (bf16[4,192,512]{2,1,0:T(8,128)(2,1)S(1)}, bf16[4,192,512]{2,1,0:T(8,128)(2,1)S(1)}, u32[]{:S(2)}, u32[]{:S(2)}) collective-permute-start(bf16[4,192,512]{2,1,0:T(8,128)(2,1)S(1)} %fusion), channel_id=1, source_target_pairs={{0,4},{4,0},{8,12},{12,8},{16,20},{20,16},{24,28},{28,24},{32,36},... | collective-permute-start | bytes 2359304 | tf_op jit(solution)/shard_map/ppermute | solution.py:290
  95.4 16.6 %copy-start.3 = (f32[16,512]{1,0:T(8,128)S(1)}, f32[16,512]{1,0:T(8,128)}, u32[]{:S(2)}) copy-start(f32[16,512]{1,0:T(8,128)} %get-tuple-element.14) | copy-start | bytes 98308
  95.4 16.6 %copy-start = (f32[1536,512]{1,0:T(8,128)S(1)}, f32[1536,512]{1,0:T(8,128)}, u32[]{:S(2)}) copy-start(f32[1536,512]{1,0:T(8,128)} %get-tuple-element.10) | copy-start | bytes 9437188
  112.4 7.9 %collective-permute-start.12 = (bf16[192,512]{1,0:T(8,128)(2,1)S(1)}, bf16[192,512]{1,0:T(8,128)(2,1)S(1)}, u32[]{:S(2)}, u32[]{:S(2)}) collective-permute-start(bf16[192,512]{1,0:T(8,128)(2,1)S(1)} %get-tuple-element.16), channel_id=1, source_target_pairs={{0,2},{1,3},{2,0},{3,1},{4,6},{5,7},{6,4},{7,5},{8,10},{9,11},{10,... | collective-permute-start | bytes 589832 | tf_op jit(solution)/shard_map/ppermute | solution.py:294
  115.3 9.4 %collective-permute-start.11 = (bf16[192,512]{1,0:T(8,128)(2,1)S(1)}, bf16[192,512]{1,0:T(8,128)(2,1)S(1)}, u32[]{:S(2)}, u32[]{:S(2)}) collective-permute-start(bf16[192,512]{1,0:T(8,128)(2,1)S(1)} %get-tuple-element.17), channel_id=1, source_target_pairs={{0,3},{1,0},{2,1},{3,2},{4,7},{5,4},{6,5},{7,6},{8,11},{9,8},{10,9... | collective-permute-start | bytes 589832 | tf_op jit(solution)/shard_map/ppermute | solution.py:294
  116.1 8.6 %collective-permute-start.10 = (bf16[192,512]{1,0:T(8,128)(2,1)S(1)}, bf16[192,512]{1,0:T(8,128)(2,1)S(1)}, u32[]{:S(2)}, u32[]{:S(2)}) collective-permute-start(bf16[192,512]{1,0:T(8,128)(2,1)S(1)} %get-tuple-element.15), channel_id=1, source_target_pairs={{0,1},{1,2},{2,3},{3,0},{4,5},{5,6},{6,7},{7,4},{8,9},{9,10},{10,1... | collective-permute-start | bytes 589832 | tf_op jit(solution)/shard_map/ppermute | solution.py:294
  124.8 37.8 %copy-start.1 = (bf16[1280,512]{1,0:T(8,128)(2,1)S(1)}, bf16[1280,512]{1,0:T(8,128)(2,1)}, u32[]{:S(2)}) copy-start(bf16[1280,512]{1,0:T(8,128)(2,1)} %get-tuple-element.9) | copy-start | bytes 3932164
  154.3 4.6 %collective-permute-start.14 = (f32[16,512]{1,0:T(8,128)S(1)}, f32[16,512]{1,0:T(8,128)S(1)}, u32[]{:S(2)}, u32[]{:S(2)}) collective-permute-start(f32[16,512]{1,0:T(8,128)S(1)} %reshape.80), channel_id=1, source_target_pairs={{0,4},{4,0},{8,12},{12,8},{16,20},{20,16},{24,28},{28,24},{32,36},... | collective-permute-start | bytes 98312 | tf_op jit(solution)/shard_map/ppermute | solution.py:310
  158.9 7.4 %collective-permute-start.17 = (f32[16,512]{1,0:T(8,128)S(1)}, f32[16,512]{1,0:T(8,128)S(1)}, u32[]{:S(2)}, u32[]{:S(2)}) collective-permute-start(f32[16,512]{1,0:T(8,128)S(1)} %add.300), channel_id=1, source_target_pairs={{0,3},{1,2},{2,1},{3,0},{4,7},{5,6},{6,5},{7,4},{8,11},{9,10},{10,... | collective-permute-start | bytes 98312 | tf_op jit(solution)/shard_map/ppermute | solution.py:311
  162.0 4.3 %collective-permute-start.16 = (f32[16,512]{1,0:T(8,128)S(1)}, f32[16,512]{1,0:T(8,128)S(1)}, u32[]{:S(2)}, u32[]{:S(2)}) collective-permute-start(f32[16,512]{1,0:T(8,128)S(1)} %add.300), channel_id=1, source_target_pairs={{0,2},{1,3},{2,0},{3,1},{4,6},{5,7},{6,4},{7,5},{8,10},{9,11},{10,... | collective-permute-start | bytes 98312 | tf_op jit(solution)/shard_map/ppermute | solution.py:311
  162.4 3.9 %collective-permute-start.15 = (f32[16,512]{1,0:T(8,128)S(1)}, f32[16,512]{1,0:T(8,128)S(1)}, u32[]{:S(2)}, u32[]{:S(2)}) collective-permute-start(f32[16,512]{1,0:T(8,128)S(1)} %add.300), channel_id=1, source_target_pairs={{0,1},{1,0},{2,3},{3,2},{4,5},{5,4},{6,7},{7,6},{8,9},{9,8},{10,11... | collective-permute-start | bytes 98312 | tf_op jit(solution)/shard_map/ppermute | solution.py:311
  165.3 2.1 %collective-permute-start.13 = (bf16[192,512]{1,0:T(8,128)(2,1)S(1)}, bf16[192,512]{1,0:T(8,128)(2,1)S(1)}, u32[]{:S(2)}, u32[]{:S(2)}) collective-permute-start(bf16[192,512]{1,0:T(8,128)(2,1)S(1)} %bitcast.66), channel_id=1, source_target_pairs={{0,4},{4,0},{8,12},{12,8},{16,20},{20,16},{24,28},{28,24},{32,36},... | collective-permute-start | bytes 589832 | tf_op jit(solution)/shard_map/ppermute | solution.py:307
Sparse Core Ops, SparseCore 0:
  12.7 30.5 all-gather.1

commit v2 on v0

v2 whole, which is shorter than its diff:
```python
import math

import jax
import jax.numpy as jnp
from jax import lax
from jax.experimental import pallas as pl
from jax.experimental.pallas import tpu as pltpu
from jax.sharding import PartitionSpec as P

f32 = jnp.float32
bf = jnp.bfloat16
WIDTH = 512
HALF = 256
ROWS = 640
VMEM_LIMIT = 60 * 1024 * 1024
T1, T2, T3 = 128, 256, 256
M1, M2, M3, MG = 256, 1280, 640, 512
NN = (((1,), (0,)), ((), ()))
NT = (((1,), (1,)), ((), ()))
TN = (((0,), (0,)), ((), ()))


def gelu_parts(y):
    d = 1.0 + 0.23164189 * jnp.abs(y)
    t = pl.reciprocal(d, approx=True)
    t = t * (2.0 - d * t)
    e = jnp.exp2(y * (y * (-0.5 * 1.4426950408889634)))
    poly = t * (0.127414796 + t * (-0.142248368 + t * (0.7107068705 + t * (-0.7265760135 + t * 0.5307027145))))
    tail = poly * e
    return jnp.where(y >= 0, 1.0 - tail, tail), e


def lane_sum(v):
    return jnp.sum(v, axis=-1, keepdims=True)


def rows8(v):
    return jnp.sum(v.reshape(v.shape[0] // 8, 8, v.shape[1]), axis=0)


def dot(a, b, dims=NN):
    return lax.dot_general(a, b, dims, preferred_element_type=f32)


def shifted_up(v, below):
    return jnp.concatenate([v, below], 0)[1:v.shape[0] + 1]


def shifted_down(v, above):
    return jnp.concatenate([above, v], 0)[7:v.shape[0] + 7]


def norm_back(q, n, inv):
    qn = q * n
    inner = lane_sum(q) * (1.0 / WIDTH)
    along = lane_sum(qn) * (1.0 / WIDTH)
    return inv * (q - inner - n * along), qn


def encoder_kernel(ids_ref, x_ref, wc_ref, par_ref, fm_ref, tail_ref, cot_hbm, wa_hbm, wb_hbm, wc_hbm, wd_hbm,
                   feat_ref, keep_ref, send_ref,
                   w2_ref, cot_ref, sems, p_ref, small_ref, c_ref, u_ref, s_ref, d_ref, sg_ref, r1_ref, dl_ref, t_ref):
    total = x_ref.shape[0]
    core = ids_ref[0]
    part = wa_hbm.shape[0]
    loads = []
    for k, src in enumerate((wa_hbm, wb_hbm, wc_hbm, wd_hbm)):
        at = pl.multiple_of((ids_ref[1] ^ k) * part, part)
        loads.append(pltpu.make_async_copy(src, w2_ref.at[pl.ds(at, part), :], sems.at[k]))
    loads.append(pltpu.make_async_copy(cot_hbm, cot_ref, sems.at[4]))
    for load in loads:
        load.start()
    gain1, shift1, gain2, shift2 = (par_ref[k:k + 1, :] for k in range(4))
    zero = jnp.zeros((8, WIDTH), f32)
    tail = tail_ref[...].astype(f32)
    length = tail[:, 0:1] * 128.0 + tail[:, 1:2]

    def rows(i, size):
        return pl.ds(pl.multiple_of(i * size, size), size)

    now = x_ref[...].astype(f32)
    later = shifted_up(now, jnp.zeros((8, now.shape[1]), f32))
    k = lax.broadcasted_iota(jnp.int32, (10, 128), 0)
    lane = lax.broadcasted_iota(jnp.int32, (10, 128), 1)
    step = lane - lane // 20 * 20
    used = lane < 60
    place = jnp.where(used & (step == k), 1.0, 0.0).astype(bf)
    place_later = jnp.where(used & (step == k + 10), 1.0, 0.0).astype(bf)
    p_ref[...] = (dot(now.astype(bf), place) + dot(later.astype(bf), place_later)).astype(bf)

    def conv1(i, _):
        r = rows(i, M1)
        c_ref[r, :] = dot(p_ref[r, 0:64], wc_ref[...])
        return 0
    lax.fori_loop(0, total // M1, conv1, 0)

    def level_one(i, below):
        r = rows(total // T1 - 1 - i, T1)
        for half in range(2):
            c = c_ref[r, half * WIDTH:(half + 1) * WIDTH]
            inv = lax.rsqrt(lane_sum(c * c) * (1.0 / WIDTH) + 1e-5)
            y = c * inv * gain1 + shift1
            phi, e = gelu_parts(y)
            h = y * phi
            sg_ref[half, r, :] = (phi + (y * 0.3989422804014327) * e) * gain1
            r1_ref[half, r, :] = inv
            u_ref[r, half * WIDTH:(half + 1) * WIDTH] = h.astype(bf)
            if half == 0:
                u_ref[r, 2 * WIDTH:] = shifted_up(h, below).astype(bf)
                first = h[0:8]
        return first
    lax.fori_loop(0, total // T1, level_one, zero)

    for load in loads[:4]:
        load.wait()

    def conv2(i, _):
        r = rows(i, M2)
        s_ref[r, :] = dot(u_ref[r, :], w2_ref[...])
        return 0
    lax.fori_loop(0, total // M2, conv2, 0)

    loads[4].wait()

    def level_two(i, carry):
        acc_a, acc_b, above = carry
        b = pl.multiple_of(i * T2, T2)
        r = pl.ds(b, T2)
        z = s_ref[r, :]
        c = z - lane_sum(z) * (1.0 / WIDTH)
        inv = lax.rsqrt(lane_sum(c * c) * (1.0 / WIDTH) + 1e-5)
        n = c * inv
        y = n * gain2 + shift2
        phi, e = gelu_parts(y)
        feat_ref[r, :] = (y * phi).astype(bf)
        slope = phi + (y * 0.3989422804014327) * e
        row = (lax.broadcasted_iota(jnp.int32, (T2, 1), 0) + b).astype(f32)
        room = jnp.where(row < ROWS, length[0:1], length[1:2] + 10.0 * ROWS)
        weight = jnp.where(10.0 * row + 19.0 < room, fm_ref[r, :], 0.0)
        q = cot_ref[r, :].astype(f32) * weight * (slope * gain2)
        back, qn = norm_back(q, n, inv)
        dl_ref[r, 0:WIDTH] = back.astype(bf)
        dl_ref[r, WIDTH:] = shifted_down(back, above).astype(bf)
        return acc_a + rows8(qn), acc_b + rows8(q), back[T2 - 8:T2]
    acc_a, acc_b, _ = lax.fori_loop(0, total // T2, level_two, (zero, zero, zero))
    small_ref[12:13, :] = jnp.sum(acc_a, axis=0, keepdims=True) / gain2
    small_ref[13:14, :] = jnp.sum(acc_b, axis=0, keepdims=True) / gain2
    small_ref[14:16, :] = jnp.zeros((2, WIDTH), f32)

    for ref, half in ((keep_ref, core), (send_ref, 1 - core)):
        for tap, shift in ((0, 0), (1, 0), (0, WIDTH)):
            base = (tap if shift == 0 else 2) * WIDTH
            cols = pl.ds(pl.multiple_of(shift + half * HALF, HALF), HALF)
            ref[base:base + WIDTH, :] = dot(u_ref[:, tap * WIDTH:(tap + 1) * WIDTH], dl_ref[:, cols], TN).astype(ref.dtype)

    def down(i, _):
        r = rows(i, M3)
        now = dl_ref[r, 0:WIDTH]
        s_ref[r, :] = dot(now, w2_ref[0:WIDTH, :], NT) + dot(dl_ref[r, WIDTH:], w2_ref[2 * WIDTH:, :], NT)
        d_ref[r, :] = dot(now, w2_ref[WIDTH:2 * WIDTH, :], NT)
        return 0
    lax.fori_loop(0, total // M3, down, 0)

    def level_one_back(i, acc):
        acc_a, acc_b = acc
        r = rows(i, T3)
        for half, down_ref in enumerate((s_ref, d_ref)):
            lanes = slice(half * WIDTH, (half + 1) * WIDTH)
            q = down_ref[r, :] * sg_ref[half, r, :]
            inv = r1_ref[half, r, :]
            back, qn = norm_back(q, c_ref[r, lanes] * inv, inv)
            t_ref[r, lanes] = back.astype(bf)
            acc_a = acc_a + rows8(qn)
            acc_b = acc_b + rows8(q)
        return acc_a, acc_b
    acc_a, acc_b = lax.fori_loop(0, total // T3, level_one_back, (zero, zero))
    small_ref[10:11, :] = jnp.sum(acc_a, axis=0, keepdims=True) / gain1
    small_ref[11:12, :] = jnp.sum(acc_b, axis=0, keepdims=True) / gain1
    taps = dot(p_ref[:, 0:32], t_ref[...], TN)
    small_ref[0:10, :] = taps[0:10, 0:WIDTH] + taps[5:15, WIDTH:]
    small = small_ref[...].astype(bf)
    for j in range(2):
        r = slice(3 * WIDTH + 16 * j, 3 * WIDTH + 16 * (j + 1))
        send_ref[r, :] = small[:, j * HALF:(j + 1) * HALF]
        keep_ref[r, :] = small[:, j * HALF:(j + 1) * HALF].astype(f32)


def encoder(ids, x, wc, par, fm, tail, cot, parts):
    total = x.shape[0]
    vm = pl.BlockSpec(memory_space=pltpu.VMEM)
    hbm = pl.BlockSpec(memory_space=pl.ANY)
    return pl.pallas_call(
        encoder_kernel,
        out_shape=(
            jax.ShapeDtypeStruct((total, WIDTH), bf),
            jax.ShapeDtypeStruct((3 * WIDTH + 32, HALF), f32),
            jax.ShapeDtypeStruct((3 * WIDTH + 32, HALF), bf),
        ),
        in_specs=[pl.BlockSpec(memory_space=pltpu.SMEM)] + [vm] * 5 + [hbm] * 5,
        out_specs=(vm,) * 3,
        scratch_shapes=[
            pltpu.VMEM((3 * WIDTH, WIDTH), bf),
            pltpu.VMEM((total, WIDTH), bf),
            pltpu.SemaphoreType.DMA((5,)),
            pltpu.VMEM((total, 128), bf),
            pltpu.VMEM((16, WIDTH), f32),
            pltpu.VMEM((total, 2 * WIDTH), f32),
            pltpu.VMEM((total, 3 * WIDTH), bf),
            pltpu.VMEM((total, WIDTH), f32),
            pltpu.VMEM((total, WIDTH), f32),
            pltpu.VMEM((2, total, WIDTH), f32),
            pltpu.VMEM((2, total, 1), f32),
            pltpu.VMEM((total, 2 * WIDTH), bf),
            pltpu.VMEM((total, 2 * WIDTH), bf),
        ],
        compiler_params=pltpu.CompilerParams(vmem_limit_bytes=VMEM_LIMIT),
        name="encoder",
    )(ids, x, wc, par, fm, tail, cot, *parts)


def prep_weights(conv1_weight):
    w1 = conv1_weight.astype(f32)
    wc = w1 - jnp.mean(w1, axis=1, keepdims=True)
    z5 = jnp.zeros((5, WIDTH), f32)
    z10 = jnp.zeros((10, WIDTH), f32)
    both = jnp.concatenate([jnp.concatenate([wc, z10], 0), jnp.concatenate([z5, wc, z5], 0)], 1)
    hi = lax.reduce_precision(both, 8, 7)
    mid = lax.reduce_precision(both - hi, 8, 7)
    low = both - hi - mid
    return jnp.concatenate([hi.astype(bf), mid.astype(bf), low.astype(bf), jnp.zeros((4, 2 * WIDTH), bf)], 0)


Y, Z, C, X = 4, 8, 2, 4
DP = Y * Z * C
CORE = [(i, i ^ 1) for i in range(DP)]
YZ_GROUPS = [[yz * C + c for yz in range(Y * Z)] for c in range(C)]


def flip(k):
    return [(i, i ^ k) for i in range(X)]


def exchange(chunks):
    return lax.all_to_all(chunks, "dp", 0, 0, axis_index_groups=YZ_GROUPS, tiled=True)


def pack(waveform, lengths):
    count, length = waveform.shape
    inside = jnp.arange(length, dtype=jnp.int32)[None, :] < lengths[:, None]
    cleaned = jnp.where(inside, waveform, jnp.zeros_like(waveform))
    tail = jnp.stack([lengths >> 7, lengths & 127], 1).astype(bf)
    return jnp.concatenate([cleaned, jnp.pad(tail, ((0, 0), (0, 126)))], 1)


def pick(source, column, other_column, core):
    count, holder = source.shape[0], source >> 3
    local = (holder & 1) == core
    crops = []
    for i in range(count):
        start = (holder[i] >> 1, source[i] & 1, 0)
        size = (1, 1, column.shape[2])
        crops.append(jnp.where(local[i], lax.dynamic_slice(column, start, size),
                               lax.dynamic_slice(other_column, start, size))[0])
    return jnp.concatenate(crops, 0)


def gather_weight(weight):
    return [weight] + [lax.ppermute(weight, "shard", flip(k)) for k in (1, 2, 3)]


def reduce_grads(keep, send, core, shadow):
    x = lax.axis_index("shard")
    part = 3 * WIDTH // X
    here = keep + lax.ppermute(send, "dp", CORE).astype(f32)
    small = here[3 * WIDTH:].astype(bf)
    here, shadow = lax.optimization_barrier((here, shadow))

    def piece(k):
        return lax.dynamic_slice_in_dim(here, (x ^ k) * part, part, 0)
    got = [lax.ppermute(jnp.concatenate([piece(k).astype(bf), small], 0), "shard", flip(k)).astype(f32)
           for k in (1, 2, 3)]
    total = (jnp.concatenate([piece(0), small.astype(f32)], 0) + got[0]) + (got[1] + got[2])
    lanes = HALF // 128
    chunk = total.astype(bf).reshape(-1, lanes, 128).transpose(1, 0, 2).reshape(Y * Z, -1, 128)
    summed = jnp.sum(exchange(chunk).astype(f32), axis=0).astype(bf)
    every = exchange(jnp.broadcast_to(summed[None], chunk.shape))
    every = every.reshape(lanes, -1, 128).transpose(1, 0, 2).reshape(-1, HALF)
    half = every[:part]
    other = lax.ppermute(half, "dp", CORE)
    grad_conv2 = jnp.where(core == 0, jnp.concatenate([half, other], 1), jnp.concatenate([other, half], 1))
    small = jnp.concatenate([every[part:part + 14], every[part + 16:part + 30]], 1)
    return grad_conv2.astype(f32), small.astype(f32), shadow


def body(waveform, lengths, source, frame_mask, cotangent, conv1_weight, gain_one, shift_one,
         conv2_weight, gain_two, shift_two):
    count, frames = frame_mask.shape
    core, x = lax.axis_index("dp") & 1, lax.axis_index("shard")
    parts = gather_weight(conv2_weight)
    loss_scale = 1.0 / math.sqrt(count * DP * X * frames)
    upstream = jnp.pad(cotangent, ((0, 0), (0, 1), (0, 0))).reshape(count * ROWS, WIDTH)
    weights = jnp.pad(frame_mask.astype(f32) * loss_scale, ((0, 0), (0, 1))).reshape(count * ROWS, 1)
    par = jnp.concatenate(
        [jnp.stack([gain_one, shift_one, gain_two, shift_two]), jnp.zeros((4, WIDTH), f32)], 0)
    wc = prep_weights(conv1_weight)
    own = pack(waveform, lengths)
    column = exchange(jnp.broadcast_to(own[None], (Y * Z,) + own.shape))
    routed = pick(source, column, lax.ppermute(column, "dp", CORE), core)
    length = waveform.shape[1]
    blocks = routed[:, :length].reshape(count * ROWS, 10)
    feat, keep, send = encoder(
        jnp.stack([core, x]), blocks, wc, par, weights, routed[:, length:], upstream, parts)
    features = feat.reshape(count, ROWS, WIDTH)[:, :frames]
    grad_conv2, grad_front, features = reduce_grads(keep, send, core, features)
    return features, grad_conv2, grad_front


def solution(mesh):
    both = P(("dp", "shard"))
    placed = (both, both, both, both, both, P(), P(), P(), P("shard"), P(), P())
    return jax.shard_map(
        body,
        mesh=mesh,
        in_specs=placed,
        out_specs=(both, P("shard"), P()),
        check_vma=False,
    )
```

time: 426 us -> 141 us (0.33)
  waiting for transfers between devices: 173 us -> 35.6 us
  blocking collectives: 96.7 us -> 13.9 us
  local copies, waits for them, and re-layouts: 73.6 us -> 15 us
  other arithmetic: 43.9 us -> 8.24 us
  starting transfers between devices: 0.11 us -> 35 us
  Pallas kernels: 0 us -> 29.3 us
  matrix products: 22.1 us -> 0 us
  between operations: 14.6 us -> 3.56 us
    psum x1 -> x0, waiting for transfers between devices: 118 us -> none  [body(): summed, grad_front = lax.psum((weight_terms, grad_small), ('dp', 'shard'))]
    psum x1 -> x0, blocking collectives: 75.7 us -> none  [body(): summed, grad_front = lax.psum((weight_terms, grad_small), ('dp', 'shard'))]
    all_gather x2 -> x0, waiting for transfers between devices: 53.7 us -> none  [the longest x1 53.7 us: body(): lax.all_gather(waveform, 'dp', axis=0, tiled=True)]
    pallas_call x0 -> x1, Pallas kernels: none -> 29.3 us  [encoder(): pl.pallas_call(encoder_kernel, out_shape=(jax.ShapeDtypeStruct((total, WI...]
    reshape x8 -> x3, local copies, waits for them, and re-layouts: 30.6 us -> 1.56 us  [the longest x1 1.43 us: body(): blocks = routed[:, :length].reshape(count * ROWS, 10)]
    all_to_all x0 -> x2, waiting for transfers between devices: none -> 23.8 us  [exchange(): lax.all_to_all(chunks, 'dp', 0, 0, axis_index_groups=YZ_GROUPS, tiled=True)]
    dot_general x5 -> x0, matrix products: 22.1 us -> none  [the longest x1 6.72 us: body(): lax.dot_general(delta_two, lax.all_gather(conv2_weight, 'shard', axis=0,...]
    unnamed x1 -> x0, blocking collectives: 21 us -> none
  transfers between devices with their start and end apart: 3 -> 11, of which waited for: 2 -> 6; matrix products, arithmetic and copies ran while one was open for 27% -> 11% of each run, Pallas kernels for 0% -> 0%
where the time goes in v2:
time: 141 us
  waiting for transfers between devices  35.6 us (25%)
  starting transfers between devices  35 us (25%)
  Pallas kernels  29.3 us (21%)
  local copies, waits for them, and re-layouts  15 us (11%)
  blocking collectives  13.9 us (10%)
  other arithmetic  8.24 us (6%)
  between operations  3.56 us (3%)
    pallas_call x1, Pallas kernels, encoder(): pl.pallas_call(encoder_kernel, out_shape=(jax.ShapeDtypeStruct((total, WI...  29.3 us
    all_to_all x2, waiting for transfers between devices, exchange(): lax.all_to_all(chunks, 'dp', 0, 0, axis_index_groups=YZ_GROUPS, tiled=True)  23.8 us
    all_to_all x2, starting transfers between devices, exchange(): lax.all_to_all(chunks, 'dp', 0, 0, axis_index_groups=YZ_GROUPS, tiled=True)  17.3 us
    all_to_all x1, blocking collectives, exchange(): lax.all_to_all(chunks, 'dp', 0, 0, axis_index_groups=YZ_GROUPS, tiled=True)  13.9 us
    ppermute x3, waiting for transfers between devices, reduce_grads(): lax.ppermute(jnp.concatenate([piece(k).astype(bf), small], 0), 'shard', f...  11.4 us
    ppermute x1, starting transfers between devices, body(): routed = pick(source, column, lax.ppermute(column, 'dp', CORE), core)  5.27 us
    ppermute x1, starting transfers between devices, reduce_grads(): other = lax.ppermute(half, 'dp', CORE)  4.37 us
    ppermute x3, starting transfers between devices, reduce_grads(): lax.ppermute(jnp.concatenate([piece(k).astype(bf), small], 0), 'shard', f...  4 us
  transfers between devices with their start and end apart: 11, of which 6 were waited for; matrix products, arithmetic and copies ran while one was open for 11% of the time, Pallas kernels for 0%

profile of v2, /device:TPU:1, one launch (start us, length us, event | category | flops | bytes accessed | tf_op | source)
XLA Modules:
  0.0 140.7 jit_solution(16098102747223250333)
XLA Ops:
  0.7 0.8 convert_bitcast_fusion.1
  1.6 0.8 compare_select_fusion.1
  2.4 1.3 broadcast_in_dim.13
  3.8 12.0 %all-to-all-start = ((bf16[32,2,6528]{2,1,0:T(2,128)(2,1)}), bf16[32,2,6528]{2,1,0:T(2,128)(2,1)S(1)}, u32[]{:S(2)}, u32[]{:S(2)}) async-start(bf16[32,2,6528]{2,1,0:T(2,128)(2,1)} %broadcast_in_dim.13), calls=%async_computation | async-start | bytes 1671168 | tf_op jit(solution)/shard_map/all_to_all | solution.py:244
  15.8 1.3 collective-permute-start.1
  17.1 2.5 %collective-permute-start.2 = (bf16[384,512]{1,0:T(8,128)(2,1)}, bf16[384,512]{1,0:T(8,128)(2,1)}, u32[]{:S(2)}, u32[]{:S(2)}) collective-permute-start(bf16[384,512]{1,0:T(8,128)(2,1)} %wa_hbm.1), channel_id=1, source_target_pairs={{0,2},{1,3},{2,0},{3,1},{4,6},{5,7},{6,4},{7,5},{8,10},{9,11},{10,... | collective-permute-start | bytes 1179656 | tf_op jit(solution)/shard_map/ppermute | solution.py:268
  19.8 0.7 fusion.11
  21.8 14.2 %all-to-all-done = bf16[32,2,6528]{2,1,0:T(2,128)(2,1)S(1)} async-done(((bf16[32,2,6528]{2,1,0:T(2,128)(2,1)}), bf16[32,2,6528]{2,1,0:T(2,128)(2,1)S(1)}, u32[]{:S(2)}, u32[]{:S(2)}) %all-to-all-start) | async-done | bytes 835616 | tf_op jit(solution)/shard_map/all_to_all | solution.py:244
  35.9 5.3 %collective-permute-start = (bf16[32,2,6528]{2,1,0:T(2,128)(2,1)S(1)}, bf16[32,2,6528]{2,1,0:T(2,128)(2,1)}, u32[]{:S(2)}, u32[]{:S(2)}) collective-permute-start(bf16[32,2,6528]{2,1,0:T(2,128)(2,1)S(1)} %all-to-all-done), channel_id=1, source_target_pairs={{0,4},{4,0},{8,12},{12,8},{16,20},{20,16},{24,28},{28,24},{32,36},... | collective-permute-start | bytes 2506760 | tf_op jit(solution)/shard_map/ppermute | solution.py:308
  41.2 0.6 pad_add_fusion.ids_ref
  44.8 1.1 copy.36
  45.9 1.2 pad.15.clone
  47.1 0.6 concatenate.48.par_ref
  47.9 0.7 maximum_maximum_fusion.wc_ref
  48.6 2.1 %fusion.6 = (bf16[1,6528]{1,0:T(2,128)(2,1)S(1)}, bf16[1,6528]{1,0:T(2,128)(2,1)S(1)}) fusion(pred[]{:T(512)} %bitcast.8, bf16[32,2,6528]{2,1,0:T(2,128)(2,1)} %collective-permute-done, s32[]{:T(128)S(6)} %select_n.60, s32[]{:T(128)S(6)} %select_n.61, bf16[32,2,6528]{2,1,0:T(2,128)(2,1)S(1)} %all-to-all-done, s32[]{:T(128)S(6)} %select_n.56, ...), kind=kLoop, calls=%fused_computation.30 | loop fusion | flops 13056 | bytes 78354 | tf_op jit(solution)/shard_map/squeeze | solution.py:262
  50.8 1.4 %reshape.46.x_ref = bf16[1280,10]{1,0:T(8,128)(2,1)} reshape(bf16[2,6400]{1,0:T(2,128)(2,1)S(1)} %fusion.8) | data formatting | bytes 51200 | tf_op jit(solution)/shard_map/reshape | solution.py:310
  52.8 29.3 %encoder.1 = (bf16[1280,512]{1,0:T(8,128)(2,1)}, f32[1568,256]{1,0:T(8,128)}, bf16[1568,256]{1,0:T(8,128)(2,1)}) custom-call(s32[2]{0:T(128)} %pad_add_fusion.ids_ref, bf16[1280,10]{1,0:T(8,128)(2,1)} %reshape.46.x_ref, bf16[64,1024]{1,0:T(8,128)(2,1)} %maximum_maximum_fusion.wc_ref, f32[8,512]{1,0:T(8,128)} %concatenate.48.par_ref, f32[1280,1]{1,0:T(8,128)} %bitcast.44, ...), custom_call_target="tpu_custom_call" | custom-call | tf_op jit(solution)/shard_map/encoder/pallas_call | solution.py:192
  82.3 3.8 %copy.31 = bf16[2,639,512]{2,0,1:T(2,128)(2,1)} copy(bf16[2,639,512]{2,1,0:T(8,128)(2,1)} %bitcast.45) | data formatting | bytes 2617344 | tf_op jit(solution)/shard_map/optimization_barrier | solution.py:276
  86.1 0.9 copy-done.2
  87.0 1.3 convert_add_fusion
  88.5 1.3 collective-permute-start.5
  89.8 2.4 %collective-permute-start.6 = (bf16[416,256]{1,0:T(8,128)(2,1)S(1)}, bf16[416,256]{1,0:T(8,128)(2,1)S(1)}, u32[]{:S(2)}, u32[]{:S(2)}) collective-permute-start(bf16[416,256]{1,0:T(8,128)(2,1)S(1)} %get-tuple-element.30), channel_id=1, source_target_pairs={{0,2},{1,3},{2,0},{3,1},{4,6},{5,7},{6,4},{7,5},{8,10},{9,11},{10,... | collective-permute-start | bytes 638984 | tf_op jit(solution)/shard_map/ppermute | solution.py:280
  92.5 2.5 %collective-permute-done.5 = bf16[416,256]{1,0:T(8,128)(2,1)S(1)} collective-permute-done((bf16[416,256]{1,0:T(8,128)(2,1)S(1)}, bf16[416,256]{1,0:T(8,128)(2,1)S(1)}, u32[]{:S(2)}, u32[]{:S(2)}) %collective-permute-start.5) | collective-permute-done | bytes 213024 | tf_op jit(solution)/shard_map/ppermute | solution.py:280
  95.0 6.8 %collective-permute-done.6 = bf16[416,256]{1,0:T(8,128)(2,1)S(1)} collective-permute-done((bf16[416,256]{1,0:T(8,128)(2,1)S(1)}, bf16[416,256]{1,0:T(8,128)(2,1)S(1)}, u32[]{:S(2)}, u32[]{:S(2)}) %collective-permute-start.6) | collective-permute-done | bytes 213024 | tf_op jit(solution)/shard_map/ppermute | solution.py:280
  101.8 2.2 %collective-permute-done.7 = bf16[416,256]{1,0:T(8,128)(2,1)S(1)} collective-permute-done((bf16[416,256]{1,0:T(8,128)(2,1)S(1)}, bf16[416,256]{1,0:T(8,128)(2,1)S(1)}, u32[]{:S(2)}, u32[]{:S(2)}) %collective-permute-start.7) | collective-permute-done | bytes 213024 | tf_op jit(solution)/shard_map/ppermute | solution.py:280
  104.1 13.9 %all_to_all.15 = bf16[32,26,128]{2,1,0:T(8,128)(2,1)S(1)} all-to-all(bf16[32,26,128]{2,1,0:T(8,128)(2,1)S(1)} %reshape.51), channel_id=1, replica_groups={{0,8,16,24,32,40,48,56,64,72,80,88,96,104,112,120,128,136,144,152,160,1..., dimensions={0} | all-to-all | bytes 425984 | tf_op jit(solution)/shard_map/all_to_all | solution.py:244
  118.1 0.7 broadcast_in_dim.33
  118.8 5.3 %all-to-all-start.2 = ((bf16[32,26,128]{2,1,0:T(8,128)(2,1)}), bf16[32,26,128]{2,1,0:T(8,128)(2,1)S(1)}, u32[]{:S(2)}, u32[]{:S(2)}) async-start(bf16[32,26,128]{2,1,0:T(8,128)(2,1)} %broadcast_in_dim.33), calls=%async_computation.2 | async-start | bytes 524288 | tf_op jit(solution)/shard_map/all_to_all | solution.py:244
  124.1 9.7 %all-to-all-done.2 = bf16[32,26,128]{2,1,0:T(8,128)(2,1)S(1)} async-done(((bf16[32,26,128]{2,1,0:T(8,128)(2,1)}), bf16[32,26,128]{2,1,0:T(8,128)(2,1)S(1)}, u32[]{:S(2)}, u32[]{:S(2)}) %all-to-all-start.2) | async-done | bytes 213024 | tf_op jit(solution)/shard_map/all_to_all | solution.py:244
  134.0 4.4 %collective-permute-start.8 = (bf16[384,256]{0,1:T(8,128)(2,1)S(1)}, bf16[384,256]{0,1:T(8,128)(2,1)S(1)}, u32[]{:S(2)}, u32[]{:S(2)}) collective-permute-start(bf16[384,256]{0,1:T(8,128)(2,1)S(1)} %bitcast.48), channel_id=1, source_target_pairs={{0,4},{4,0},{8,12},{12,8},{16,20},{20,16},{24,28},{28,24},{32,36},... | collective-permute-start | bytes 589832 | tf_op jit(solution)/shard_map/ppermute | solution.py:289
  138.5 0.6 maximum_convert_fusion
  139.6 1.1 copy.30
  (67 shorter events, 4.3 us)
Async XLA Ops:
  0.6 19.1 %copy-start.9 = (s32[2]{0:T(128)S(1)}, s32[2]{0:T(128)}, u32[]{:S(2)}) copy-start(s32[2]{0:T(128)} %param.13) | copy-start | bytes 28
  0.6 20.4 %copy-start.4 = (s32[2,639]{1,0:T(2,128)S(1)}, s32[2,639]{1,0:T(2,128)}, u32[]{:S(2)}) copy-start(s32[2,639]{1,0:T(2,128)} %param.14) | copy-start | bytes 15340
  0.7 21.0 %copy-start.3 = (bf16[10,512]{1,0:T(8,128)(2,1)S(1)}, bf16[10,512]{1,0:T(8,128)(2,1)}, u32[]{:S(2)}) copy-start(bf16[10,512]{1,0:T(8,128)(2,1)} %param.16) | copy-start | bytes 30724
  0.7 43.8 %copy-start.1 = (bf16[2,639,512]{2,0,1:T(2,128)(2,1)S(1)}, bf16[2,639,512]{2,0,1:T(2,128)(2,1)}, u32[]{:S(2)}) copy-start(bf16[2,639,512]{2,0,1:T(2,128)(2,1)} %param.15) | copy-start | bytes 3926020
  3.8 32.2 %all-to-all-start = ((bf16[32,2,6528]{2,1,0:T(2,128)(2,1)}), bf16[32,2,6528]{2,1,0:T(2,128)(2,1)S(1)}, u32[]{:S(2)}, u32[]{:S(2)}) async-start(bf16[32,2,6528]{2,1,0:T(2,128)(2,1)} %broadcast_in_dim.13), calls=%async_computation | async-start | bytes 1671168 | tf_op jit(solution)/shard_map/all_to_all | solution.py:244
  15.8 37.0 %collective-permute-start.1 = (bf16[384,512]{1,0:T(8,128)(2,1)}, bf16[384,512]{1,0:T(8,128)(2,1)}, u32[]{:S(2)}, u32[]{:S(2)}) collective-permute-start(bf16[384,512]{1,0:T(8,128)(2,1)} %wa_hbm.1), channel_id=1, source_target_pairs={{0,1},{1,0},{2,3},{3,2},{4,5},{5,4},{6,7},{7,6},{8,9},{9,8},{10,11... | collective-permute-start | bytes 1179656 | tf_op jit(solution)/shard_map/ppermute | solution.py:268
  17.1 35.7 %collective-permute-start.2 = (bf16[384,512]{1,0:T(8,128)(2,1)}, bf16[384,512]{1,0:T(8,128)(2,1)}, u32[]{:S(2)}, u32[]{:S(2)}) collective-permute-start(bf16[384,512]{1,0:T(8,128)(2,1)} %wa_hbm.1), channel_id=1, source_target_pairs={{0,2},{1,3},{2,0},{3,1},{4,6},{5,7},{6,4},{7,5},{8,10},{9,11},{10,... | collective-permute-start | bytes 1179656 | tf_op jit(solution)/shard_map/ppermute | solution.py:268
  19.6 33.2 %collective-permute-start.3 = (bf16[384,512]{1,0:T(8,128)(2,1)}, bf16[384,512]{1,0:T(8,128)(2,1)}, u32[]{:S(2)}, u32[]{:S(2)}) collective-permute-start(bf16[384,512]{1,0:T(8,128)(2,1)} %wa_hbm.1), channel_id=1, source_target_pairs={{0,3},{1,2},{2,1},{3,0},{4,7},{5,6},{6,5},{7,4},{8,11},{9,10},{10,... | collective-permute-start | bytes 1179656 | tf_op jit(solution)/shard_map/ppermute | solution.py:268
  35.9 12.7 %collective-permute-start = (bf16[32,2,6528]{2,1,0:T(2,128)(2,1)S(1)}, bf16[32,2,6528]{2,1,0:T(2,128)(2,1)}, u32[]{:S(2)}, u32[]{:S(2)}) collective-permute-start(bf16[32,2,6528]{2,1,0:T(2,128)(2,1)S(1)} %all-to-all-done), channel_id=1, source_target_pairs={{0,4},{4,0},{8,12},{12,8},{16,20},{20,16},{24,28},{28,24},{32,36},... | collective-permute-start | bytes 2506760 | tf_op jit(solution)/shard_map/ppermute | solution.py:308
  44.7 2.4 %copy-start.5 = (f32[512]{0:T(512)S(1)}, f32[512]{0:T(512)}, u32[]{:S(2)}) copy-start(f32[512]{0:T(512)} %param.17) | copy-start | bytes 6148
  44.7 2.4 %copy-start.6 = (f32[512]{0:T(512)S(1)}, f32[512]{0:T(512)}, u32[]{:S(2)}) copy-start(f32[512]{0:T(512)} %param.18) | copy-start | bytes 6148
  44.8 2.4 %copy-start.7 = (f32[512]{0:T(512)S(1)}, f32[512]{0:T(512)}, u32[]{:S(2)}) copy-start(f32[512]{0:T(512)} %param.20) | copy-start | bytes 6148
  44.8 2.4 %copy-start.8 = (f32[512]{0:T(512)S(1)}, f32[512]{0:T(512)}, u32[]{:S(2)}) copy-start(f32[512]{0:T(512)} %param.21) | copy-start | bytes 6148
  82.1 4.9 %copy-start = (f32[1568,256]{1,0:T(8,128)S(1)}, f32[1568,256]{1,0:T(8,128)}, u32[]{:S(2)}) copy-start(f32[1568,256]{1,0:T(8,128)} %get-tuple-element.8) | copy-start | bytes 4816900
  82.2 4.0 %collective-permute-start.4 = (bf16[1568,256]{1,0:T(8,128)(2,1)}, bf16[1568,256]{1,0:T(8,128)(2,1)S(1)}, u32[]{:S(2)}, u32[]{:S(2)}) collective-permute-start(bf16[1568,256]{1,0:T(8,128)(2,1)} %get-tuple-element.9), channel_id=1, source_target_pairs={{0,4},{4,0},{8,12},{12,8},{16,20},{20,16},{24,28},{28,24},{32,36},... | collective-permute-start | bytes 2408456 | tf_op jit(solution)/shard_map/ppermute | solution.py:274
  86.1 0.9 copy-start.2
  88.5 6.6 %collective-permute-start.5 = (bf16[416,256]{1,0:T(8,128)(2,1)S(1)}, bf16[416,256]{1,0:T(8,128)(2,1)S(1)}, u32[]{:S(2)}, u32[]{:S(2)}) collective-permute-start(bf16[416,256]{1,0:T(8,128)(2,1)S(1)} %get-tuple-element.28), channel_id=1, source_target_pairs={{0,1},{1,0},{2,3},{3,2},{4,5},{5,4},{6,7},{7,6},{8,9},{9,8},{10,11... | collective-permute-start | bytes 638984 | tf_op jit(solution)/shard_map/ppermute | solution.py:280
  89.8 12.0 %collective-permute-start.6 = (bf16[416,256]{1,0:T(8,128)(2,1)S(1)}, bf16[416,256]{1,0:T(8,128)(2,1)S(1)}, u32[]{:S(2)}, u32[]{:S(2)}) collective-permute-start(bf16[416,256]{1,0:T(8,128)(2,1)S(1)} %get-tuple-element.30), channel_id=1, source_target_pairs={{0,2},{1,3},{2,0},{3,1},{4,6},{5,7},{6,4},{7,5},{8,10},{9,11},{10,... | collective-permute-start | bytes 638984 | tf_op jit(solution)/shard_map/ppermute | solution.py:280
  92.2 11.8 %collective-permute-start.7 = (bf16[416,256]{1,0:T(8,128)(2,1)S(1)}, bf16[416,256]{1,0:T(8,128)(2,1)S(1)}, u32[]{:S(2)}, u32[]{:S(2)}) collective-permute-start(bf16[416,256]{1,0:T(8,128)(2,1)S(1)} %get-tuple-element.29), channel_id=1, source_target_pairs={{0,3},{1,2},{2,1},{3,0},{4,7},{5,6},{6,5},{7,4},{8,11},{9,10},{10,... | collective-permute-start | bytes 638984 | tf_op jit(solution)/shard_map/ppermute | solution.py:280
  118.8 14.9 %all-to-all-start.2 = ((bf16[32,26,128]{2,1,0:T(8,128)(2,1)}), bf16[32,26,128]{2,1,0:T(8,128)(2,1)S(1)}, u32[]{:S(2)}, u32[]{:S(2)}) async-start(bf16[32,26,128]{2,1,0:T(8,128)(2,1)} %broadcast_in_dim.33), calls=%async_computation.2 | async-start | bytes 524288 | tf_op jit(solution)/shard_map/all_to_all | solution.py:244
  134.0 5.4 %collective-permute-start.8 = (bf16[384,256]{0,1:T(8,128)(2,1)S(1)}, bf16[384,256]{0,1:T(8,128)(2,1)S(1)}, u32[]{:S(2)}, u32[]{:S(2)}) collective-permute-start(bf16[384,256]{0,1:T(8,128)(2,1)S(1)} %bitcast.48), channel_id=1, source_target_pairs={{0,4},{4,0},{8,12},{12,8},{16,20},{20,16},{24,28},{28,24},{32,36},... | collective-permute-start | bytes 589832 | tf_op jit(solution)/shard_map/ppermute | solution.py:289

commit v3 on v2

v3 whole, which is shorter than its diff:
```python
import math

import jax
import jax.numpy as jnp
from jax import lax
from jax.experimental import pallas as pl
from jax.experimental.pallas import tpu as pltpu
from jax.sharding import Mesh
from jax.sharding import PartitionSpec as P

f32 = jnp.float32
bf = jnp.bfloat16
WIDTH = 512
HALF = 256
ROWS = 640
SAMPLES = 6400
LOSS_SCALE = 1.0 / math.sqrt(512 * 639)
PART = 96
SLOTS = PART + 16
VMEM_LIMIT = 60 * 1024 * 1024
M1, TA, TB, TC = 256, 256, 256, 320
NN = (((1,), (0,)), ((), ()))
NT = (((1,), (1,)), ((), ()))
TN = (((0,), (0,)), ((), ()))


def gelu_parts(y):
    d = 1.0 + 0.23164189 * jnp.abs(y)
    t = pl.reciprocal(d, approx=True)
    t = t * (2.0 - d * t)
    e = jnp.exp2(y * (y * (-0.5 * 1.4426950408889634)))
    poly = t * (0.127414796 + t * (-0.142248368 + t * (0.7107068705 + t * (-0.7265760135 + t * 0.5307027145))))
    tail = poly * e
    return jnp.where(y >= 0, 1.0 - tail, tail), e


def lane_sum(v):
    return jnp.sum(v, axis=-1, keepdims=True)


def rows8(v):
    return jnp.sum(v.reshape(v.shape[0] // 8, 8, v.shape[1]), axis=0)


def dot(a, b, dims=NN):
    return lax.dot_general(a, b, dims, preferred_element_type=f32)


def shifted_up(v, below):
    return jnp.concatenate([v, below], 0)[1:v.shape[0] + 1]


def shifted_down(v, above):
    return jnp.concatenate([above, v], 0)[7:v.shape[0] + 7]


def norm_back(q, n, inv):
    qn = q * n
    inner = lane_sum(q) * (1.0 / WIDTH)
    along = lane_sum(qn) * (1.0 / WIDTH)
    return inv * (q - inner - n * along), qn


def encoder_kernel(ids_ref, x_ref, wc_ref, par_ref, tail_ref, cot_hbm, wa_hbm, wb_hbm, wc_hbm, wd_hbm,
                   feat_ref, keep_ref, send_ref,
                   w2_ref, cot_ref, sems, p_ref, small_ref, c_ref, u_ref, s_ref, d_ref, sg_ref, r1_ref, dl_ref, t_ref):
    total = x_ref.shape[0]
    core = ids_ref[0]
    part = wa_hbm.shape[0]
    loads = []
    for k, src in enumerate((wa_hbm, wb_hbm, wc_hbm, wd_hbm)):
        at = pl.multiple_of((ids_ref[1] ^ k) * part, part)
        loads.append(pltpu.make_async_copy(src, w2_ref.at[pl.ds(at, part), :], sems.at[k]))
    loads.append(pltpu.make_async_copy(cot_hbm, cot_ref, sems.at[4]))
    for load in loads:
        load.start()
    gain1, shift1, gain2, shift2 = (par_ref[k:k + 1, :] for k in range(4))
    zero = jnp.zeros((8, WIDTH), f32)
    tail = tail_ref[:, SAMPLES:].astype(f32)
    length = tail[:, 0:1] * 128.0 + tail[:, 1:2]

    def rows(i, size):
        return pl.ds(pl.multiple_of(i * size, size), size)

    now = x_ref[...].astype(f32)
    later = shifted_up(now, jnp.zeros((8, now.shape[1]), f32))
    k = lax.broadcasted_iota(jnp.int32, (10, 128), 0)
    lane = lax.broadcasted_iota(jnp.int32, (10, 128), 1)
    step = lane - lane // 20 * 20
    used = lane < 60
    place = jnp.where(used & (step == k), 1.0, 0.0).astype(bf)
    place_later = jnp.where(used & (step == k + 10), 1.0, 0.0).astype(bf)
    p_ref[...] = (dot(now.astype(bf), place) + dot(later.astype(bf), place_later)).astype(bf)

    def conv1(i, _):
        r = rows(i, M1)
        c_ref[r, :] = dot(p_ref[r, 0:64], wc_ref[...])
        return 0
    lax.fori_loop(0, total // M1, conv1, 0)

    def level_one(t, below):
        r = rows(t, TA)
        for half in range(2):
            c = c_ref[r, half * WIDTH:(half + 1) * WIDTH]
            inv = lax.rsqrt(lane_sum(c * c) * (1.0 / WIDTH) + 1e-5)
            y = c * inv * gain1 + shift1
            phi, e = gelu_parts(y)
            h = y * phi
            sg_ref[half, r, :] = (phi + (y * 0.3989422804014327) * e) * gain1
            r1_ref[half, r, :] = inv
            u_ref[r, half * WIDTH:(half + 1) * WIDTH] = h.astype(bf)
            if half == 0:
                u_ref[r, 2 * WIDTH:] = shifted_up(h, below).astype(bf)
                first = h[0:8]
        return first

    def conv2(t):
        r = rows(t, TA)
        s_ref[r, :] = dot(u_ref[r, :], w2_ref[...])

    def forward(i, below):
        t = total // TA - 2 - i
        conv2(t + 1)
        return level_one(t, below)
    below = level_one(total // TA - 1, zero)
    for load in loads[:4]:
        load.wait()
    lax.fori_loop(0, total // TA - 1, forward, below)
    conv2(0)

    loads[4].wait()

    def level_two(t, carry):
        acc_a, acc_b, above = carry
        b = pl.multiple_of(t * TB, TB)
        r = pl.ds(b, TB)
        z = s_ref[r, :]
        c = z - lane_sum(z) * (1.0 / WIDTH)
        inv = lax.rsqrt(lane_sum(c * c) * (1.0 / WIDTH) + 1e-5)
        n = c * inv
        y = n * gain2 + shift2
        phi, e = gelu_parts(y)
        feat_ref[r, :] = (y * phi).astype(bf)
        slope = phi + (y * 0.3989422804014327) * e
        row = (lax.broadcasted_iota(jnp.int32, (TB, 1), 0) + b).astype(f32)
        room = jnp.where(row < ROWS, length[0:1], length[1:2] + 10.0 * ROWS)
        weight = jnp.where(10.0 * row + 19.0 < room, LOSS_SCALE, 0.0)
        q = cot_ref[r, :].astype(f32) * weight * (slope * gain2)
        back, qn = norm_back(q, n, inv)
        dl_ref[r, 0:WIDTH] = back.astype(bf)
        dl_ref[r, WIDTH:] = shifted_down(back, above).astype(bf)
        return acc_a + rows8(qn), acc_b + rows8(q), back[TB - 8:TB]

    def down(t):
        r = rows(t, TB)
        now = dl_ref[r, 0:WIDTH]
        d_ref[r, 0:WIDTH] = dot(now, w2_ref[0:WIDTH, :], NT) + dot(dl_ref[r, WIDTH:], w2_ref[2 * WIDTH:, :], NT)
        d_ref[r, WIDTH:] = dot(now, w2_ref[WIDTH:2 * WIDTH, :], NT)

    def middle(t, carry):
        down(t - 1)
        return level_two(t, carry)
    carry = level_two(0, (zero, zero, zero))
    acc_a, acc_b, _ = lax.fori_loop(1, total // TB, middle, carry)
    down(total // TB - 1)
    small_ref[12:13, :] = jnp.sum(acc_a, axis=0, keepdims=True) / gain2
    small_ref[13:14, :] = jnp.sum(acc_b, axis=0, keepdims=True) / gain2
    small_ref[14:16, :] = jnp.zeros((2, WIDTH), f32)

    def backward(i, acc):
        acc_a, acc_b = acc
        chunk = 3 * WIDTH // (total // TC)
        for ref, half in ((keep_ref, core), (send_ref, 1 - core)):
            cols = pl.ds(pl.multiple_of(half * HALF, HALF), HALF)
            grad = dot(u_ref[:, pl.ds(pl.multiple_of(i * chunk, chunk), chunk)], dl_ref[:, cols], TN).astype(ref.dtype)
            for j in range(4):
                ref[4 * j + i, 0:PART, :] = grad[j * PART:(j + 1) * PART]
        r = rows(i, TC)
        for half in range(2):
            lanes = slice(half * WIDTH, (half + 1) * WIDTH)
            q = d_ref[r, lanes] * sg_ref[half, r, :]
            inv = r1_ref[half, r, :]
            back, qn = norm_back(q, c_ref[r, lanes] * inv, inv)
            t_ref[r, lanes] = back.astype(bf)
            acc_a = acc_a + rows8(qn)
            acc_b = acc_b + rows8(q)
        return acc_a, acc_b
    acc_a, acc_b = lax.fori_loop(0, total // TC, backward, (zero, zero))
    small_ref[10:11, :] = jnp.sum(acc_a, axis=0, keepdims=True) / gain1
    small_ref[11:12, :] = jnp.sum(acc_b, axis=0, keepdims=True) / gain1
    taps = dot(p_ref[:, 0:32], t_ref[...], TN)
    small_ref[0:10, :] = taps[0:10, 0:WIDTH] + taps[5:15, WIDTH:]
    small = small_ref[...].astype(bf)
    for j in range(4):
        quarter = jnp.concatenate([small[:, 128 * j:128 * (j + 1)], jnp.zeros((16, 128), bf)], 1)
        for i in range(4):
            send_ref[4 * j + i, PART:SLOTS, :] = quarter
            keep_ref[4 * j + i, PART:SLOTS, :] = quarter.astype(f32)


def pick_kernel(ids_ref, source_ref, own_hbm, other_hbm, out_ref, slab_ref, sems):
    for i in range(2):
        holder = source_ref[i] >> 3
        local = (holder & 1) == ids_ref[0]

        @pl.when(local)
        def _():
            pltpu.make_async_copy(own_hbm.at[holder >> 1], slab_ref.at[i], sems.at[i]).start()

        @pl.when(jnp.logical_not(local))
        def _():
            pltpu.make_async_copy(other_hbm.at[holder >> 1], slab_ref.at[i], sems.at[i]).start()
    crops = []
    for i in range(2):
        pltpu.make_async_copy(own_hbm.at[0], slab_ref.at[i], sems.at[i]).wait()
        both = slab_ref[i].astype(f32)
        crops.append(jnp.where((source_ref[i] & 1) == 0, both[0:1], both[1:2]))
    row = lax.broadcasted_iota(jnp.int32, out_ref.shape, 0)
    out_ref[...] = jnp.where(row == 0, crops[0], crops[1]).astype(bf)


def pick(ids, source, own, other):
    smem, hbm = pl.BlockSpec(memory_space=pltpu.SMEM), pl.BlockSpec(memory_space=pl.ANY)
    shape = own.shape[1:]
    return pl.pallas_call(
        pick_kernel,
        out_shape=jax.ShapeDtypeStruct(shape, bf),
        in_specs=[smem, smem, hbm, hbm],
        out_specs=pl.BlockSpec(memory_space=pltpu.VMEM),
        scratch_shapes=[pltpu.VMEM((2,) + shape, bf), pltpu.SemaphoreType.DMA((2,))],
        name="pick",
    )(ids, source, own, other)


def encoder(ids, x, wc, par, tail, cot, parts):
    total = x.shape[0]
    vm = pl.BlockSpec(memory_space=pltpu.VMEM)
    hbm = pl.BlockSpec(memory_space=pl.ANY)
    return pl.pallas_call(
        encoder_kernel,
        out_shape=(
            jax.ShapeDtypeStruct((total, WIDTH), bf),
            jax.ShapeDtypeStruct((16, SLOTS, HALF), f32),
            jax.ShapeDtypeStruct((16, SLOTS, HALF), bf),
        ),
        in_specs=[pl.BlockSpec(memory_space=pltpu.SMEM)] + [vm] * 4 + [hbm] * 5,
        out_specs=(vm,) * 3,
        scratch_shapes=[
            pltpu.VMEM((3 * WIDTH, WIDTH), bf),
            pltpu.VMEM((total, WIDTH), bf),
            pltpu.SemaphoreType.DMA((5,)),
            pltpu.VMEM((total, 128), bf),
            pltpu.VMEM((16, WIDTH), f32),
            pltpu.VMEM((total, 2 * WIDTH), f32),
            pltpu.VMEM((total, 3 * WIDTH), bf),
            pltpu.VMEM((total, WIDTH), f32),
            pltpu.VMEM((total, 2 * WIDTH), f32),
            pltpu.VMEM((2, total, WIDTH), f32),
            pltpu.VMEM((2, total, 1), f32),
            pltpu.VMEM((total, 2 * WIDTH), bf),
            pltpu.VMEM((total, 2 * WIDTH), bf),
        ],
        compiler_params=pltpu.CompilerParams(vmem_limit_bytes=VMEM_LIMIT),
        name="encoder",
    )(ids, x, wc, par, tail, cot, *parts)


def prep_weights(conv1_weight):
    w1 = conv1_weight.astype(f32)
    wc = w1 - jnp.mean(w1, axis=1, keepdims=True)
    z5 = jnp.zeros((5, WIDTH), f32)
    z10 = jnp.zeros((10, WIDTH), f32)
    both = jnp.concatenate([jnp.concatenate([wc, z10], 0), jnp.concatenate([z5, wc, z5], 0)], 1)
    hi = lax.reduce_precision(both, 8, 7)
    mid = lax.reduce_precision(both - hi, 8, 7)
    low = both - hi - mid
    return jnp.concatenate([hi.astype(bf), mid.astype(bf), low.astype(bf), jnp.zeros((4, 2 * WIDTH), bf)], 0)


Y, Z, C, X = 4, 8, 2, 4
AXES = ("y", "z", "c", "x")


def flip(value, axis, size, k):
    return lax.ppermute(value, axis, [(i, i ^ k) for i in range(size)])


def turn(value, axis, size, k):
    return lax.ppermute(value, axis, [(i, (i + k) % size) for i in range(size)])


def exchange(chunks, axes):
    return lax.all_to_all(chunks, axes, 0, 0, tiled=True)


def pack(waveform, lengths):
    count = waveform.shape[0]
    at = lax.broadcasted_iota(jnp.int32, (count, SAMPLES + 128), 1)
    end = lengths[:, None]
    wide = jnp.pad(waveform, ((0, 0), (0, 128)))
    code = jnp.where(at == SAMPLES, end >> 7, jnp.where(at == SAMPLES + 1, end & 127, 0)).astype(bf)
    return jnp.where(at < SAMPLES, jnp.where(at < end, wide, jnp.zeros_like(wide)), code)


def reduce_grads(keep, send, core, shadow):
    chunks = (keep + flip(send, "c", C, 1).astype(f32)).astype(bf)
    total = jnp.sum(exchange(chunks, ("y", "x")).astype(f32), axis=0).astype(bf)
    total, shadow = lax.optimization_barrier((total, shadow))
    total = (total.astype(f32) + flip(total, "z", Z, 1).astype(f32)).astype(bf)
    a, b, c = (turn(total, "z", Z, k).astype(f32) for k in (2, 4, 6))
    total = ((total.astype(f32) + b) + (a + c)).astype(bf)
    quarters = jnp.stack([total] + [flip(total, "y", Y, k) for k in (1, 2, 3)])
    y = lax.axis_index("y")
    every = jnp.concatenate([lax.dynamic_slice_in_dim(quarters, y ^ q, 1, 0) for q in range(Y)], 0)
    half = every[:, :PART].reshape(-1, HALF)
    other = flip(half, "c", C, 1)
    grad_conv2 = jnp.where(core == 0, jnp.concatenate([half, other], 1), jnp.concatenate([other, half], 1))
    small = jnp.concatenate([every[q, PART:PART + 14, :128] for q in range(Y)], 1)
    return grad_conv2.astype(f32), small.astype(f32), shadow


def body(waveform, lengths, source, frame_mask, cotangent, conv1_weight, gain_one, shift_one,
         conv2_weight, gain_two, shift_two):
    count, frames = frame_mask.shape
    core, x = lax.axis_index("c"), lax.axis_index("x")
    own = pack(waveform, lengths)
    column = exchange(jnp.broadcast_to(own[None], (Y * Z,) + own.shape), ("y", "z"))
    parts = [conv2_weight] + [flip(conv2_weight, "x", X, k) for k in (1, 2, 3)]
    masked = cotangent * frame_mask[:, :, None].astype(bf)
    upstream = jnp.pad(masked, ((0, 0), (0, 1), (0, 0))).reshape(count * ROWS, WIDTH)
    par = jnp.concatenate(
        [jnp.stack([gain_one, shift_one, gain_two, shift_two]), jnp.zeros((4, WIDTH), f32)], 0)
    wc = prep_weights(conv1_weight)
    ids = jnp.stack([core, x])
    column, parts, upstream, par, wc, ids = lax.optimization_barrier((column, parts, upstream, par, wc, ids))
    routed = pick(ids, source, column, flip(column, "c", C, 1))
    blocks = routed[:, :SAMPLES].reshape(count * ROWS, 10)
    feat, keep, send = encoder(ids, blocks, wc, par, routed, upstream, parts)
    features = feat.reshape(count, ROWS, WIDTH)[:, :frames]
    grad_conv2, grad_front, features = reduce_grads(keep, send, core, features)
    return features, grad_conv2, grad_front


def solution(mesh):
    grid = Mesh(mesh.devices.reshape(Y, Z, C, X), AXES)
    both = P(AXES)
    placed = (both, both, both, both, both, P(), P(), P(), P("x"), P(), P())
    return jax.shard_map(
        body,
        mesh=grid,
        in_specs=placed,
        out_specs=(both, P("x"), P()),
        check_vma=False,
    )
```

time: 141 us -> 126 us (0.89)
  blocking collectives: 13.9 us -> 0 us
  starting transfers between devices: 35 us -> 41.2 us
  local copies, waits for them, and re-layouts: 15 us -> 9.2 us
  between operations: 3.56 us -> 0.85 us
  Pallas kernels: 29.3 us -> 27.2 us
  other arithmetic: 8.24 us -> 9.94 us
    all_to_all x1 -> x0, blocking collectives: 13.9 us -> none  [exchange(): lax.all_to_all(chunks, 'dp', 0, 0, axis_index_groups=YZ_GROUPS, tiled=True)]
    ppermute x9 -> x13, waiting for transfers between devices: 11.8 us -> 24.1 us  [the longest x10 21.4 us: flip(): return lax.ppermute(value, axis, [(i, i ^ k) for i in range(size)])]
    all_to_all x2, waiting for transfers between devices: 23.8 us -> 12.5 us  [exchange(): return lax.all_to_all(chunks, axes, 0, 0, tiled=True)]
    ppermute x9 -> x13, starting transfers between devices: 17.7 us -> 24.7 us  [the longest x10 17.1 us: flip(): return lax.ppermute(value, axis, [(i, i ^ k) for i in range(size)])]
    pallas_call x1, Pallas kernels: 29.3 us -> 25.1 us  [encoder(): pl.pallas_call(encoder_kernel, out_shape=(jax.ShapeDtypeStruct((total, WI...]
    convert_element_type x1 -> x4, other arithmetic: 0.01 us -> 2.81 us  [the longest x1 2.75 us: reduce_grads(): chunks = (keep + flip(send, 'c', C, 1).astype(f32)).astype(bf)]
    unnamed x30 -> x27, local copies, waits for them, and re-layouts: 3.58 us -> 1.19 us
    squeeze x1 -> x0, other arithmetic: 2.13 us -> none  [pick(): jnp.where(local[i], lax.dynamic_slice(column, start, size), lax.dynamic_s...]
  transfers between devices with their start and end apart: 11 -> 15, of which waited for: 6 -> 11; matrix products, arithmetic and copies ran while one was open for 11% -> 7% of each run, Pallas kernels for 0% -> 0%
where the time goes in v3:
time: 126 us; the launch traced here: 125 us
  starting transfers between devices  41.2 us (33%)
  waiting for transfers between devices  36.6 us (29%)
  Pallas kernels  27.2 us (22%)
  other arithmetic  9.94 us (8%)
  local copies, waits for them, and re-layouts  9.2 us (7%)
    pallas_call x1, Pallas kernels, encoder(): pl.pallas_call(encoder_kernel, out_shape=(jax.ShapeDtypeStruct((total, WI...  25.1 us
    ppermute x10, waiting for transfers between devices, flip(): return lax.ppermute(value, axis, [(i, i ^ k) for i in range(size)])  21.4 us
    ppermute x10, starting transfers between devices, flip(): return lax.ppermute(value, axis, [(i, i ^ k) for i in range(size)])  17.1 us
    all_to_all x2, starting transfers between devices, exchange(): return lax.all_to_all(chunks, axes, 0, 0, tiled=True)  16.5 us
    all_to_all x2, waiting for transfers between devices, exchange(): return lax.all_to_all(chunks, axes, 0, 0, tiled=True)  12.5 us
    ppermute x3, starting transfers between devices, turn(): return lax.ppermute(value, axis, [(i, (i + k) % size) for i in range(size)])  7.64 us
    convert_element_type x1, other arithmetic, reduce_grads(): chunks = (keep + flip(send, 'c', C, 1).astype(f32)).astype(bf)  2.75 us
    ppermute x3, waiting for transfers between devices, turn(): return lax.ppermute(value, axis, [(i, (i + k) % size) for i in range(size)])  2.74 us
  transfers between devices with their start and end apart: 15, of which 11 were waited for; matrix products, arithmetic and copies ran while one was open for 7% of the time, Pallas kernels for 0%

profile of v3, /device:TPU:1, one launch (start us, length us, event | category | flops | bytes accessed | tf_op | source)
XLA Modules:
  0.0 125.0 jit_solution(13381107502391823998)
XLA Ops:
  1.4 0.9 broadcast_select_fusion
  2.3 1.3 %broadcast_in_dim.46 = bf16[32,2,6528]{2,1,0:T(2,128)(2,1)} broadcast(bf16[2,6528]{1,0:T(2,128)(2,1)S(1)} %broadcast_select_fusion), dimensions={1,2} | broadcast | bytes 861696 | tf_op jit(solution)/shard_map/broadcast_in_dim | solution.py:327
  3.7 12.0 %all-to-all-start = ((bf16[32,2,6528]{2,1,0:T(2,128)(2,1)}), bf16[32,2,6528]{2,1,0:T(2,128)(2,1)S(1)}, u32[]{:S(2)}, u32[]{:S(2)}) async-start(bf16[32,2,6528]{2,1,0:T(2,128)(2,1)} %broadcast_in_dim.46), calls=%async_computation | async-start | bytes 1671168 | tf_op jit(solution)/shard_map/all_to_all | solution.py:293
  15.7 1.3 %collective-permute-start = (bf16[384,512]{1,0:T(8,128)(2,1)S(1)}, bf16[384,512]{1,0:T(8,128)(2,1)S(1)}, u32[]{:S(2)}, u32[]{:S(2)}) collective-permute-start(bf16[384,512]{1,0:T(8,128)(2,1)S(1)} %copy-done.4), channel_id=1, source_target_pairs={{0,1},{1,0},{2,3},{3,2},{4,5},{5,4},{6,7},{7,6},{8,9},{9,8},{10,11... | collective-permute-start | bytes 1179656 | tf_op jit(solution)/shard_map/ppermute | solution.py:285
  17.0 2.5 %collective-permute-start.1 = (bf16[384,512]{1,0:T(8,128)(2,1)S(1)}, bf16[384,512]{1,0:T(8,128)(2,1)S(1)}, u32[]{:S(2)}, u32[]{:S(2)}) collective-permute-start(bf16[384,512]{1,0:T(8,128)(2,1)S(1)} %copy-done.4), channel_id=1, source_target_pairs={{0,2},{1,3},{2,0},{3,1},{4,6},{5,7},{6,4},{7,5},{8,10},{9,11},{10,... | collective-permute-start | bytes 1179656 | tf_op jit(solution)/shard_map/ppermute | solution.py:285
  20.1 2.0 %broadcast_multiply_fusion = bf16[2,639,512]{2,0,1:T(2,128)(2,1)S(1)} fusion(bf16[2,639,512]{2,0,1:T(2,128)(2,1)S(1)} %copy-done.2, bf16[2,639]{0,1:T(8,128)(2,1)S(1)} %copy.17), kind=kLoop, calls=%fused_computation.1 | loop fusion | flops 654336 | bytes 2619900 | tf_op jit(solution)/shard_map/mul | solution.py:329
  23.0 1.2 pad.10.clone
  25.0 0.8 maximum_maximum_fusion.wc_ref
  25.7 10.4 %collective-permute-done.1.wc_hbm = bf16[384,512]{1,0:T(8,128)(2,1)S(1)} collective-permute-done((bf16[384,512]{1,0:T(8,128)(2,1)S(1)}, bf16[384,512]{1,0:T(8,128)(2,1)S(1)}, u32[]{:S(2)}, u32[]{:S(2)}) %collective-permute-start.1) | collective-permute-done | bytes 393248 | tf_op jit(solution)/shard_map/ppermute | solution.py:285
  36.1 2.2 %collective-permute-done.2.wd_hbm = bf16[384,512]{1,0:T(8,128)(2,1)} collective-permute-done((bf16[384,512]{1,0:T(8,128)(2,1)S(1)}, bf16[384,512]{1,0:T(8,128)(2,1)}, u32[]{:S(2)}, u32[]{:S(2)}) %collective-permute-start.2) | collective-permute-done | bytes 393248 | tf_op jit(solution)/shard_map/ppermute | solution.py:285
  38.3 2.8 %collective-permute-start.3 = (bf16[32,2,6528]{2,1,0:T(2,128)(2,1)S(1)}, bf16[32,2,6528]{2,1,0:T(2,128)(2,1)S(1)}, u32[]{:S(2)}, u32[]{:S(2)}) collective-permute-start(bf16[32,2,6528]{2,1,0:T(2,128)(2,1)S(1)} %all-to-all-done.own_hbm), channel_id=1, source_target_pairs={{0,4},{4,0},{1,5},{5,1},{2,6},{6,2},{3,7},{7,3},{8,12},{12,8},{9,1... | collective-permute-start | bytes 2506760 | tf_op jit(solution)/shard_map/ppermute | solution.py:285
  41.1 2.0 %collective-permute-done.3.other_hbm = bf16[32,2,6528]{2,1,0:T(2,128)(2,1)S(1)} collective-permute-done((bf16[32,2,6528]{2,1,0:T(2,128)(2,1)S(1)}, bf16[32,2,6528]{2,1,0:T(2,128)(2,1)S(1)}, u32[]{:S(2)}, u32[]{:S(2)}) %collective-permute-start.3) | collective-permute-done | bytes 835616 | tf_op jit(solution)/shard_map/ppermute | solution.py:285
  43.1 0.9 copy-done.3
  44.0 2.1 %pick.1.tail_ref = bf16[2,6528]{1,0:T(2,128)(2,1)} custom-call(s32[2]{0:T(128)} %pad_add_fusion.ids_ref, s32[2]{0:T(128)} %source_ref.1, bf16[32,2,6528]{2,1,0:T(2,128)(2,1)} %copy-done, bf16[32,2,6528]{2,1,0:T(2,128)(2,1)} %copy-done.3), custom_call_target="tpu_custom_call" | custom-call | tf_op jit(solution)/shard_map/pick/pallas_call | solution.py:225
  46.1 0.8 slice.28
  46.9 1.4 %reshape.31.x_ref = bf16[1280,10]{1,0:T(8,128)(2,1)} reshape(bf16[2,6400]{1,0:T(2,128)(2,1)S(1)} %slice.28) | data formatting | bytes 51200 | tf_op jit(solution)/shard_map/reshape | solution.py:337
  48.3 25.1 %encoder.1 = (bf16[1280,512]{1,0:T(8,128)(2,1)}, f32[16,112,256]{2,1,0:T(8,128)}, bf16[16,112,256]{2,1,0:T(8,128)(2,1)}) custom-call(s32[2]{0:T(128)} %pad_add_fusion.ids_ref, bf16[1280,10]{1,0:T(8,128)(2,1)} %reshape.31.x_ref, bf16[64,1024]{1,0:T(8,128)(2,1)} %maximum_maximum_fusion.wc_ref, f32[8,512]{1,0:T(8,128)} %concatenate.27.par_ref, ...), custom_call_target="tpu_custom_call" | custom-call | tf_op jit(solution)/shard_map/encoder/pallas_call | solution.py:239
  74.0 2.3 %collective-permute-done.4 = bf16[16,112,256]{2,1,0:T(8,128)(2,1)S(1)} collective-permute-done((bf16[16,112,256]{2,1,0:T(8,128)(2,1)}, bf16[16,112,256]{2,1,0:T(8,128)(2,1)S(1)}, u32[]{:S(2)}, u32[]{:S(2)}) %collective-permute-start.4) | collective-permute-done | bytes 917536 | tf_op jit(solution)/shard_map/ppermute | solution.py:285
  76.3 2.8 %add_convert_fusion = bf16[16,112,256]{2,1,0:T(8,128)(2,1)} fusion(f32[16,112,256]{2,1,0:T(8,128)} %get-tuple-element.26, bf16[16,112,256]{2,1,0:T(8,128)(2,1)S(1)} %collective-permute-done.4), kind=kLoop, calls=%fused_computation | loop fusion | flops 1376256 | bytes 3670016 | tf_op jit(solution)/shard_map/convert_element_type | solution.py:306
  79.0 4.5 %all-to-all-start.1 = ((bf16[16,112,256]{2,1,0:T(8,128)(2,1)}), bf16[16,112,256]{2,1,0:T(8,128)(2,1)S(1)}, u32[]{:S(2)}, u32[]{:S(2)}) async-start(bf16[16,112,256]{2,1,0:T(8,128)(2,1)} %add_convert_fusion), calls=%async_computation.1 | async-start | bytes 1835008 | tf_op jit(solution)/shard_map/all_to_all | solution.py:293
  83.5 2.4 %copy.20 = bf16[2,639,512]{2,0,1:T(2,128)(2,1)} copy(bf16[2,639,512]{2,1,0:T(8,128)(2,1)S(1)} %bitcast.23) | data formatting | bytes 2617344 | tf_op jit(solution)/shard_map/optimization_barrier | solution.py:308
  85.9 12.5 %all-to-all-done.1 = bf16[16,112,256]{2,1,0:T(8,128)(2,1)S(1)} async-done(((bf16[16,112,256]{2,1,0:T(8,128)(2,1)}), bf16[16,112,256]{2,1,0:T(8,128)(2,1)S(1)}, u32[]{:S(2)}, u32[]{:S(2)}) %all-to-all-start.1) | async-done | bytes 917536 | tf_op jit(solution)/shard_map/all_to_all | solution.py:293
  98.6 2.3 %collective-permute-start.5 = (bf16[112,256]{1,0:T(8,128)(2,1)S(1)}, bf16[112,256]{1,0:T(8,128)(2,1)S(1)}, u32[]{:S(2)}, u32[]{:S(2)}) collective-permute-start(bf16[112,256]{1,0:T(8,128)(2,1)S(1)} %reduce_sum.22), channel_id=1, source_target_pairs={{0,8},{8,0},{16,24},{24,16},{32,40},{40,32},{48,56},{56,48},{1,9},... | collective-permute-start | bytes 172040 | tf_op jit(solution)/shard_map/ppermute | solution.py:285
  100.8 1.6 %collective-permute-done.5 = bf16[112,256]{1,0:T(8,128)(2,1)S(1)} collective-permute-done((bf16[112,256]{1,0:T(8,128)(2,1)S(1)}, bf16[112,256]{1,0:T(8,128)(2,1)S(1)}, u32[]{:S(2)}, u32[]{:S(2)}) %collective-permute-start.5) | collective-permute-done | bytes 57376 | tf_op jit(solution)/shard_map/ppermute | solution.py:285
  102.4 4.1 %collective-permute-start.6 = (bf16[112,256]{1,0:T(8,128)(2,1)S(1)}, bf16[112,256]{1,0:T(8,128)(2,1)S(1)}, u32[]{:S(2)}, u32[]{:S(2)}) collective-permute-start(bf16[112,256]{1,0:T(8,128)(2,1)S(1)} %add_convert_fusion.2), channel_id=1, source_target_pairs={{0,32},{8,40},{16,48},{24,56},{32,0},{40,8},{48,16},{56,24},{1,33}... | collective-permute-start | bytes 172040 | tf_op jit(solution)/shard_map/ppermute | solution.py:289
  106.8 3.3 %collective-permute-start.8 = (bf16[112,256]{1,0:T(8,128)(2,1)S(1)}, bf16[112,256]{1,0:T(8,128)(2,1)S(1)}, u32[]{:S(2)}, u32[]{:S(2)}) collective-permute-start(bf16[112,256]{1,0:T(8,128)(2,1)S(1)} %add_convert_fusion.2), channel_id=1, source_target_pairs={{0,48},{8,56},{16,0},{24,8},{32,16},{40,24},{48,32},{56,40},{1,49}... | collective-permute-start | bytes 172040 | tf_op jit(solution)/shard_map/ppermute | solution.py:289
  110.1 2.0 %collective-permute-done.7 = bf16[112,256]{1,0:T(8,128)(2,1)S(1)} collective-permute-done((bf16[112,256]{1,0:T(8,128)(2,1)S(1)}, bf16[112,256]{1,0:T(8,128)(2,1)S(1)}, u32[]{:S(2)}, u32[]{:S(2)}) %collective-permute-start.7) | collective-permute-done | bytes 57376 | tf_op jit(solution)/shard_map/ppermute | solution.py:289
  113.5 1.0 collective-permute-start.11
  114.5 1.1 collective-permute-start.9
  115.6 1.9 %collective-permute-done.10 = bf16[112,256]{1,0:T(8,128)(2,1)S(1)} collective-permute-done((bf16[112,256]{1,0:T(8,128)(2,1)S(1)}, bf16[112,256]{1,0:T(8,128)(2,1)S(1)}, u32[]{:S(2)}, u32[]{:S(2)}) %collective-permute-start.10) | collective-permute-done | bytes 57376 | tf_op jit(solution)/shard_map/ppermute | solution.py:285
  118.2 4.8 %collective-permute-start.12 = (bf16[384,256]{1,0:T(8,128)(2,1)S(1)}, bf16[384,256]{1,0:T(8,128)(2,1)S(1)}, u32[]{:S(2)}, u32[]{:S(2)}) collective-permute-start(bf16[384,256]{1,0:T(8,128)(2,1)S(1)} %bitcast.24), channel_id=1, source_target_pairs={{0,4},{4,0},{1,5},{5,1},{2,6},{6,2},{3,7},{7,3},{8,12},{12,8},{9,1... | collective-permute-start | bytes 589832 | tf_op jit(solution)/shard_map/ppermute | solution.py:285
  124.0 1.0 fusion
  (60 shorter events, 7.1 us)
Async XLA Ops:
  0.6 15.1 %copy-start.4 = (bf16[384,512]{1,0:T(8,128)(2,1)S(1)}, bf16[384,512]{1,0:T(8,128)(2,1)}, u32[]{:S(2)}) copy-start(bf16[384,512]{1,0:T(8,128)(2,1)} %wa_hbm) | copy-start | bytes 1179652
  1.4 18.3 %copy-start.8 = (s32[2,639]{1,0:T(2,128)S(1)}, s32[2,639]{1,0:T(2,128)}, u32[]{:S(2)}) copy-start(s32[2,639]{1,0:T(2,128)} %param.14) | copy-start | bytes 15340
  2.3 17.6 %copy-start.7 = (bf16[10,512]{1,0:T(8,128)(2,1)S(1)}, bf16[10,512]{1,0:T(8,128)(2,1)}, u32[]{:S(2)}) copy-start(bf16[10,512]{1,0:T(8,128)(2,1)} %param.16) | copy-start | bytes 30724
  2.3 17.8 %copy-start.2 = (bf16[2,639,512]{2,0,1:T(2,128)(2,1)S(1)}, bf16[2,639,512]{2,0,1:T(2,128)(2,1)}, u32[]{:S(2)}) copy-start(bf16[2,639,512]{2,0,1:T(2,128)(2,1)} %param.15) | copy-start | bytes 3926020
  3.7 34.6 %all-to-all-start = ((bf16[32,2,6528]{2,1,0:T(2,128)(2,1)}), bf16[32,2,6528]{2,1,0:T(2,128)(2,1)S(1)}, u32[]{:S(2)}, u32[]{:S(2)}) async-start(bf16[32,2,6528]{2,1,0:T(2,128)(2,1)} %broadcast_in_dim.46), calls=%async_computation | async-start | bytes 1671168 | tf_op jit(solution)/shard_map/all_to_all | solution.py:293
  15.7 10.0 %collective-permute-start = (bf16[384,512]{1,0:T(8,128)(2,1)S(1)}, bf16[384,512]{1,0:T(8,128)(2,1)S(1)}, u32[]{:S(2)}, u32[]{:S(2)}) collective-permute-start(bf16[384,512]{1,0:T(8,128)(2,1)S(1)} %copy-done.4), channel_id=1, source_target_pairs={{0,1},{1,0},{2,3},{3,2},{4,5},{5,4},{6,7},{7,6},{8,9},{9,8},{10,11... | collective-permute-start | bytes 1179656 | tf_op jit(solution)/shard_map/ppermute | solution.py:285
  17.0 19.1 %collective-permute-start.1 = (bf16[384,512]{1,0:T(8,128)(2,1)S(1)}, bf16[384,512]{1,0:T(8,128)(2,1)S(1)}, u32[]{:S(2)}, u32[]{:S(2)}) collective-permute-start(bf16[384,512]{1,0:T(8,128)(2,1)S(1)} %copy-done.4), channel_id=1, source_target_pairs={{0,2},{1,3},{2,0},{3,1},{4,6},{5,7},{6,4},{7,5},{8,10},{9,11},{10,... | collective-permute-start | bytes 1179656 | tf_op jit(solution)/shard_map/ppermute | solution.py:285
  19.5 18.8 %collective-permute-start.2 = (bf16[384,512]{1,0:T(8,128)(2,1)S(1)}, bf16[384,512]{1,0:T(8,128)(2,1)}, u32[]{:S(2)}, u32[]{:S(2)}) collective-permute-start(bf16[384,512]{1,0:T(8,128)(2,1)S(1)} %copy-done.4), channel_id=1, source_target_pairs={{0,3},{1,2},{2,1},{3,0},{4,7},{5,6},{6,5},{7,4},{8,11},{9,10},{10,... | collective-permute-start | bytes 1179656 | tf_op jit(solution)/shard_map/ppermute | solution.py:285
  23.0 1.3 %copy-start.9 = (f32[512]{0:T(512)S(1)}, f32[512]{0:T(512)}, u32[]{:S(2)}) copy-start(f32[512]{0:T(512)} %param.17) | copy-start | bytes 6148
  23.0 1.3 %copy-start.10 = (f32[512]{0:T(512)S(1)}, f32[512]{0:T(512)}, u32[]{:S(2)}) copy-start(f32[512]{0:T(512)} %param.18) | copy-start | bytes 6148
  23.0 1.3 %copy-start.11 = (f32[512]{0:T(512)S(1)}, f32[512]{0:T(512)}, u32[]{:S(2)}) copy-start(f32[512]{0:T(512)} %param.20) | copy-start | bytes 6148
  23.0 1.3 %copy-start.12 = (f32[512]{0:T(512)S(1)}, f32[512]{0:T(512)}, u32[]{:S(2)}) copy-start(f32[512]{0:T(512)} %param.21) | copy-start | bytes 6148
  25.7 22.6 %copy-start.5 = (bf16[384,512]{1,0:T(8,128)(2,1)}, bf16[384,512]{1,0:T(8,128)(2,1)S(1)}, u32[]{:S(2)}) copy-start(bf16[384,512]{1,0:T(8,128)(2,1)S(1)} %collective-permute-done.wb_hbm) | copy-start | bytes 1179652
  36.1 12.2 %copy-start.6 = (bf16[384,512]{1,0:T(8,128)(2,1)}, bf16[384,512]{1,0:T(8,128)(2,1)S(1)}, u32[]{:S(2)}) copy-start(bf16[384,512]{1,0:T(8,128)(2,1)S(1)} %collective-permute-done.1.wc_hbm) | copy-start | bytes 1179652
  38.3 4.8 %copy-start = (bf16[32,2,6528]{2,1,0:T(2,128)(2,1)}, bf16[32,2,6528]{2,1,0:T(2,128)(2,1)S(1)}, u32[]{:S(2)}) copy-start(bf16[32,2,6528]{2,1,0:T(2,128)(2,1)S(1)} %all-to-all-done.own_hbm) | copy-start | bytes 2506756
  38.3 4.8 %collective-permute-start.3 = (bf16[32,2,6528]{2,1,0:T(2,128)(2,1)S(1)}, bf16[32,2,6528]{2,1,0:T(2,128)(2,1)S(1)}, u32[]{:S(2)}, u32[]{:S(2)}) collective-permute-start(bf16[32,2,6528]{2,1,0:T(2,128)(2,1)S(1)} %all-to-all-done.own_hbm), channel_id=1, source_target_pairs={{0,4},{4,0},{1,5},{5,1},{2,6},{6,2},{3,7},{7,3},{8,12},{12,8},{9,1... | collective-permute-start | bytes 2506760 | tf_op jit(solution)/shard_map/ppermute | solution.py:285
  43.1 0.9 copy-start.3
  73.4 2.8 %collective-permute-start.4 = (bf16[16,112,256]{2,1,0:T(8,128)(2,1)}, bf16[16,112,256]{2,1,0:T(8,128)(2,1)S(1)}, u32[]{:S(2)}, u32[]{:S(2)}) collective-permute-start(bf16[16,112,256]{2,1,0:T(8,128)(2,1)} %get-tuple-element.27), channel_id=1, source_target_pairs={{0,4},{4,0},{1,5},{5,1},{2,6},{6,2},{3,7},{7,3},{8,12},{12,8},{9,1... | collective-permute-start | bytes 2752520 | tf_op jit(solution)/shard_map/ppermute | solution.py:285
  79.0 4.5 %copy-start.1 = (bf16[1280,512]{1,0:T(8,128)(2,1)S(1)}, bf16[1280,512]{1,0:T(8,128)(2,1)}, u32[]{:S(2)}) copy-start(bf16[1280,512]{1,0:T(8,128)(2,1)} %get-tuple-element.28) | copy-start | bytes 3932164
  79.0 19.4 %all-to-all-start.1 = ((bf16[16,112,256]{2,1,0:T(8,128)(2,1)}), bf16[16,112,256]{2,1,0:T(8,128)(2,1)S(1)}, u32[]{:S(2)}, u32[]{:S(2)}) async-start(bf16[16,112,256]{2,1,0:T(8,128)(2,1)} %add_convert_fusion), calls=%async_computation.1 | async-start | bytes 1835008 | tf_op jit(solution)/shard_map/all_to_all | solution.py:293
  98.6 3.8 %collective-permute-start.5 = (bf16[112,256]{1,0:T(8,128)(2,1)S(1)}, bf16[112,256]{1,0:T(8,128)(2,1)S(1)}, u32[]{:S(2)}, u32[]{:S(2)}) collective-permute-start(bf16[112,256]{1,0:T(8,128)(2,1)S(1)} %reduce_sum.22), channel_id=1, source_target_pairs={{0,8},{8,0},{16,24},{24,16},{32,40},{40,32},{48,56},{56,48},{1,9},... | collective-permute-start | bytes 172040 | tf_op jit(solution)/shard_map/ppermute | solution.py:285
  102.4 7.6 %collective-permute-start.6 = (bf16[112,256]{1,0:T(8,128)(2,1)S(1)}, bf16[112,256]{1,0:T(8,128)(2,1)S(1)}, u32[]{:S(2)}, u32[]{:S(2)}) collective-permute-start(bf16[112,256]{1,0:T(8,128)(2,1)S(1)} %add_convert_fusion.2), channel_id=1, source_target_pairs={{0,32},{8,40},{16,48},{24,56},{32,0},{40,8},{48,16},{56,24},{1,33}... | collective-permute-start | bytes 172040 | tf_op jit(solution)/shard_map/ppermute | solution.py:289
  106.5 5.6 %collective-permute-start.7 = (bf16[112,256]{1,0:T(8,128)(2,1)S(1)}, bf16[112,256]{1,0:T(8,128)(2,1)S(1)}, u32[]{:S(2)}, u32[]{:S(2)}) collective-permute-start(bf16[112,256]{1,0:T(8,128)(2,1)S(1)} %add_convert_fusion.2), channel_id=1, source_target_pairs={{0,16},{8,24},{16,32},{24,40},{32,48},{40,56},{48,0},{56,8},{1,17}... | collective-permute-start | bytes 172040 | tf_op jit(solution)/shard_map/ppermute | solution.py:289
  106.8 6.0 %collective-permute-start.8 = (bf16[112,256]{1,0:T(8,128)(2,1)S(1)}, bf16[112,256]{1,0:T(8,128)(2,1)S(1)}, u32[]{:S(2)}, u32[]{:S(2)}) collective-permute-start(bf16[112,256]{1,0:T(8,128)(2,1)S(1)} %add_convert_fusion.2), channel_id=1, source_target_pairs={{0,48},{8,56},{16,0},{24,8},{32,16},{40,24},{48,32},{56,40},{1,49}... | collective-permute-start | bytes 172040 | tf_op jit(solution)/shard_map/ppermute | solution.py:289
  112.9 4.7 %collective-permute-start.10 = (bf16[112,256]{1,0:T(8,128)(2,1)S(1)}, bf16[112,256]{1,0:T(8,128)(2,1)S(1)}, u32[]{:S(2)}, u32[]{:S(2)}) collective-permute-start(bf16[112,256]{1,0:T(8,128)(2,1)S(1)} %add_convert_fusion.1), channel_id=1, source_target_pairs={{0,128},{64,192},{128,0},{192,64},{1,129},{65,193},{129,1},{193,65... | collective-permute-start | bytes 172040 | tf_op jit(solution)/shard_map/ppermute | solution.py:285
  113.5 4.6 %collective-permute-start.11 = (bf16[112,256]{1,0:T(8,128)(2,1)S(1)}, bf16[112,256]{1,0:T(8,128)(2,1)S(1)}, u32[]{:S(2)}, u32[]{:S(2)}) collective-permute-start(bf16[112,256]{1,0:T(8,128)(2,1)S(1)} %add_convert_fusion.1), channel_id=1, source_target_pairs={{0,192},{64,128},{128,64},{192,0},{1,193},{65,129},{129,65},{193,1... | collective-permute-start | bytes 172040 | tf_op jit(solution)/shard_map/ppermute | solution.py:285
  114.5 3.6 %collective-permute-start.9 = (bf16[112,256]{1,0:T(8,128)(2,1)S(1)}, bf16[112,256]{1,0:T(8,128)(2,1)S(1)}, u32[]{:S(2)}, u32[]{:S(2)}) collective-permute-start(bf16[112,256]{1,0:T(8,128)(2,1)S(1)} %add_convert_fusion.1), channel_id=1, source_target_pairs={{0,64},{64,0},{128,192},{192,128},{1,65},{65,1},{129,193},{193,129... | collective-permute-start | bytes 172040 | tf_op jit(solution)/shard_map/ppermute | solution.py:285
  118.2 5.8 %collective-permute-start.12 = (bf16[384,256]{1,0:T(8,128)(2,1)S(1)}, bf16[384,256]{1,0:T(8,128)(2,1)S(1)}, u32[]{:S(2)}, u32[]{:S(2)}) collective-permute-start(bf16[384,256]{1,0:T(8,128)(2,1)S(1)} %bitcast.24), channel_id=1, source_target_pairs={{0,4},{4,0},{1,5},{5,1},{2,6},{6,2},{3,7},{7,3},{8,12},{12,8},{9,1... | collective-permute-start | bytes 589832 | tf_op jit(solution)/shard_map/ppermute | solution.py:285

commit v4 on v3

v4 whole, which is shorter than its diff:
```python
import math

import jax
import jax.numpy as jnp
from jax import lax
from jax.experimental import pallas as pl
from jax.experimental.pallas import tpu as pltpu
from jax.sharding import Mesh
from jax.sharding import PartitionSpec as P

f32 = jnp.float32
bf = jnp.bfloat16
WIDTH = 512
HALF = 256
ROWS = 640
SAMPLES = 6400
LOSS_SCALE = 1.0 / math.sqrt(512 * 639)
PART = 96
STRIP = 192
STEP = 64
SLOTS = PART + 16
VMEM_LIMIT = 42 * 1024 * 1024
M1, TA, TB, TC = 256, 256, 256, 320
SA, SB, SC = 64, 128, 160
NN = (((1,), (0,)), ((), ()))
NT = (((1,), (1,)), ((), ()))
TN = (((0,), (0,)), ((), ()))


def gelu_parts(y):
    d = 1.0 + 0.23164189 * jnp.abs(y)
    t = pl.reciprocal(d, approx=True)
    t = t * (2.0 - d * t)
    e = jnp.exp2(y * (y * (-0.5 * 1.4426950408889634)))
    poly = t * (0.127414796 + t * (-0.142248368 + t * (0.7107068705 + t * (-0.7265760135 + t * 0.5307027145))))
    tail = poly * e
    return jnp.where(y >= 0, 1.0 - tail, tail), e


def lane_sum(v):
    return jnp.sum(v, axis=-1, keepdims=True)


def rows8(v):
    return jnp.sum(v.reshape(v.shape[0] // 8, 8, v.shape[1]), axis=0)


def dot(a, b, dims=NN):
    return lax.dot_general(a, b, dims, preferred_element_type=f32)


def shifted_up(v, below):
    return jnp.concatenate([v, below], 0)[1:v.shape[0] + 1]


def shifted_down(v, above):
    return jnp.concatenate([above, v], 0)[7:v.shape[0] + 7]


def norm_back(q, n, inv):
    qn = q * n
    inner = lane_sum(q) * (1.0 / WIDTH)
    along = lane_sum(qn) * (1.0 / WIDTH)
    return inv * (q - inner - n * along), qn


def encoder_kernel(ids_ref, source_ref, wc_ref, par_ref, own_hbm, other_hbm, cot_hbm, mine_hbm, theirs_hbm,
                   feat_ref, keep_ref, send_ref,
                   slab_ref, slab_sems, w2_ref, cot_ref, sems, p_ref, small_ref, c_ref, u_ref, s_ref, d_ref, sg_ref, r1_ref, dl_ref, t_ref):
    total = cot_hbm.shape[0]
    core = ids_ref[0]
    for i in range(2):
        holder = source_ref[i] >> 3
        local = (holder & 1) == core

        @pl.when(local)
        def _():
            pltpu.make_async_copy(own_hbm.at[holder >> 1], slab_ref.at[i], slab_sems.at[i]).start()

        @pl.when(jnp.logical_not(local))
        def _():
            pltpu.make_async_copy(other_hbm.at[holder >> 1], slab_ref.at[i], slab_sems.at[i]).start()
    loads = []
    for n, (src, half) in enumerate(((mine_hbm, core), (theirs_hbm, 1 - core))):
        for k in range(4):
            at = pl.multiple_of((ids_ref[1] ^ k) * 2 * STRIP + half * STRIP, STRIP)
            loads.append(pltpu.make_async_copy(
                src.at[k * STRIP:(k + 1) * STRIP, :], w2_ref.at[pl.ds(at, STRIP), :], sems.at[4 * n + k]))
    loads.append(pltpu.make_async_copy(cot_hbm, cot_ref, sems.at[8]))
    for load in loads:
        load.start()
    gain1, shift1, gain2, shift2 = (par_ref[k:k + 1, :] for k in range(4))
    zero = jnp.zeros((8, WIDTH), f32)
    lengths = []

    def rows(i, size):
        return pl.ds(pl.multiple_of(i * size, size), size)

    span = 10 * STEP + 128
    tap = lax.broadcasted_iota(jnp.int32, (16, span), 0)
    at = lax.broadcasted_iota(jnp.int32, (16, span), 1)
    keep_tap = at - jnp.floor((at.astype(f32) + 0.5) * 0.1).astype(jnp.int32) * 10 == tap
    lane = lax.broadcasted_iota(jnp.int32, (span, 256), 1)
    first = ((lane & (STEP - 1)) + (lane >> 7)) * 10
    source_at = lax.broadcasted_iota(jnp.int32, (span, 256), 0)
    move = jnp.where((source_at >= first) & (source_at < first + 10), 1.0, 0.0).astype(bf)
    spread = []
    for i in range(2):
        pltpu.make_async_copy(own_hbm.at[0], slab_ref.at[i], slab_sems.at[i]).wait()
        both = slab_ref[i].astype(f32)
        crop = jnp.where((source_ref[i] & 1) == 0, both[0:1], both[1:2])
        lengths.append(crop[:, SAMPLES:SAMPLES + 1] * 128.0 + crop[:, SAMPLES + 1:SAMPLES + 2])
        for g in range(10):
            part = crop[:, g * 10 * STEP:g * 10 * STEP + span]
            spread.append(jnp.where(keep_tap, part, 0.0).astype(bf))
    moved = dot(jnp.concatenate(spread, 0), move)
    left = lax.broadcasted_iota(jnp.int32, (16, 128), 1) < STEP
    for g in range(10):
        for n in range(2):
            lanes = slice(128 * n, 128 * (n + 1))
            pair = jnp.where(left, moved[32 * g:32 * g + 16, lanes], moved[32 * g + 16:32 * g + 32, lanes]).astype(bf)
            for copy in range(3):
                p_ref[32 * copy + 16 * n:32 * copy + 16 * (n + 1), 128 * g:128 * (g + 1)] = pair

    def conv1(i, _):
        r = rows(i, M1)
        c_ref[r, :] = dot(p_ref[:, r], wc_ref[...], TN)
        return 0
    lax.fori_loop(0, total // M1, conv1, 0)

    def level_one(t, below):
        for j in reversed(range(TA // SA)):
            below = level_one_rows(pl.ds(pl.multiple_of(t * TA + j * SA, SA), SA), below)
        return below

    def level_one_rows(r, below):
        for half in range(2):
            c = c_ref[r, half * WIDTH:(half + 1) * WIDTH]
            inv = lax.rsqrt(lane_sum(c * c) * (1.0 / WIDTH) + 1e-5)
            y = c * inv * gain1 + shift1
            phi, e = gelu_parts(y)
            h = y * phi
            sg_ref[half, r, :] = (phi + (y * 0.3989422804014327) * e) * gain1
            r1_ref[half, r, :] = inv
            u_ref[r, half * WIDTH:(half + 1) * WIDTH] = h.astype(bf)
            if half == 0:
                u_ref[r, 2 * WIDTH:] = shifted_up(h, below).astype(bf)
                first = h[0:8]
        return first

    def conv2(t):
        r = rows(t, TA)
        s_ref[r, :] = dot(u_ref[r, :], w2_ref[...])

    def forward(i, below):
        t = total // TA - 2 - i
        conv2(t + 1)
        return level_one(t, below)
    below = level_one(total // TA - 1, zero)
    for load in loads[:8]:
        load.wait()
    lax.fori_loop(0, total // TA - 1, forward, below)
    conv2(0)

    loads[8].wait()

    def level_two(t, carry):
        for j in range(TB // SB):
            carry = level_two_rows(pl.multiple_of(t * TB + j * SB, SB), carry)
        return carry

    def level_two_rows(b, carry):
        acc_a, acc_b, above = carry
        r = pl.ds(b, SB)
        z = s_ref[r, :]
        c = z - lane_sum(z) * (1.0 / WIDTH)
        inv = lax.rsqrt(lane_sum(c * c) * (1.0 / WIDTH) + 1e-5)
        n = c * inv
        y = n * gain2 + shift2
        phi, e = gelu_parts(y)
        feat_ref[r, :] = (y * phi).astype(bf)
        slope = phi + (y * 0.3989422804014327) * e
        row = (lax.broadcasted_iota(jnp.int32, (SB, 1), 0) + b).astype(f32)
        room = jnp.where(row < ROWS, lengths[0], lengths[1] + 10.0 * ROWS)
        weight = jnp.where(10.0 * row + 19.0 < room, LOSS_SCALE, 0.0)
        q = cot_ref[r, :].astype(f32) * weight * (slope * gain2)
        back, qn = norm_back(q, n, inv)
        dl_ref[r, 0:WIDTH] = back.astype(bf)
        dl_ref[r, WIDTH:] = shifted_down(back, above).astype(bf)
        return acc_a + rows8(qn), acc_b + rows8(q), back[SB - 8:SB]

    def down(t):
        r = rows(t, TB)
        now = dl_ref[r, 0:WIDTH]
        d_ref[r, 0:WIDTH] = dot(now, w2_ref[0:WIDTH, :], NT) + dot(dl_ref[r, WIDTH:], w2_ref[2 * WIDTH:, :], NT)
        d_ref[r, WIDTH:] = dot(now, w2_ref[WIDTH:2 * WIDTH, :], NT)

    def middle(t, carry):
        down(t - 1)
        return level_two(t, carry)
    carry = level_two(0, (zero, zero, zero))
    acc_a, acc_b, _ = lax.fori_loop(1, total // TB, middle, carry)
    down(total // TB - 1)
    small_ref[12:13, :] = jnp.sum(acc_a, axis=0, keepdims=True) / gain2
    small_ref[13:14, :] = jnp.sum(acc_b, axis=0, keepdims=True) / gain2
    small_ref[14:16, :] = jnp.zeros((2, WIDTH), f32)

    def level_one_back(r, acc_a, acc_b):
        for half in range(2):
            lanes = slice(half * WIDTH, (half + 1) * WIDTH)
            q = d_ref[r, lanes] * sg_ref[half, r, :]
            inv = r1_ref[half, r, :]
            back, qn = norm_back(q, c_ref[r, lanes] * inv, inv)
            t_ref[r, lanes] = back.astype(bf)
            acc_a = acc_a + rows8(qn)
            acc_b = acc_b + rows8(q)
        return acc_a, acc_b

    def backward(i, acc):
        acc_a, acc_b = acc
        chunk = 3 * WIDTH // (total // TC)
        for ref, half in ((keep_ref, core), (send_ref, 1 - core)):
            cols = pl.ds(pl.multiple_of(half * HALF, HALF), HALF)
            grad = dot(u_ref[:, pl.ds(pl.multiple_of(i * chunk, chunk), chunk)], dl_ref[:, cols], TN).astype(ref.dtype)
            for j in range(4):
                ref[4 * j + i, 0:PART, :] = grad[j * PART:(j + 1) * PART]
        for j in range(TC // SC):
            acc_a, acc_b = level_one_back(pl.ds(pl.multiple_of(i * TC + j * SC, SC), SC), acc_a, acc_b)
        return acc_a, acc_b
    acc_a, acc_b = lax.fori_loop(0, total // TC, backward, (zero, zero))
    small_ref[10:11, :] = jnp.sum(acc_a, axis=0, keepdims=True) / gain1
    small_ref[11:12, :] = jnp.sum(acc_b, axis=0, keepdims=True) / gain1
    taps = dot(p_ref[0:32, :], t_ref[...])
    odd = jnp.concatenate([taps[5:10, WIDTH:], taps[16:21, WIDTH:]], 0)
    small_ref[0:10, :] = taps[0:10, 0:WIDTH] + odd
    small = small_ref[...].astype(bf)
    for j in range(4):
        quarter = jnp.concatenate([small[:, 128 * j:128 * (j + 1)], jnp.zeros((16, 128), bf)], 1)
        for i in range(4):
            send_ref[4 * j + i, PART:SLOTS, :] = quarter
            keep_ref[4 * j + i, PART:SLOTS, :] = quarter.astype(f32)


def encoder(ids, source, wc, par, own, other, cot, mine, theirs):
    total = cot.shape[0]
    vm = pl.BlockSpec(memory_space=pltpu.VMEM)
    hbm = pl.BlockSpec(memory_space=pl.ANY)
    return pl.pallas_call(
        encoder_kernel,
        out_shape=(
            jax.ShapeDtypeStruct((total, WIDTH), bf),
            jax.ShapeDtypeStruct((16, SLOTS, HALF), f32),
            jax.ShapeDtypeStruct((16, SLOTS, HALF), bf),
        ),
        in_specs=[pl.BlockSpec(memory_space=pltpu.SMEM)] * 2 + [vm] * 2 + [hbm] * 5,
        out_specs=(vm,) * 3,
        scratch_shapes=[
            pltpu.VMEM((2,) + own.shape[1:], bf),
            pltpu.SemaphoreType.DMA((2,)),
            pltpu.VMEM((3 * WIDTH, WIDTH), bf),
            pltpu.VMEM((total, WIDTH), bf),
            pltpu.SemaphoreType.DMA((9,)),
            pltpu.VMEM((96, total), bf),
            pltpu.VMEM((16, WIDTH), f32),
            pltpu.VMEM((total, 2 * WIDTH), f32),
            pltpu.VMEM((total, 3 * WIDTH), bf),
            pltpu.VMEM((total, WIDTH), f32),
            pltpu.VMEM((total, 2 * WIDTH), f32),
            pltpu.VMEM((2, total, WIDTH), f32),
            pltpu.VMEM((2, total, 1), f32),
            pltpu.VMEM((total, 2 * WIDTH), bf),
            pltpu.VMEM((total, 2 * WIDTH), bf),
        ],
        compiler_params=pltpu.CompilerParams(vmem_limit_bytes=VMEM_LIMIT),
        name="encoder",
    )(ids, source, wc, par, own, other, cot, mine, theirs)


def prep_weights(conv1_weight):
    w1 = conv1_weight.astype(f32)
    wc = w1 - jnp.mean(w1, axis=1, keepdims=True)
    even = jnp.pad(wc, ((0, 22), (0, 0)))
    odd = jnp.pad(jnp.concatenate([wc[:5], jnp.zeros((6, WIDTH), f32), wc[5:]], 0), ((5, 11), (0, 0)))
    both = jnp.concatenate([even, odd], 1)
    hi = lax.reduce_precision(both, 8, 7)
    mid = lax.reduce_precision(both - hi, 8, 7)
    low = both - hi - mid
    return jnp.concatenate([hi.astype(bf), mid.astype(bf), low.astype(bf)], 0)


def pack_kernel(lengths_ref, wave_ref, out_ref):
    row = lax.broadcasted_iota(jnp.int32, (2, SAMPLES), 0)
    at = lax.broadcasted_iota(jnp.int32, (2, SAMPLES), 1)
    end = jnp.where(row == 0, lengths_ref[0], lengths_ref[1])
    cleaned = jnp.where(at < end, wave_ref[...].astype(f32), 0.0)
    lane, last = at[:, :128], end[:, :128]
    code = jnp.where(lane == 0, last >> 7, jnp.where(lane == 1, last & 127, 0)).astype(f32)
    block = jnp.concatenate([cleaned, code], 1).astype(bf)
    for k in range(out_ref.shape[0]):
        out_ref[k] = block


def pack(waveform, lengths, copies):
    return pl.pallas_call(
        pack_kernel,
        out_shape=jax.ShapeDtypeStruct((copies, 2, SAMPLES + 128), bf),
        in_specs=[pl.BlockSpec(memory_space=pltpu.SMEM), pl.BlockSpec(memory_space=pltpu.VMEM)],
        out_specs=pl.BlockSpec(memory_space=pltpu.VMEM),
        name="pack",
    )(lengths, waveform)


Y, Z, C, X = 4, 8, 2, 4
AXES = ("y", "z", "c", "x")


def flip(value, axis, size, k):
    return lax.ppermute(value, axis, [(i, i ^ k) for i in range(size)])


def turn(value, axis, size, k):
    return lax.ppermute(value, axis, [(i, (i + k) % size) for i in range(size)])


def exchange(chunks, axes):
    return lax.all_to_all(chunks, axes, 0, 0, tiled=True)


def reduce_grads(keep, send, core, shadow):
    chunks = (keep + flip(send, "c", C, 1).astype(f32)).astype(bf)
    total = jnp.sum(exchange(chunks, ("y", "x")).astype(f32), axis=0).astype(bf)
    total, shadow = lax.optimization_barrier((total, shadow))
    a, b, c = (turn(total, "z", Z, k).astype(f32) for k in (2, 4, 6))
    total = ((total.astype(f32) + b) + (a + c)).astype(bf)
    total = (total.astype(f32) + flip(total, "z", Z, 1).astype(f32)).astype(bf)
    quarters = jnp.stack([total] + [flip(total, "y", Y, k) for k in (1, 2, 3)])
    y = lax.axis_index("y")
    every = jnp.concatenate([lax.dynamic_slice_in_dim(quarters, y ^ q, 1, 0) for q in range(Y)], 0)
    half = every[:, :PART].reshape(-1, HALF)
    other = flip(half, "c", C, 1)
    grad_conv2 = jnp.where(core == 0, jnp.concatenate([half, other], 1), jnp.concatenate([other, half], 1))
    small = jnp.concatenate([every[q, PART:PART + 14, :128] for q in range(Y)], 1)
    return grad_conv2.astype(f32), small.astype(f32), shadow


def body(waveform, lengths, source, frame_mask, cotangent, conv1_weight, gain_one, shift_one,
         conv2_weight, gain_two, shift_two):
    count, frames = frame_mask.shape
    core, x = lax.axis_index("c"), lax.axis_index("x")
    column = exchange(pack(waveform, lengths, Y * Z), ("y", "z"))
    strip = lax.dynamic_slice_in_dim(conv2_weight, core * STRIP, STRIP, 0)
    pair = jnp.concatenate([strip, flip(strip, "x", X, 1)], 0)
    mine = jnp.concatenate([pair, flip(pair, "x", X, 2)], 0)
    theirs = flip(mine, "c", C, 1)
    masked = cotangent * frame_mask[:, :, None].astype(bf)
    upstream = jnp.pad(masked, ((0, 0), (0, 1), (0, 0))).reshape(count * ROWS, WIDTH)
    par = jnp.concatenate(
        [jnp.stack([gain_one, shift_one, gain_two, shift_two]), jnp.zeros((4, WIDTH), f32)], 0)
    wc = prep_weights(conv1_weight)
    ids = jnp.stack([core, x])
    column, mine, theirs, upstream, par, wc, ids = lax.optimization_barrier(
        (column, mine, theirs, upstream, par, wc, ids))
    feat, keep, send = encoder(ids, source, wc, par, column, flip(column, "c", C, 1), upstream, mine, theirs)
    features = feat.reshape(count, ROWS, WIDTH)[:, :frames]
    grad_conv2, grad_front, features = reduce_grads(keep, send, core, features)
    return features, grad_conv2, grad_front


def solution(mesh):
    grid = Mesh(mesh.devices.reshape(Y, Z, C, X), AXES)
    both = P(AXES)
    placed = (both, both, both, both, both, P(), P(), P(), P("x"), P(), P())
    return jax.shard_map(
        body,
        mesh=grid,
        in_specs=placed,
        out_specs=(both, P("x"), P()),
        check_vma=False,
    )
```

time: 126 us -> 122 us (0.968)
  other arithmetic: 9.94 us -> 7.84 us
  local copies, waits for them, and re-layouts: 9.2 us -> 7.65 us
    unnamed x27, local copies, waits for them, and re-layouts: 1.19 us -> 4.81 us
    convert_element_type x1, other arithmetic: 2.75 us -> 1.23 us  [reduce_grads(): chunks = (keep + flip(send, 'c', C, 1).astype(f32)).astype(bf)]
    ppermute x10, starting transfers between devices: 17.1 us -> 18.5 us  [flip(): return lax.ppermute(value, axis, [(i, i ^ k) for i in range(size)])]
    reshape x1 -> x0, local copies, waits for them, and re-layouts: 1.44 us -> none  [body(): blocks = routed[:, :SAMPLES].reshape(count * ROWS, 10)]
    broadcast_in_dim x3 -> x1, local copies, waits for them, and re-layouts: 1.33 us -> 0.01 us  [prep_weights(): jnp.zeros((6, WIDTH), f32)]
    mul x1, other arithmetic: 2.04 us -> 3.36 us  [body(): masked = cotangent * frame_mask[:, :, None].astype(bf)]
    pallas_call x1, Pallas kernels: 25.1 us -> 26.4 us  [encoder(): pl.pallas_call(encoder_kernel, out_shape=(jax.ShapeDtypeStruct((total, WI...]
    ppermute x10, waiting for transfers between devices: 21.4 us -> 20.1 us  [flip(): return lax.ppermute(value, axis, [(i, i ^ k) for i in range(size)])]
  transfers between devices with their start and end apart: 15 -> 15, of which waited for: 11 -> 10; matrix products, arithmetic and copies ran while one was open for 7% -> 7% of each run, Pallas kernels for 0% -> 1%
where the time goes in v4:
time: 122 us
  starting transfers between devices  41.7 us (34%)
  waiting for transfers between devices  35.7 us (29%)
  Pallas kernels  28.1 us (23%)
  other arithmetic  7.84 us (6%)
  local copies, waits for them, and re-layouts  7.65 us (6%)
    pallas_call x1, Pallas kernels, encoder(): pl.pallas_call(encoder_kernel, out_shape=(jax.ShapeDtypeStruct((total, WI...  26.4 us
    ppermute x10, waiting for transfers between devices, flip(): return lax.ppermute(value, axis, [(i, i ^ k) for i in range(size)])  20.1 us
    ppermute x10, starting transfers between devices, flip(): return lax.ppermute(value, axis, [(i, i ^ k) for i in range(size)])  18.5 us
    all_to_all x2, starting transfers between devices, exchange(): return lax.all_to_all(chunks, axes, 0, 0, tiled=True)  15.4 us
    all_to_all x2, waiting for transfers between devices, exchange(): return lax.all_to_all(chunks, axes, 0, 0, tiled=True)  12.5 us
    ppermute x3, starting transfers between devices, turn(): return lax.ppermute(value, axis, [(i, (i + k) % size) for i in range(size)])  7.78 us
    unnamed x27, local copies, waits for them, and re-layouts  4.81 us
    mul x1, other arithmetic, body(): masked = cotangent * frame_mask[:, :, None].astype(bf)  3.36 us
  transfers between devices with their start and end apart: 15, of which 10 were waited for; matrix products, arithmetic and copies ran while one was open for 7% of the time, Pallas kernels for 1%

profile of v4, /device:TPU:1, one launch (start us, length us, event | category | flops | bytes accessed | tf_op | source)
XLA Modules:
  0.0 121.9 jit_solution(7200773251663735096)
XLA Ops:
  0.7 1.0 copy-done
  1.6 2.1 %collective-permute-start = (bf16[192,512]{1,0:T(8,128)(2,1)S(1)}, bf16[192,512]{1,0:T(8,128)(2,1)S(1)}, u32[]{:S(2)}, u32[]{:S(2)}) collective-permute-start(bf16[192,512]{1,0:T(8,128)(2,1)S(1)} %constant_dynamic-slice_fusion.4), channel_id=1, source_target_pairs={{0,1},{1,0},{2,3},{3,2},{4,5},{5,4},{6,7},{7,6},{8,9},{9,8},{10,11... | collective-permute-start | bytes 589832 | tf_op jit(solution)/shard_map/ppermute | solution.py:318
  3.8 1.7 %pack.1 = bf16[32,2,6528]{2,1,0:T(2,128)(2,1)} custom-call(s32[2]{0:T(128)} %lengths_ref.1, bf16[2,6400]{1,0:T(2,128)(2,1)} %wave_ref.1), custom_call_target="tpu_custom_call" | custom-call | tf_op jit(solution)/shard_map/pack/pallas_call | solution.py:304
  5.5 11.2 %all-to-all-start = ((bf16[32,2,6528]{2,1,0:T(2,128)(2,1)}), bf16[32,2,6528]{2,1,0:T(2,128)(2,1)S(1)}, u32[]{:S(2)}, u32[]{:S(2)}) async-start(bf16[32,2,6528]{2,1,0:T(2,128)(2,1)} %pack.1), calls=%async_computation | async-start | bytes 1671168 | tf_op jit(solution)/shard_map/all_to_all | solution.py:326
  16.9 3.4 %broadcast_multiply_fusion = bf16[2,639,512]{2,0,1:T(2,128)(2,1)S(1)} fusion(bf16[2,639,512]{2,0,1:T(2,128)(2,1)} %param.15, bf16[2,639]{0,1:T(8,128)(2,1)S(1)} %copy.14), kind=kLoop, calls=%fused_computation.2 | loop fusion | flops 654336 | bytes 2619900 | tf_op jit(solution)/shard_map/mul | solution.py:355
  21.5 2.5 %collective-permute-start.1 = (bf16[384,512]{1,0:T(8,128)(2,1)S(1)}, bf16[384,512]{1,0:T(8,128)(2,1)S(1)}, u32[]{:S(2)}, u32[]{:S(2)}) collective-permute-start(bf16[384,512]{1,0:T(8,128)(2,1)S(1)} %pad_maximum_fusion.1), channel_id=1, source_target_pairs={{0,2},{1,3},{2,0},{3,1},{4,6},{5,7},{6,4},{7,5},{8,10},{9,11},{10,... | collective-permute-start | bytes 1179656 | tf_op jit(solution)/shard_map/ppermute | solution.py:318
  24.1 8.3 %collective-permute-done.1 = bf16[384,512]{1,0:T(8,128)(2,1)S(1)} collective-permute-done((bf16[384,512]{1,0:T(8,128)(2,1)S(1)}, bf16[384,512]{1,0:T(8,128)(2,1)S(1)}, u32[]{:S(2)}, u32[]{:S(2)}) %collective-permute-start.1) | collective-permute-done | bytes 393248 | tf_op jit(solution)/shard_map/ppermute | solution.py:318
  32.4 1.0 pad_maximum_fusion.mine_hbm
  33.4 2.2 %collective-permute-start.2 = (bf16[768,512]{1,0:T(8,128)(2,1)S(1)}, bf16[768,512]{1,0:T(8,128)(2,1)S(1)}, u32[]{:S(2)}, u32[]{:S(2)}) collective-permute-start(bf16[768,512]{1,0:T(8,128)(2,1)S(1)} %pad_maximum_fusion.mine_hbm), channel_id=1, source_target_pairs={{0,4},{4,0},{1,5},{5,1},{2,6},{6,2},{3,7},{7,3},{8,12},{12,8},{9,1... | collective-permute-start | bytes 2359304 | tf_op jit(solution)/shard_map/ppermute | solution.py:318
  35.9 1.7 %collective-permute-done.2.theirs_hbm = bf16[768,512]{1,0:T(8,128)(2,1)S(1)} collective-permute-done((bf16[768,512]{1,0:T(8,128)(2,1)S(1)}, bf16[768,512]{1,0:T(8,128)(2,1)S(1)}, u32[]{:S(2)}, u32[]{:S(2)}) %collective-permute-start.2) | collective-permute-done | bytes 786464 | tf_op jit(solution)/shard_map/ppermute | solution.py:318
  37.6 0.9 copy-done.3
  38.5 3.6 %collective-permute-start.3 = (bf16[32,2,6528]{2,1,0:T(2,128)(2,1)S(1)}, bf16[32,2,6528]{2,1,0:T(2,128)(2,1)S(1)}, u32[]{:S(2)}, u32[]{:S(2)}) collective-permute-start(bf16[32,2,6528]{2,1,0:T(2,128)(2,1)S(1)} %all-to-all-done.own_hbm), channel_id=1, source_target_pairs={{0,4},{4,0},{1,5},{5,1},{2,6},{6,2},{3,7},{7,3},{8,12},{12,8},{9,1... | collective-permute-start | bytes 2506760 | tf_op jit(solution)/shard_map/ppermute | solution.py:318
  42.1 2.0 %collective-permute-done.3.other_hbm = bf16[32,2,6528]{2,1,0:T(2,128)(2,1)S(1)} collective-permute-done((bf16[32,2,6528]{2,1,0:T(2,128)(2,1)S(1)}, bf16[32,2,6528]{2,1,0:T(2,128)(2,1)S(1)}, u32[]{:S(2)}, u32[]{:S(2)}) %collective-permute-start.3) | collective-permute-done | bytes 835616 | tf_op jit(solution)/shard_map/ppermute | solution.py:318
  44.0 1.1 copy-done.4
  45.2 26.4 %encoder.1 = (bf16[1280,512]{1,0:T(8,128)(2,1)S(1)}, f32[16,112,256]{2,1,0:T(8,128)S(1)}, bf16[16,112,256]{2,1,0:T(8,128)(2,1)S(1)}) custom-call(s32[2]{0:T(128)S(1)} %pad_add_fusion.ids_ref, s32[2]{0:T(128)S(1)} %copy-done.5, bf16[96,1024]{1,0:T(8,128)(2,1)S(1)} %pad_maximum_fusion.6.wc_ref, f32[8,512]{1,0:T(8,128)S(1)} %concatenate.33.par_ref, ...), custom_call_target="tpu_custom_call" | custom-call | tf_op jit(solution)/shard_map/encoder/pallas_call | solution.py:248
  71.6 1.1 copy-done.1
  73.1 2.1 %collective-permute-done.4 = bf16[16,112,256]{2,1,0:T(8,128)(2,1)S(1)} collective-permute-done((bf16[16,112,256]{2,1,0:T(8,128)(2,1)S(1)}, bf16[16,112,256]{2,1,0:T(8,128)(2,1)S(1)}, u32[]{:S(2)}, u32[]{:S(2)}) %collective-permute-start.4) | collective-permute-done | bytes 917536 | tf_op jit(solution)/shard_map/ppermute | solution.py:318
  75.2 1.2 %add_convert_fusion = bf16[16,112,256]{2,1,0:T(8,128)(2,1)} fusion(f32[16,112,256]{2,1,0:T(8,128)S(1)} %get-tuple-element.22, bf16[16,112,256]{2,1,0:T(8,128)(2,1)S(1)} %collective-permute-done.4), kind=kLoop, calls=%fused_computation | loop fusion | flops 1376256 | bytes 3670016 | tf_op jit(solution)/shard_map/convert_element_type | solution.py:330
  76.4 4.2 %all-to-all-start.1 = ((bf16[16,112,256]{2,1,0:T(8,128)(2,1)}), bf16[16,112,256]{2,1,0:T(8,128)(2,1)S(1)}, u32[]{:S(2)}, u32[]{:S(2)}) async-start(bf16[16,112,256]{2,1,0:T(8,128)(2,1)} %add_convert_fusion), calls=%async_computation.1 | async-start | bytes 1835008 | tf_op jit(solution)/shard_map/all_to_all | solution.py:326
  80.6 2.4 %copy.17 = bf16[2,639,512]{2,0,1:T(2,128)(2,1)} copy(bf16[2,639,512]{2,1,0:T(8,128)(2,1)S(1)} %bitcast.23) | data formatting | bytes 2617344 | tf_op jit(solution)/shard_map/optimization_barrier | solution.py:332
  83.0 12.5 %all-to-all-done.1 = bf16[16,112,256]{2,1,0:T(8,128)(2,1)S(1)} async-done(((bf16[16,112,256]{2,1,0:T(8,128)(2,1)}), bf16[16,112,256]{2,1,0:T(8,128)(2,1)S(1)}, u32[]{:S(2)}, u32[]{:S(2)}) %all-to-all-start.1) | async-done | bytes 917536 | tf_op jit(solution)/shard_map/all_to_all | solution.py:326
  95.6 4.2 %collective-permute-start.5 = (bf16[112,256]{1,0:T(8,128)(2,1)S(1)}, bf16[112,256]{1,0:T(8,128)(2,1)S(1)}, u32[]{:S(2)}, u32[]{:S(2)}) collective-permute-start(bf16[112,256]{1,0:T(8,128)(2,1)S(1)} %reduce_sum.22), channel_id=1, source_target_pairs={{0,32},{8,40},{16,48},{24,56},{32,0},{40,8},{48,16},{56,24},{1,33}... | collective-permute-start | bytes 172040 | tf_op jit(solution)/shard_map/ppermute | solution.py:322
  100.1 3.3 %collective-permute-start.7 = (bf16[112,256]{1,0:T(8,128)(2,1)S(1)}, bf16[112,256]{1,0:T(8,128)(2,1)S(1)}, u32[]{:S(2)}, u32[]{:S(2)}) collective-permute-start(bf16[112,256]{1,0:T(8,128)(2,1)S(1)} %reduce_sum.22), channel_id=1, source_target_pairs={{0,48},{8,56},{16,0},{24,8},{32,16},{40,24},{48,32},{56,40},{1,49}... | collective-permute-start | bytes 172040 | tf_op jit(solution)/shard_map/ppermute | solution.py:322
  103.4 3.1 %collective-permute-done.6 = bf16[112,256]{1,0:T(8,128)(2,1)S(1)} collective-permute-done((bf16[112,256]{1,0:T(8,128)(2,1)S(1)}, bf16[112,256]{1,0:T(8,128)(2,1)S(1)}, u32[]{:S(2)}, u32[]{:S(2)}) %collective-permute-start.6) | collective-permute-done | bytes 57376 | tf_op jit(solution)/shard_map/ppermute | solution.py:322
  106.6 3.0 %collective-permute-done.8 = bf16[112,256]{1,0:T(8,128)(2,1)S(1)} collective-permute-done((bf16[112,256]{1,0:T(8,128)(2,1)S(1)}, bf16[112,256]{1,0:T(8,128)(2,1)S(1)}, u32[]{:S(2)}, u32[]{:S(2)}) %collective-permute-start.8) | collective-permute-done | bytes 57376 | tf_op jit(solution)/shard_map/ppermute | solution.py:318
  109.7 0.7 collective-permute-start.10
  110.3 0.7 collective-permute-start.11
  111.0 1.4 %collective-permute-start.9 = (bf16[112,256]{1,0:T(8,128)(2,1)S(1)}, bf16[112,256]{1,0:T(8,128)(2,1)S(1)}, u32[]{:S(2)}, u32[]{:S(2)}) collective-permute-start(bf16[112,256]{1,0:T(8,128)(2,1)S(1)} %add_convert_fusion.1), channel_id=1, source_target_pairs={{0,64},{64,0},{128,192},{192,128},{1,65},{65,1},{129,193},{193,129... | collective-permute-start | bytes 172040 | tf_op jit(solution)/shard_map/ppermute | solution.py:318
  112.4 1.9 %collective-permute-done.10 = bf16[112,256]{1,0:T(8,128)(2,1)S(1)} collective-permute-done((bf16[112,256]{1,0:T(8,128)(2,1)S(1)}, bf16[112,256]{1,0:T(8,128)(2,1)S(1)}, u32[]{:S(2)}, u32[]{:S(2)}) %collective-permute-start.10) | collective-permute-done | bytes 57376 | tf_op jit(solution)/shard_map/ppermute | solution.py:318
  115.0 4.8 %collective-permute-start.12 = (bf16[384,256]{1,0:T(8,128)(2,1)S(1)}, bf16[384,256]{1,0:T(8,128)(2,1)S(1)}, u32[]{:S(2)}, u32[]{:S(2)}) collective-permute-start(bf16[384,256]{1,0:T(8,128)(2,1)S(1)} %bitcast.24), channel_id=1, source_target_pairs={{0,4},{4,0},{1,5},{5,1},{2,6},{6,2},{3,7},{7,3},{8,12},{12,8},{9,1... | collective-permute-start | bytes 589832 | tf_op jit(solution)/shard_map/ppermute | solution.py:318
  119.8 0.6 maximum_convert_fusion
  120.9 1.0 fusion
  (57 shorter events, 3.7 us)
Async XLA Ops:
  0.6 1.0 copy-start
  0.6 16.1 %copy-start.8 = (s32[2,639]{1,0:T(2,128)S(1)}, s32[2,639]{1,0:T(2,128)}, u32[]{:S(2)}) copy-start(s32[2,639]{1,0:T(2,128)} %param.14) | copy-start | bytes 15340
  1.6 19.8 %collective-permute-start = (bf16[192,512]{1,0:T(8,128)(2,1)S(1)}, bf16[192,512]{1,0:T(8,128)(2,1)S(1)}, u32[]{:S(2)}, u32[]{:S(2)}) collective-permute-start(bf16[192,512]{1,0:T(8,128)(2,1)S(1)} %constant_dynamic-slice_fusion.4), channel_id=1, source_target_pairs={{0,1},{1,0},{2,3},{3,2},{4,5},{5,4},{6,7},{7,6},{8,9},{9,8},{10,11... | collective-permute-start | bytes 589832 | tf_op jit(solution)/shard_map/ppermute | solution.py:318
  5.5 33.0 %all-to-all-start = ((bf16[32,2,6528]{2,1,0:T(2,128)(2,1)}), bf16[32,2,6528]{2,1,0:T(2,128)(2,1)S(1)}, u32[]{:S(2)}, u32[]{:S(2)}) async-start(bf16[32,2,6528]{2,1,0:T(2,128)(2,1)} %pack.1), calls=%async_computation | async-start | bytes 1671168 | tf_op jit(solution)/shard_map/all_to_all | solution.py:326
  20.5 0.7 copy-start.9
  20.5 0.7 copy-start.10
  20.5 0.7 copy-start.11
  20.6 0.7 copy-start.12
  20.6 0.7 copy-start.7
  21.4 22.6 %copy-start.5 = (s32[2]{0:T(128)S(1)}, s32[2]{0:T(128)}, u32[]{:S(2)}) copy-start(s32[2]{0:T(128)} %source_ref.1) | copy-start | bytes 28
  21.4 2.7 %copy-start.6 = (bf16[192,512]{1,0:T(8,128)(2,1)}, bf16[192,512]{1,0:T(8,128)(2,1)S(1)}, u32[]{:S(2)}) copy-start(bf16[192,512]{1,0:T(8,128)(2,1)S(1)} %collective-permute-done) | copy-start | bytes 589828
  21.5 11.0 %collective-permute-start.1 = (bf16[384,512]{1,0:T(8,128)(2,1)S(1)}, bf16[384,512]{1,0:T(8,128)(2,1)S(1)}, u32[]{:S(2)}, u32[]{:S(2)}) collective-permute-start(bf16[384,512]{1,0:T(8,128)(2,1)S(1)} %pad_maximum_fusion.1), channel_id=1, source_target_pairs={{0,2},{1,3},{2,0},{3,1},{4,6},{5,7},{6,4},{7,5},{8,10},{9,11},{10,... | collective-permute-start | bytes 1179656 | tf_op jit(solution)/shard_map/ppermute | solution.py:318
  33.4 4.2 %collective-permute-start.2 = (bf16[768,512]{1,0:T(8,128)(2,1)S(1)}, bf16[768,512]{1,0:T(8,128)(2,1)S(1)}, u32[]{:S(2)}, u32[]{:S(2)}) collective-permute-start(bf16[768,512]{1,0:T(8,128)(2,1)S(1)} %pad_maximum_fusion.mine_hbm), channel_id=1, source_target_pairs={{0,4},{4,0},{1,5},{5,1},{2,6},{6,2},{3,7},{7,3},{8,12},{12,8},{9,1... | collective-permute-start | bytes 2359304 | tf_op jit(solution)/shard_map/ppermute | solution.py:318
  37.6 0.9 copy-start.3
  38.5 5.6 %collective-permute-start.3 = (bf16[32,2,6528]{2,1,0:T(2,128)(2,1)S(1)}, bf16[32,2,6528]{2,1,0:T(2,128)(2,1)S(1)}, u32[]{:S(2)}, u32[]{:S(2)}) collective-permute-start(bf16[32,2,6528]{2,1,0:T(2,128)(2,1)S(1)} %all-to-all-done.own_hbm), channel_id=1, source_target_pairs={{0,4},{4,0},{1,5},{5,1},{2,6},{6,2},{3,7},{7,3},{8,12},{12,8},{9,1... | collective-permute-start | bytes 2506760 | tf_op jit(solution)/shard_map/ppermute | solution.py:318
  44.0 1.1 copy-start.4
  71.6 1.1 copy-start.1
  72.6 2.5 %collective-permute-start.4 = (bf16[16,112,256]{2,1,0:T(8,128)(2,1)S(1)}, bf16[16,112,256]{2,1,0:T(8,128)(2,1)S(1)}, u32[]{:S(2)}, u32[]{:S(2)}) collective-permute-start(bf16[16,112,256]{2,1,0:T(8,128)(2,1)S(1)} %get-tuple-element.23), channel_id=1, source_target_pairs={{0,4},{4,0},{1,5},{5,1},{2,6},{6,2},{3,7},{7,3},{8,12},{12,8},{9,1... | collective-permute-start | bytes 2752520 | tf_op jit(solution)/shard_map/ppermute | solution.py:318
  76.4 4.2 %copy-start.2 = (bf16[1280,512]{1,0:T(8,128)(2,1)S(1)}, bf16[1280,512]{1,0:T(8,128)(2,1)}, u32[]{:S(2)}) copy-start(bf16[1280,512]{1,0:T(8,128)(2,1)} %copy-done.1) | copy-start | bytes 3932164
  76.4 19.1 %all-to-all-start.1 = ((bf16[16,112,256]{2,1,0:T(8,128)(2,1)}), bf16[16,112,256]{2,1,0:T(8,128)(2,1)S(1)}, u32[]{:S(2)}, u32[]{:S(2)}) async-start(bf16[16,112,256]{2,1,0:T(8,128)(2,1)} %add_convert_fusion), calls=%async_computation.1 | async-start | bytes 1835008 | tf_op jit(solution)/shard_map/all_to_all | solution.py:326
  95.6 7.8 %collective-permute-start.5 = (bf16[112,256]{1,0:T(8,128)(2,1)S(1)}, bf16[112,256]{1,0:T(8,128)(2,1)S(1)}, u32[]{:S(2)}, u32[]{:S(2)}) collective-permute-start(bf16[112,256]{1,0:T(8,128)(2,1)S(1)} %reduce_sum.22), channel_id=1, source_target_pairs={{0,32},{8,40},{16,48},{24,56},{32,0},{40,8},{48,16},{56,24},{1,33}... | collective-permute-start | bytes 172040 | tf_op jit(solution)/shard_map/ppermute | solution.py:322
  99.8 6.7 %collective-permute-start.6 = (bf16[112,256]{1,0:T(8,128)(2,1)S(1)}, bf16[112,256]{1,0:T(8,128)(2,1)S(1)}, u32[]{:S(2)}, u32[]{:S(2)}) collective-permute-start(bf16[112,256]{1,0:T(8,128)(2,1)S(1)} %reduce_sum.22), channel_id=1, source_target_pairs={{0,16},{8,24},{16,32},{24,40},{32,48},{40,56},{48,0},{56,8},{1,17}... | collective-permute-start | bytes 172040 | tf_op jit(solution)/shard_map/ppermute | solution.py:322
  100.1 6.4 %collective-permute-start.7 = (bf16[112,256]{1,0:T(8,128)(2,1)S(1)}, bf16[112,256]{1,0:T(8,128)(2,1)S(1)}, u32[]{:S(2)}, u32[]{:S(2)}) collective-permute-start(bf16[112,256]{1,0:T(8,128)(2,1)S(1)} %reduce_sum.22), channel_id=1, source_target_pairs={{0,48},{8,56},{16,0},{24,8},{32,16},{40,24},{48,32},{56,40},{1,49}... | collective-permute-start | bytes 172040 | tf_op jit(solution)/shard_map/ppermute | solution.py:322
  106.5 3.1 %collective-permute-start.8 = (bf16[112,256]{1,0:T(8,128)(2,1)S(1)}, bf16[112,256]{1,0:T(8,128)(2,1)S(1)}, u32[]{:S(2)}, u32[]{:S(2)}) collective-permute-start(bf16[112,256]{1,0:T(8,128)(2,1)S(1)} %add_convert_fusion.2), channel_id=1, source_target_pairs={{0,8},{8,0},{16,24},{24,16},{32,40},{40,32},{48,56},{56,48},{1,9},... | collective-permute-start | bytes 172040 | tf_op jit(solution)/shard_map/ppermute | solution.py:318
  109.7 4.7 %collective-permute-start.10 = (bf16[112,256]{1,0:T(8,128)(2,1)S(1)}, bf16[112,256]{1,0:T(8,128)(2,1)S(1)}, u32[]{:S(2)}, u32[]{:S(2)}) collective-permute-start(bf16[112,256]{1,0:T(8,128)(2,1)S(1)} %add_convert_fusion.1), channel_id=1, source_target_pairs={{0,128},{64,192},{128,0},{192,64},{1,129},{65,193},{129,1},{193,65... | collective-permute-start | bytes 172040 | tf_op jit(solution)/shard_map/ppermute | solution.py:318
  110.3 4.6 %collective-permute-start.11 = (bf16[112,256]{1,0:T(8,128)(2,1)S(1)}, bf16[112,256]{1,0:T(8,128)(2,1)S(1)}, u32[]{:S(2)}, u32[]{:S(2)}) collective-permute-start(bf16[112,256]{1,0:T(8,128)(2,1)S(1)} %add_convert_fusion.1), channel_id=1, source_target_pairs={{0,192},{64,128},{128,64},{192,0},{1,193},{65,129},{129,65},{193,1... | collective-permute-start | bytes 172040 | tf_op jit(solution)/shard_map/ppermute | solution.py:318
  111.0 3.9 %collective-permute-start.9 = (bf16[112,256]{1,0:T(8,128)(2,1)S(1)}, bf16[112,256]{1,0:T(8,128)(2,1)S(1)}, u32[]{:S(2)}, u32[]{:S(2)}) collective-permute-start(bf16[112,256]{1,0:T(8,128)(2,1)S(1)} %add_convert_fusion.1), channel_id=1, source_target_pairs={{0,64},{64,0},{128,192},{192,128},{1,65},{65,1},{129,193},{193,129... | collective-permute-start | bytes 172040 | tf_op jit(solution)/shard_map/ppermute | solution.py:318
  115.0 5.9 %collective-permute-start.12 = (bf16[384,256]{1,0:T(8,128)(2,1)S(1)}, bf16[384,256]{1,0:T(8,128)(2,1)S(1)}, u32[]{:S(2)}, u32[]{:S(2)}) collective-permute-start(bf16[384,256]{1,0:T(8,128)(2,1)S(1)} %bitcast.24), channel_id=1, source_target_pairs={{0,4},{4,0},{1,5},{5,1},{2,6},{6,2},{3,7},{7,3},{8,12},{12,8},{9,1... | collective-permute-start | bytes 589832 | tf_op jit(solution)/shard_map/ppermute | solution.py:318

commit v5 on v4

--- a/solution.py
+++ b/solution.py
@@ -17,11 +17,12 @@
 LOSS_SCALE = 1.0 / math.sqrt(512 * 639)
 PART = 96
 STRIP = 192
+BLOCK = 384
 STEP = 64
 SLOTS = PART + 16
 VMEM_LIMIT = 42 * 1024 * 1024
-M1, TA, TB, TC = 256, 256, 256, 320
-SA, SB, SC = 64, 128, 160
+M1, TA, TB, TC = 256, 640, 640, 640
+SA, SB, SC = 64, 320, 320
 NN = (((1,), (0,)), ((), ()))
 NT = (((1,), (1,)), ((), ()))
 TN = (((0,), (0,)), ((), ()))
@@ -222,8 +223,11 @@
         for ref, half in ((keep_ref, core), (send_ref, 1 - core)):
             cols = pl.ds(pl.multiple_of(half * HALF, HALF), HALF)
             grad = dot(u_ref[:, pl.ds(pl.multiple_of(i * chunk, chunk), chunk)], dl_ref[:, cols], TN).astype(ref.dtype)
-            for j in range(4):
-                ref[4 * j + i, 0:PART, :] = grad[j * PART:(j + 1) * PART]
+            blocks = chunk // BLOCK
+            for b in range(blocks):
+                for j in range(4):
+                    start = b * BLOCK + j * PART
+                    ref[4 * j + blocks * i + b, 0:PART, :] = grad[start:start + PART]
         for j in range(TC // SC):
             acc_a, acc_b = level_one_back(pl.ds(pl.multiple_of(i * TC + j * SC, SC), SC), acc_a, acc_b)
         return acc_a, acc_b

time: 122 us -> 121 us (level)
  Pallas kernels: 28.1 us -> 26.6 us
    pallas_call x1, Pallas kernels: 26.4 us -> 24.9 us  [encoder(): pl.pallas_call(encoder_kernel, out_shape=(jax.ShapeDtypeStruct((total, WI...]
where the time goes in v5:
time: 121 us; the launch traced here: 120 us
  starting transfers between devices  41.7 us (34%)
  waiting for transfers between devices  35.7 us (30%)
  Pallas kernels  26.6 us (22%)
  other arithmetic  7.84 us (6%)
  local copies, waits for them, and re-layouts  7.65 us (6%)
    pallas_call x1, Pallas kernels, encoder(): pl.pallas_call(encoder_kernel, out_shape=(jax.ShapeDtypeStruct((total, WI...  24.9 us
    ppermute x10, waiting for transfers between devices, flip(): return lax.ppermute(value, axis, [(i, i ^ k) for i in range(size)])  20.1 us
    ppermute x10, starting transfers between devices, flip(): return lax.ppermute(value, axis, [(i, i ^ k) for i in range(size)])  18.6 us
    all_to_all x2, starting transfers between devices, exchange(): return lax.all_to_all(chunks, axes, 0, 0, tiled=True)  15.4 us
    all_to_all x2, waiting for transfers between devices, exchange(): return lax.all_to_all(chunks, axes, 0, 0, tiled=True)  12.5 us
    ppermute x3, starting transfers between devices, turn(): return lax.ppermute(value, axis, [(i, (i + k) % size) for i in range(size)])  7.76 us
    unnamed x27, local copies, waits for them, and re-layouts  4.81 us
    mul x1, other arithmetic, body(): masked = cotangent * frame_mask[:, :, None].astype(bf)  3.36 us
  transfers between devices with their start and end apart: 15, of which 10 were waited for; matrix products, arithmetic and copies ran while one was open for 7% of the time, Pallas kernels for 1%

profile of v5, /device:TPU:1, one launch (start us, length us, event | category | flops | bytes accessed | tf_op | source)
XLA Modules:
  0.0 120.4 jit_solution(18233919300152183663)
XLA Ops:
  0.7 1.0 copy-done
  1.6 2.1 %collective-permute-start = (bf16[192,512]{1,0:T(8,128)(2,1)S(1)}, bf16[192,512]{1,0:T(8,128)(2,1)S(1)}, u32[]{:S(2)}, u32[]{:S(2)}) collective-permute-start(bf16[192,512]{1,0:T(8,128)(2,1)S(1)} %constant_dynamic-slice_fusion.4), channel_id=1, source_target_pairs={{0,1},{1,0},{2,3},{3,2},{4,5},{5,4},{6,7},{7,6},{8,9},{9,8},{10,11... | collective-permute-start | bytes 589832 | tf_op jit(solution)/shard_map/ppermute | solution.py:322
  3.8 1.7 %pack.1 = bf16[32,2,6528]{2,1,0:T(2,128)(2,1)} custom-call(s32[2]{0:T(128)} %lengths_ref.1, bf16[2,6400]{1,0:T(2,128)(2,1)} %wave_ref.1), custom_call_target="tpu_custom_call" | custom-call | tf_op jit(solution)/shard_map/pack/pallas_call | solution.py:308
  5.5 11.2 %all-to-all-start = ((bf16[32,2,6528]{2,1,0:T(2,128)(2,1)}), bf16[32,2,6528]{2,1,0:T(2,128)(2,1)S(1)}, u32[]{:S(2)}, u32[]{:S(2)}) async-start(bf16[32,2,6528]{2,1,0:T(2,128)(2,1)} %pack.1), calls=%async_computation | async-start | bytes 1671168 | tf_op jit(solution)/shard_map/all_to_all | solution.py:330
  16.9 3.4 %broadcast_multiply_fusion = bf16[2,639,512]{2,0,1:T(2,128)(2,1)S(1)} fusion(bf16[2,639,512]{2,0,1:T(2,128)(2,1)} %param.15, bf16[2,639]{0,1:T(8,128)(2,1)S(1)} %copy.14), kind=kLoop, calls=%fused_computation.2 | loop fusion | flops 654336 | bytes 2619900 | tf_op jit(solution)/shard_map/mul | solution.py:359
  21.5 2.5 %collective-permute-start.1 = (bf16[384,512]{1,0:T(8,128)(2,1)S(1)}, bf16[384,512]{1,0:T(8,128)(2,1)S(1)}, u32[]{:S(2)}, u32[]{:S(2)}) collective-permute-start(bf16[384,512]{1,0:T(8,128)(2,1)S(1)} %pad_maximum_fusion.1), channel_id=1, source_target_pairs={{0,2},{1,3},{2,0},{3,1},{4,6},{5,7},{6,4},{7,5},{8,10},{9,11},{10,... | collective-permute-start | bytes 1179656 | tf_op jit(solution)/shard_map/ppermute | solution.py:322
  24.1 8.3 %collective-permute-done.1 = bf16[384,512]{1,0:T(8,128)(2,1)S(1)} collective-permute-done((bf16[384,512]{1,0:T(8,128)(2,1)S(1)}, bf16[384,512]{1,0:T(8,128)(2,1)S(1)}, u32[]{:S(2)}, u32[]{:S(2)}) %collective-permute-start.1) | collective-permute-done | bytes 393248 | tf_op jit(solution)/shard_map/ppermute | solution.py:322
  32.4 1.0 pad_maximum_fusion.mine_hbm
  33.4 2.2 %collective-permute-start.2 = (bf16[768,512]{1,0:T(8,128)(2,1)S(1)}, bf16[768,512]{1,0:T(8,128)(2,1)S(1)}, u32[]{:S(2)}, u32[]{:S(2)}) collective-permute-start(bf16[768,512]{1,0:T(8,128)(2,1)S(1)} %pad_maximum_fusion.mine_hbm), channel_id=1, source_target_pairs={{0,4},{4,0},{1,5},{5,1},{2,6},{6,2},{3,7},{7,3},{8,12},{12,8},{9,1... | collective-permute-start | bytes 2359304 | tf_op jit(solution)/shard_map/ppermute | solution.py:322
  35.9 1.7 %collective-permute-done.2.theirs_hbm = bf16[768,512]{1,0:T(8,128)(2,1)S(1)} collective-permute-done((bf16[768,512]{1,0:T(8,128)(2,1)S(1)}, bf16[768,512]{1,0:T(8,128)(2,1)S(1)}, u32[]{:S(2)}, u32[]{:S(2)}) %collective-permute-start.2) | collective-permute-done | bytes 786464 | tf_op jit(solution)/shard_map/ppermute | solution.py:322
  37.6 0.9 copy-done.3
  38.5 3.6 %collective-permute-start.3 = (bf16[32,2,6528]{2,1,0:T(2,128)(2,1)S(1)}, bf16[32,2,6528]{2,1,0:T(2,128)(2,1)S(1)}, u32[]{:S(2)}, u32[]{:S(2)}) collective-permute-start(bf16[32,2,6528]{2,1,0:T(2,128)(2,1)S(1)} %all-to-all-done.own_hbm), channel_id=1, source_target_pairs={{0,4},{4,0},{1,5},{5,1},{2,6},{6,2},{3,7},{7,3},{8,12},{12,8},{9,1... | collective-permute-start | bytes 2506760 | tf_op jit(solution)/shard_map/ppermute | solution.py:322
  42.1 2.0 %collective-permute-done.3.other_hbm = bf16[32,2,6528]{2,1,0:T(2,128)(2,1)S(1)} collective-permute-done((bf16[32,2,6528]{2,1,0:T(2,128)(2,1)S(1)}, bf16[32,2,6528]{2,1,0:T(2,128)(2,1)S(1)}, u32[]{:S(2)}, u32[]{:S(2)}) %collective-permute-start.3) | collective-permute-done | bytes 835616 | tf_op jit(solution)/shard_map/ppermute | solution.py:322
  44.0 1.1 copy-done.4
  45.2 24.9 %encoder.1 = (bf16[1280,512]{1,0:T(8,128)(2,1)S(1)}, f32[16,112,256]{2,1,0:T(8,128)S(1)}, bf16[16,112,256]{2,1,0:T(8,128)(2,1)S(1)}) custom-call(s32[2]{0:T(128)S(1)} %pad_add_fusion.ids_ref, s32[2]{0:T(128)S(1)} %copy-done.5, bf16[96,1024]{1,0:T(8,128)(2,1)S(1)} %pad_maximum_fusion.6.wc_ref, f32[8,512]{1,0:T(8,128)S(1)} %concatenate.33.par_ref, ...), custom_call_target="tpu_custom_call" | custom-call | tf_op jit(solution)/shard_map/encoder/pallas_call | solution.py:252
  70.1 1.1 copy-done.1
  71.6 2.1 %collective-permute-done.4 = bf16[16,112,256]{2,1,0:T(8,128)(2,1)S(1)} collective-permute-done((bf16[16,112,256]{2,1,0:T(8,128)(2,1)S(1)}, bf16[16,112,256]{2,1,0:T(8,128)(2,1)S(1)}, u32[]{:S(2)}, u32[]{:S(2)}) %collective-permute-start.4) | collective-permute-done | bytes 917536 | tf_op jit(solution)/shard_map/ppermute | solution.py:322
  73.7 1.2 %add_convert_fusion = bf16[16,112,256]{2,1,0:T(8,128)(2,1)} fusion(f32[16,112,256]{2,1,0:T(8,128)S(1)} %get-tuple-element.22, bf16[16,112,256]{2,1,0:T(8,128)(2,1)S(1)} %collective-permute-done.4), kind=kLoop, calls=%fused_computation | loop fusion | flops 1376256 | bytes 3670016 | tf_op jit(solution)/shard_map/convert_element_type | solution.py:334
  74.9 4.2 %all-to-all-start.1 = ((bf16[16,112,256]{2,1,0:T(8,128)(2,1)}), bf16[16,112,256]{2,1,0:T(8,128)(2,1)S(1)}, u32[]{:S(2)}, u32[]{:S(2)}) async-start(bf16[16,112,256]{2,1,0:T(8,128)(2,1)} %add_convert_fusion), calls=%async_computation.1 | async-start | bytes 1835008 | tf_op jit(solution)/shard_map/all_to_all | solution.py:330
  79.1 2.4 %copy.17 = bf16[2,639,512]{2,0,1:T(2,128)(2,1)} copy(bf16[2,639,512]{2,1,0:T(8,128)(2,1)S(1)} %bitcast.23) | data formatting | bytes 2617344 | tf_op jit(solution)/shard_map/optimization_barrier | solution.py:336
  81.5 12.5 %all-to-all-done.1 = bf16[16,112,256]{2,1,0:T(8,128)(2,1)S(1)} async-done(((bf16[16,112,256]{2,1,0:T(8,128)(2,1)}), bf16[16,112,256]{2,1,0:T(8,128)(2,1)S(1)}, u32[]{:S(2)}, u32[]{:S(2)}) %all-to-all-start.1) | async-done | bytes 917536 | tf_op jit(solution)/shard_map/all_to_all | solution.py:330
  94.2 4.2 %collective-permute-start.5 = (bf16[112,256]{1,0:T(8,128)(2,1)S(1)}, bf16[112,256]{1,0:T(8,128)(2,1)S(1)}, u32[]{:S(2)}, u32[]{:S(2)}) collective-permute-start(bf16[112,256]{1,0:T(8,128)(2,1)S(1)} %reduce_sum.22), channel_id=1, source_target_pairs={{0,32},{8,40},{16,48},{24,56},{32,0},{40,8},{48,16},{56,24},{1,33}... | collective-permute-start | bytes 172040 | tf_op jit(solution)/shard_map/ppermute | solution.py:326
  98.7 3.3 %collective-permute-start.7 = (bf16[112,256]{1,0:T(8,128)(2,1)S(1)}, bf16[112,256]{1,0:T(8,128)(2,1)S(1)}, u32[]{:S(2)}, u32[]{:S(2)}) collective-permute-start(bf16[112,256]{1,0:T(8,128)(2,1)S(1)} %reduce_sum.22), channel_id=1, source_target_pairs={{0,48},{8,56},{16,0},{24,8},{32,16},{40,24},{48,32},{56,40},{1,49}... | collective-permute-start | bytes 172040 | tf_op jit(solution)/shard_map/ppermute | solution.py:326
  101.9 3.1 %collective-permute-done.6 = bf16[112,256]{1,0:T(8,128)(2,1)S(1)} collective-permute-done((bf16[112,256]{1,0:T(8,128)(2,1)S(1)}, bf16[112,256]{1,0:T(8,128)(2,1)S(1)}, u32[]{:S(2)}, u32[]{:S(2)}) %collective-permute-start.6) | collective-permute-done | bytes 57376 | tf_op jit(solution)/shard_map/ppermute | solution.py:326
  105.1 3.0 %collective-permute-done.8 = bf16[112,256]{1,0:T(8,128)(2,1)S(1)} collective-permute-done((bf16[112,256]{1,0:T(8,128)(2,1)S(1)}, bf16[112,256]{1,0:T(8,128)(2,1)S(1)}, u32[]{:S(2)}, u32[]{:S(2)}) %collective-permute-start.8) | collective-permute-done | bytes 57376 | tf_op jit(solution)/shard_map/ppermute | solution.py:322
  108.2 0.7 collective-permute-start.10
  108.8 0.7 collective-permute-start.11
  109.5 1.4 %collective-permute-start.9 = (bf16[112,256]{1,0:T(8,128)(2,1)S(1)}, bf16[112,256]{1,0:T(8,128)(2,1)S(1)}, u32[]{:S(2)}, u32[]{:S(2)}) collective-permute-start(bf16[112,256]{1,0:T(8,128)(2,1)S(1)} %add_convert_fusion.1), channel_id=1, source_target_pairs={{0,64},{64,0},{128,192},{192,128},{1,65},{65,1},{129,193},{193,129... | collective-permute-start | bytes 172040 | tf_op jit(solution)/shard_map/ppermute | solution.py:322
  110.9 1.9 %collective-permute-done.10 = bf16[112,256]{1,0:T(8,128)(2,1)S(1)} collective-permute-done((bf16[112,256]{1,0:T(8,128)(2,1)S(1)}, bf16[112,256]{1,0:T(8,128)(2,1)S(1)}, u32[]{:S(2)}, u32[]{:S(2)}) %collective-permute-start.10) | collective-permute-done | bytes 57376 | tf_op jit(solution)/shard_map/ppermute | solution.py:322
  113.5 4.8 %collective-permute-start.12 = (bf16[384,256]{1,0:T(8,128)(2,1)S(1)}, bf16[384,256]{1,0:T(8,128)(2,1)S(1)}, u32[]{:S(2)}, u32[]{:S(2)}) collective-permute-start(bf16[384,256]{1,0:T(8,128)(2,1)S(1)} %bitcast.24), channel_id=1, source_target_pairs={{0,4},{4,0},{1,5},{5,1},{2,6},{6,2},{3,7},{7,3},{8,12},{12,8},{9,1... | collective-permute-start | bytes 589832 | tf_op jit(solution)/shard_map/ppermute | solution.py:322
  118.3 0.6 maximum_convert_fusion
  119.4 1.0 fusion
  (57 shorter events, 3.7 us)
Async XLA Ops:
  0.6 1.0 copy-start
  0.6 16.1 %copy-start.8 = (s32[2,639]{1,0:T(2,128)S(1)}, s32[2,639]{1,0:T(2,128)}, u32[]{:S(2)}) copy-start(s32[2,639]{1,0:T(2,128)} %param.14) | copy-start | bytes 15340
  1.6 19.8 %collective-permute-start = (bf16[192,512]{1,0:T(8,128)(2,1)S(1)}, bf16[192,512]{1,0:T(8,128)(2,1)S(1)}, u32[]{:S(2)}, u32[]{:S(2)}) collective-permute-start(bf16[192,512]{1,0:T(8,128)(2,1)S(1)} %constant_dynamic-slice_fusion.4), channel_id=1, source_target_pairs={{0,1},{1,0},{2,3},{3,2},{4,5},{5,4},{6,7},{7,6},{8,9},{9,8},{10,11... | collective-permute-start | bytes 589832 | tf_op jit(solution)/shard_map/ppermute | solution.py:322
  5.5 33.0 %all-to-all-start = ((bf16[32,2,6528]{2,1,0:T(2,128)(2,1)}), bf16[32,2,6528]{2,1,0:T(2,128)(2,1)S(1)}, u32[]{:S(2)}, u32[]{:S(2)}) async-start(bf16[32,2,6528]{2,1,0:T(2,128)(2,1)} %pack.1), calls=%async_computation | async-start | bytes 1671168 | tf_op jit(solution)/shard_map/all_to_all | solution.py:330
  20.5 0.7 copy-start.9
  20.5 0.7 copy-start.10
  20.5 0.7 copy-start.11
  20.6 0.7 copy-start.12
  20.6 0.7 copy-start.7
  21.4 22.6 %copy-start.5 = (s32[2]{0:T(128)S(1)}, s32[2]{0:T(128)}, u32[]{:S(2)}) copy-start(s32[2]{0:T(128)} %source_ref.1) | copy-start | bytes 28
  21.4 2.7 %copy-start.6 = (bf16[192,512]{1,0:T(8,128)(2,1)}, bf16[192,512]{1,0:T(8,128)(2,1)S(1)}, u32[]{:S(2)}) copy-start(bf16[192,512]{1,0:T(8,128)(2,1)S(1)} %collective-permute-done) | copy-start | bytes 589828
  21.5 11.0 %collective-permute-start.1 = (bf16[384,512]{1,0:T(8,128)(2,1)S(1)}, bf16[384,512]{1,0:T(8,128)(2,1)S(1)}, u32[]{:S(2)}, u32[]{:S(2)}) collective-permute-start(bf16[384,512]{1,0:T(8,128)(2,1)S(1)} %pad_maximum_fusion.1), channel_id=1, source_target_pairs={{0,2},{1,3},{2,0},{3,1},{4,6},{5,7},{6,4},{7,5},{8,10},{9,11},{10,... | collective-permute-start | bytes 1179656 | tf_op jit(solution)/shard_map/ppermute | solution.py:322
  33.4 4.2 %collective-permute-start.2 = (bf16[768,512]{1,0:T(8,128)(2,1)S(1)}, bf16[768,512]{1,0:T(8,128)(2,1)S(1)}, u32[]{:S(2)}, u32[]{:S(2)}) collective-permute-start(bf16[768,512]{1,0:T(8,128)(2,1)S(1)} %pad_maximum_fusion.mine_hbm), channel_id=1, source_target_pairs={{0,4},{4,0},{1,5},{5,1},{2,6},{6,2},{3,7},{7,3},{8,12},{12,8},{9,1... | collective-permute-start | bytes 2359304 | tf_op jit(solution)/shard_map/ppermute | solution.py:322
  37.6 0.9 copy-start.3
  38.5 5.6 %collective-permute-start.3 = (bf16[32,2,6528]{2,1,0:T(2,128)(2,1)S(1)}, bf16[32,2,6528]{2,1,0:T(2,128)(2,1)S(1)}, u32[]{:S(2)}, u32[]{:S(2)}) collective-permute-start(bf16[32,2,6528]{2,1,0:T(2,128)(2,1)S(1)} %all-to-all-done.own_hbm), channel_id=1, source_target_pairs={{0,4},{4,0},{1,5},{5,1},{2,6},{6,2},{3,7},{7,3},{8,12},{12,8},{9,1... | collective-permute-start | bytes 2506760 | tf_op jit(solution)/shard_map/ppermute | solution.py:322
  44.0 1.1 copy-start.4
  70.1 1.1 copy-start.1
  71.2 2.5 %collective-permute-start.4 = (bf16[16,112,256]{2,1,0:T(8,128)(2,1)S(1)}, bf16[16,112,256]{2,1,0:T(8,128)(2,1)S(1)}, u32[]{:S(2)}, u32[]{:S(2)}) collective-permute-start(bf16[16,112,256]{2,1,0:T(8,128)(2,1)S(1)} %get-tuple-element.23), channel_id=1, source_target_pairs={{0,4},{4,0},{1,5},{5,1},{2,6},{6,2},{3,7},{7,3},{8,12},{12,8},{9,1... | collective-permute-start | bytes 2752520 | tf_op jit(solution)/shard_map/ppermute | solution.py:322
  74.9 4.2 %copy-start.2 = (bf16[1280,512]{1,0:T(8,128)(2,1)S(1)}, bf16[1280,512]{1,0:T(8,128)(2,1)}, u32[]{:S(2)}) copy-start(bf16[1280,512]{1,0:T(8,128)(2,1)} %copy-done.1) | copy-start | bytes 3932164
  74.9 19.1 %all-to-all-start.1 = ((bf16[16,112,256]{2,1,0:T(8,128)(2,1)}), bf16[16,112,256]{2,1,0:T(8,128)(2,1)S(1)}, u32[]{:S(2)}, u32[]{:S(2)}) async-start(bf16[16,112,256]{2,1,0:T(8,128)(2,1)} %add_convert_fusion), calls=%async_computation.1 | async-start | bytes 1835008 | tf_op jit(solution)/shard_map/all_to_all | solution.py:330
  94.2 7.8 %collective-permute-start.5 = (bf16[112,256]{1,0:T(8,128)(2,1)S(1)}, bf16[112,256]{1,0:T(8,128)(2,1)S(1)}, u32[]{:S(2)}, u32[]{:S(2)}) collective-permute-start(bf16[112,256]{1,0:T(8,128)(2,1)S(1)} %reduce_sum.22), channel_id=1, source_target_pairs={{0,32},{8,40},{16,48},{24,56},{32,0},{40,8},{48,16},{56,24},{1,33}... | collective-permute-start | bytes 172040 | tf_op jit(solution)/shard_map/ppermute | solution.py:326
  98.4 6.6 %collective-permute-start.6 = (bf16[112,256]{1,0:T(8,128)(2,1)S(1)}, bf16[112,256]{1,0:T(8,128)(2,1)S(1)}, u32[]{:S(2)}, u32[]{:S(2)}) collective-permute-start(bf16[112,256]{1,0:T(8,128)(2,1)S(1)} %reduce_sum.22), channel_id=1, source_target_pairs={{0,16},{8,24},{16,32},{24,40},{32,48},{40,56},{48,0},{56,8},{1,17}... | collective-permute-start | bytes 172040 | tf_op jit(solution)/shard_map/ppermute | solution.py:326
  98.7 6.3 %collective-permute-start.7 = (bf16[112,256]{1,0:T(8,128)(2,1)S(1)}, bf16[112,256]{1,0:T(8,128)(2,1)S(1)}, u32[]{:S(2)}, u32[]{:S(2)}) collective-permute-start(bf16[112,256]{1,0:T(8,128)(2,1)S(1)} %reduce_sum.22), channel_id=1, source_target_pairs={{0,48},{8,56},{16,0},{24,8},{32,16},{40,24},{48,32},{56,40},{1,49}... | collective-permute-start | bytes 172040 | tf_op jit(solution)/shard_map/ppermute | solution.py:326
  105.0 3.1 %collective-permute-start.8 = (bf16[112,256]{1,0:T(8,128)(2,1)S(1)}, bf16[112,256]{1,0:T(8,128)(2,1)S(1)}, u32[]{:S(2)}, u32[]{:S(2)}) collective-permute-start(bf16[112,256]{1,0:T(8,128)(2,1)S(1)} %add_convert_fusion.2), channel_id=1, source_target_pairs={{0,8},{8,0},{16,24},{24,16},{32,40},{40,32},{48,56},{56,48},{1,9},... | collective-permute-start | bytes 172040 | tf_op jit(solution)/shard_map/ppermute | solution.py:322
  108.2 4.7 %collective-permute-start.10 = (bf16[112,256]{1,0:T(8,128)(2,1)S(1)}, bf16[112,256]{1,0:T(8,128)(2,1)S(1)}, u32[]{:S(2)}, u32[]{:S(2)}) collective-permute-start(bf16[112,256]{1,0:T(8,128)(2,1)S(1)} %add_convert_fusion.1), channel_id=1, source_target_pairs={{0,128},{64,192},{128,0},{192,64},{1,129},{65,193},{129,1},{193,65... | collective-permute-start | bytes 172040 | tf_op jit(solution)/shard_map/ppermute | solution.py:322
  108.8 4.6 %collective-permute-start.11 = (bf16[112,256]{1,0:T(8,128)(2,1)S(1)}, bf16[112,256]{1,0:T(8,128)(2,1)S(1)}, u32[]{:S(2)}, u32[]{:S(2)}) collective-permute-start(bf16[112,256]{1,0:T(8,128)(2,1)S(1)} %add_convert_fusion.1), channel_id=1, source_target_pairs={{0,192},{64,128},{128,64},{192,0},{1,193},{65,129},{129,65},{193,1... | collective-permute-start | bytes 172040 | tf_op jit(solution)/shard_map/ppermute | solution.py:322
  109.5 3.9 %collective-permute-start.9 = (bf16[112,256]{1,0:T(8,128)(2,1)S(1)}, bf16[112,256]{1,0:T(8,128)(2,1)S(1)}, u32[]{:S(2)}, u32[]{:S(2)}) collective-permute-start(bf16[112,256]{1,0:T(8,128)(2,1)S(1)} %add_convert_fusion.1), channel_id=1, source_target_pairs={{0,64},{64,0},{128,192},{192,128},{1,65},{65,1},{129,193},{193,129... | collective-permute-start | bytes 172040 | tf_op jit(solution)/shard_map/ppermute | solution.py:322
  113.5 5.9 %collective-permute-start.12 = (bf16[384,256]{1,0:T(8,128)(2,1)S(1)}, bf16[384,256]{1,0:T(8,128)(2,1)S(1)}, u32[]{:S(2)}, u32[]{:S(2)}) collective-permute-start(bf16[384,256]{1,0:T(8,128)(2,1)S(1)} %bitcast.24), channel_id=1, source_target_pairs={{0,4},{4,0},{1,5},{5,1},{2,6},{6,2},{3,7},{7,3},{8,12},{12,8},{9,1... | collective-permute-start | bytes 589832 | tf_op jit(solution)/shard_map/ppermute | solution.py:322

commit v6 on v5

--- a/solution.py
+++ b/solution.py
@@ -20,8 +20,8 @@
 BLOCK = 384
 STEP = 64
 SLOTS = PART + 16
-VMEM_LIMIT = 42 * 1024 * 1024
-M1, TA, TB, TC = 256, 640, 640, 640
+VMEM_LIMIT = 52 * 1024 * 1024
+M1, TA, TB, TC = 640, 640, 640, 640
 SA, SB, SC = 64, 320, 320
 NN = (((1,), (0,)), ((), ()))
 NT = (((1,), (1,)), ((), ()))

time: 121 us -> 121 us (level)
  starting transfers between devices: 41.7 us -> 44.5 us
  waiting for transfers between devices: 35.7 us -> 33.5 us
  local copies, waits for them, and re-layouts: 7.65 us -> 6.06 us
    ppermute x10, starting transfers between devices: 18.6 us -> 22.6 us  [flip(): return lax.ppermute(value, axis, [(i, i ^ k) for i in range(size)])]
    unnamed x27 -> x23, local copies, waits for them, and re-layouts: 4.81 us -> 2.15 us
    convert_element_type x1, other arithmetic: 1.23 us -> 2.74 us  [reduce_grads(): chunks = (keep + flip(send, 'c', C, 1).astype(f32)).astype(bf)]
    ppermute x3, starting transfers between devices: 7.76 us -> 6.52 us  [turn(): return lax.ppermute(value, axis, [(i, (i + k) % size) for i in range(size)])]
    ppermute x10, waiting for transfers between devices: 20.1 us -> 18.9 us  [flip(): return lax.ppermute(value, axis, [(i, i ^ k) for i in range(size)])]
  transfers between devices with their start and end apart: 15 -> 15, of which waited for: 10 -> 12; matrix products, arithmetic and copies ran while one was open for 7% -> 7% of each run, Pallas kernels for 1% -> 1%
where the time goes in v6:
time: 121 us
  starting transfers between devices  44.5 us (37%)
  waiting for transfers between devices  33.5 us (28%)
  Pallas kernels  27.4 us (23%)
  other arithmetic  8.41 us (7%)
  local copies, waits for them, and re-layouts  6.06 us (5%)
    pallas_call x1, Pallas kernels, encoder(): pl.pallas_call(encoder_kernel, out_shape=(jax.ShapeDtypeStruct((total, WI...  25.7 us
    ppermute x10, starting transfers between devices, flip(): return lax.ppermute(value, axis, [(i, i ^ k) for i in range(size)])  22.6 us
    ppermute x10, waiting for transfers between devices, flip(): return lax.ppermute(value, axis, [(i, i ^ k) for i in range(size)])  18.9 us
    all_to_all x2, starting transfers between devices, exchange(): return lax.all_to_all(chunks, axes, 0, 0, tiled=True)  15.4 us
    all_to_all x2, waiting for transfers between devices, exchange(): return lax.all_to_all(chunks, axes, 0, 0, tiled=True)  12.5 us
    ppermute x3, starting transfers between devices, turn(): return lax.ppermute(value, axis, [(i, (i + k) % size) for i in range(size)])  6.52 us
    mul x1, other arithmetic, body(): masked = cotangent * frame_mask[:, :, None].astype(bf)  3.35 us
    convert_element_type x1, other arithmetic, reduce_grads(): chunks = (keep + flip(send, 'c', C, 1).astype(f32)).astype(bf)  2.74 us
  transfers between devices with their start and end apart: 15, of which 12 were waited for; matrix products, arithmetic and copies ran while one was open for 7% of the time, Pallas kernels for 1%

profile of v6, /device:TPU:1, one launch (start us, length us, event | category | flops | bytes accessed | tf_op | source)
XLA Modules:
  0.0 120.7 jit_solution(5389185832293992254)
XLA Ops:
  0.7 1.0 copy-done
  1.6 2.1 %collective-permute-start = (bf16[192,512]{1,0:T(8,128)(2,1)S(1)}, bf16[192,512]{1,0:T(8,128)(2,1)S(1)}, u32[]{:S(2)}, u32[]{:S(2)}) collective-permute-start(bf16[192,512]{1,0:T(8,128)(2,1)S(1)} %constant_dynamic-slice_fusion.4), channel_id=1, source_target_pairs={{0,1},{1,0},{2,3},{3,2},{4,5},{5,4},{6,7},{7,6},{8,9},{9,8},{10,11... | collective-permute-start | bytes 589832 | tf_op jit(solution)/shard_map/ppermute | solution.py:322
  3.8 1.7 %pack.1 = bf16[32,2,6528]{2,1,0:T(2,128)(2,1)} custom-call(s32[2]{0:T(128)} %lengths_ref.1, bf16[2,6400]{1,0:T(2,128)(2,1)} %wave_ref.1), custom_call_target="tpu_custom_call" | custom-call | tf_op jit(solution)/shard_map/pack/pallas_call | solution.py:308
  5.5 11.2 %all-to-all-start = ((bf16[32,2,6528]{2,1,0:T(2,128)(2,1)}), bf16[32,2,6528]{2,1,0:T(2,128)(2,1)S(1)}, u32[]{:S(2)}, u32[]{:S(2)}) async-start(bf16[32,2,6528]{2,1,0:T(2,128)(2,1)} %pack.1), calls=%async_computation | async-start | bytes 1671168 | tf_op jit(solution)/shard_map/all_to_all | solution.py:330
  16.9 3.4 %broadcast_multiply_fusion = bf16[2,639,512]{2,0,1:T(2,128)(2,1)S(1)} fusion(bf16[2,639,512]{2,0,1:T(2,128)(2,1)} %param.15, bf16[2,639]{0,1:T(8,128)(2,1)S(1)} %copy.14), kind=kLoop, calls=%fused_computation.2 | loop fusion | flops 654336 | bytes 2619900 | tf_op jit(solution)/shard_map/mul | solution.py:359
  20.7 1.2 pad.12.clone
  22.0 2.5 %collective-permute-start.1 = (bf16[384,512]{1,0:T(8,128)(2,1)S(1)}, bf16[384,512]{1,0:T(8,128)(2,1)S(1)}, u32[]{:S(2)}, u32[]{:S(2)}) collective-permute-start(bf16[384,512]{1,0:T(8,128)(2,1)S(1)} %pad_maximum_fusion.1), channel_id=1, source_target_pairs={{0,2},{1,3},{2,0},{3,1},{4,6},{5,7},{6,4},{7,5},{8,10},{9,11},{10,... | collective-permute-start | bytes 1179656 | tf_op jit(solution)/shard_map/ppermute | solution.py:322
  24.7 8.3 %collective-permute-done.1 = bf16[384,512]{1,0:T(8,128)(2,1)S(1)} collective-permute-done((bf16[384,512]{1,0:T(8,128)(2,1)S(1)}, bf16[384,512]{1,0:T(8,128)(2,1)S(1)}, u32[]{:S(2)}, u32[]{:S(2)}) %collective-permute-start.1) | collective-permute-done | bytes 393248 | tf_op jit(solution)/shard_map/ppermute | solution.py:322
  33.1 2.2 %collective-permute-start.2 = (bf16[768,512]{1,0:T(8,128)(2,1)S(1)}, bf16[768,512]{1,0:T(8,128)(2,1)S(1)}, u32[]{:S(2)}, u32[]{:S(2)}) collective-permute-start(bf16[768,512]{1,0:T(8,128)(2,1)S(1)} %pad_maximum_fusion.mine_hbm), channel_id=1, source_target_pairs={{0,4},{4,0},{1,5},{5,1},{2,6},{6,2},{3,7},{7,3},{8,12},{12,8},{9,1... | collective-permute-start | bytes 2359304 | tf_op jit(solution)/shard_map/ppermute | solution.py:322
  35.5 1.7 %collective-permute-done.2.theirs_hbm = bf16[768,512]{1,0:T(8,128)(2,1)S(1)} collective-permute-done((bf16[768,512]{1,0:T(8,128)(2,1)S(1)}, bf16[768,512]{1,0:T(8,128)(2,1)S(1)}, u32[]{:S(2)}, u32[]{:S(2)}) %collective-permute-start.2) | collective-permute-done | bytes 786464 | tf_op jit(solution)/shard_map/ppermute | solution.py:322
  37.2 4.8 %collective-permute-start.3 = (bf16[32,2,6528]{2,1,0:T(2,128)(2,1)S(1)}, bf16[32,2,6528]{2,1,0:T(2,128)(2,1)S(1)}, u32[]{:S(2)}, u32[]{:S(2)}) collective-permute-start(bf16[32,2,6528]{2,1,0:T(2,128)(2,1)S(1)} %all-to-all-done.own_hbm), channel_id=1, source_target_pairs={{0,4},{4,0},{1,5},{5,1},{2,6},{6,2},{3,7},{7,3},{8,12},{12,8},{9,1... | collective-permute-start | bytes 2506760 | tf_op jit(solution)/shard_map/ppermute | solution.py:322
  42.1 2.0 %collective-permute-done.3.other_hbm = bf16[32,2,6528]{2,1,0:T(2,128)(2,1)S(1)} collective-permute-done((bf16[32,2,6528]{2,1,0:T(2,128)(2,1)S(1)}, bf16[32,2,6528]{2,1,0:T(2,128)(2,1)S(1)}, u32[]{:S(2)}, u32[]{:S(2)}) %collective-permute-start.3) | collective-permute-done | bytes 835616 | tf_op jit(solution)/shard_map/ppermute | solution.py:322
  44.1 0.9 copy-done.4
  45.0 25.7 %encoder.1 = (bf16[1280,512]{1,0:T(8,128)(2,1)}, f32[16,112,256]{2,1,0:T(8,128)}, bf16[16,112,256]{2,1,0:T(8,128)(2,1)}) custom-call(s32[2]{0:T(128)S(1)} %pad_add_fusion.ids_ref, s32[2]{0:T(128)S(1)} %copy-done.1, bf16[96,1024]{1,0:T(8,128)(2,1)S(1)} %pad_maximum_fusion.6.wc_ref, f32[8,512]{1,0:T(8,128)S(1)} %concatenate.33.par_ref, ...), custom_call_target="tpu_custom_call" | custom-call | tf_op jit(solution)/shard_map/encoder/pallas_call | solution.py:252
  71.2 2.3 %collective-permute-done.4 = bf16[16,112,256]{2,1,0:T(8,128)(2,1)S(1)} collective-permute-done((bf16[16,112,256]{2,1,0:T(8,128)(2,1)}, bf16[16,112,256]{2,1,0:T(8,128)(2,1)S(1)}, u32[]{:S(2)}, u32[]{:S(2)}) %collective-permute-start.4) | collective-permute-done | bytes 917536 | tf_op jit(solution)/shard_map/ppermute | solution.py:322
  73.5 2.7 %add_convert_fusion = bf16[16,112,256]{2,1,0:T(8,128)(2,1)} fusion(f32[16,112,256]{2,1,0:T(8,128)} %get-tuple-element.22, bf16[16,112,256]{2,1,0:T(8,128)(2,1)S(1)} %collective-permute-done.4), kind=kLoop, calls=%fused_computation | loop fusion | flops 1376256 | bytes 3670016 | tf_op jit(solution)/shard_map/convert_element_type | solution.py:334
  76.2 4.2 %all-to-all-start.1 = ((bf16[16,112,256]{2,1,0:T(8,128)(2,1)}), bf16[16,112,256]{2,1,0:T(8,128)(2,1)S(1)}, u32[]{:S(2)}, u32[]{:S(2)}) async-start(bf16[16,112,256]{2,1,0:T(8,128)(2,1)} %add_convert_fusion), calls=%async_computation.1 | async-start | bytes 1835008 | tf_op jit(solution)/shard_map/all_to_all | solution.py:330
  80.4 2.4 %copy.17 = bf16[2,639,512]{2,0,1:T(2,128)(2,1)} copy(bf16[2,639,512]{2,1,0:T(8,128)(2,1)S(1)} %bitcast.23) | data formatting | bytes 2617344 | tf_op jit(solution)/shard_map/optimization_barrier | solution.py:336
  82.8 12.5 %all-to-all-done.1 = bf16[16,112,256]{2,1,0:T(8,128)(2,1)S(1)} async-done(((bf16[16,112,256]{2,1,0:T(8,128)(2,1)}), bf16[16,112,256]{2,1,0:T(8,128)(2,1)S(1)}, u32[]{:S(2)}, u32[]{:S(2)}) %all-to-all-start.1) | async-done | bytes 917536 | tf_op jit(solution)/shard_map/all_to_all | solution.py:330
  95.5 2.9 %collective-permute-start.5 = (bf16[112,256]{1,0:T(8,128)(2,1)S(1)}, bf16[112,256]{1,0:T(8,128)(2,1)S(1)}, u32[]{:S(2)}, u32[]{:S(2)}) collective-permute-start(bf16[112,256]{1,0:T(8,128)(2,1)S(1)} %reduce_sum.22), channel_id=1, source_target_pairs={{0,32},{8,40},{16,48},{24,56},{32,0},{40,8},{48,16},{56,24},{1,33}... | collective-permute-start | bytes 172040 | tf_op jit(solution)/shard_map/ppermute | solution.py:326
  98.4 1.0 collective-permute-start.6
  99.4 2.6 %collective-permute-start.7 = (bf16[112,256]{1,0:T(8,128)(2,1)S(1)}, bf16[112,256]{1,0:T(8,128)(2,1)S(1)}, u32[]{:S(2)}, u32[]{:S(2)}) collective-permute-start(bf16[112,256]{1,0:T(8,128)(2,1)S(1)} %reduce_sum.22), channel_id=1, source_target_pairs={{0,48},{8,56},{16,0},{24,8},{32,16},{40,24},{48,32},{56,40},{1,49}... | collective-permute-start | bytes 172040 | tf_op jit(solution)/shard_map/ppermute | solution.py:326
  102.0 0.7 collective-permute-done.5
  102.7 1.1 collective-permute-done.6
  104.2 2.8 %collective-permute-start.8 = (bf16[112,256]{1,0:T(8,128)(2,1)S(1)}, bf16[112,256]{1,0:T(8,128)(2,1)S(1)}, u32[]{:S(2)}, u32[]{:S(2)}) collective-permute-start(bf16[112,256]{1,0:T(8,128)(2,1)S(1)} %add_convert_fusion.2), channel_id=1, source_target_pairs={{0,8},{8,0},{16,24},{24,16},{32,40},{40,32},{48,56},{56,48},{1,9},... | collective-permute-start | bytes 172040 | tf_op jit(solution)/shard_map/ppermute | solution.py:322
  107.0 1.6 %collective-permute-done.8 = bf16[112,256]{1,0:T(8,128)(2,1)S(1)} collective-permute-done((bf16[112,256]{1,0:T(8,128)(2,1)S(1)}, bf16[112,256]{1,0:T(8,128)(2,1)S(1)}, u32[]{:S(2)}, u32[]{:S(2)}) %collective-permute-start.8) | collective-permute-done | bytes 57376 | tf_op jit(solution)/shard_map/ppermute | solution.py:322
  108.5 0.7 collective-permute-start.10
  109.2 1.3 %collective-permute-start.11 = (bf16[112,256]{1,0:T(8,128)(2,1)S(1)}, bf16[112,256]{1,0:T(8,128)(2,1)S(1)}, u32[]{:S(2)}, u32[]{:S(2)}) collective-permute-start(bf16[112,256]{1,0:T(8,128)(2,1)S(1)} %add_convert_fusion.1), channel_id=1, source_target_pairs={{0,192},{64,128},{128,64},{192,0},{1,193},{65,129},{129,65},{193,1... | collective-permute-start | bytes 172040 | tf_op jit(solution)/shard_map/ppermute | solution.py:322
  110.5 0.8 collective-permute-start.9
  111.3 1.9 %collective-permute-done.10 = bf16[112,256]{1,0:T(8,128)(2,1)S(1)} collective-permute-done((bf16[112,256]{1,0:T(8,128)(2,1)S(1)}, bf16[112,256]{1,0:T(8,128)(2,1)S(1)}, u32[]{:S(2)}, u32[]{:S(2)}) %collective-permute-start.10) | collective-permute-done | bytes 57376 | tf_op jit(solution)/shard_map/ppermute | solution.py:322
  113.9 4.8 %collective-permute-start.12 = (bf16[384,256]{1,0:T(8,128)(2,1)S(1)}, bf16[384,256]{1,0:T(8,128)(2,1)S(1)}, u32[]{:S(2)}, u32[]{:S(2)}) collective-permute-start(bf16[384,256]{1,0:T(8,128)(2,1)S(1)} %bitcast.24), channel_id=1, source_target_pairs={{0,4},{4,0},{1,5},{5,1},{2,6},{6,2},{3,7},{7,3},{8,12},{12,8},{9,1... | collective-permute-start | bytes 589832 | tf_op jit(solution)/shard_map/ppermute | solution.py:322
  119.7 1.0 fusion
  (53 shorter events, 3.8 us)
Async XLA Ops:
  0.6 1.0 copy-start
  0.6 16.1 %copy-start.6 = (s32[2,639]{1,0:T(2,128)S(1)}, s32[2,639]{1,0:T(2,128)}, u32[]{:S(2)}) copy-start(s32[2,639]{1,0:T(2,128)} %param.14) | copy-start | bytes 15340
  1.6 20.4 %collective-permute-start = (bf16[192,512]{1,0:T(8,128)(2,1)S(1)}, bf16[192,512]{1,0:T(8,128)(2,1)S(1)}, u32[]{:S(2)}, u32[]{:S(2)}) collective-permute-start(bf16[192,512]{1,0:T(8,128)(2,1)S(1)} %constant_dynamic-slice_fusion.4), channel_id=1, source_target_pairs={{0,1},{1,0},{2,3},{3,2},{4,5},{5,4},{6,7},{7,6},{8,9},{9,8},{10,11... | collective-permute-start | bytes 589832 | tf_op jit(solution)/shard_map/ppermute | solution.py:322
  5.5 31.7 %all-to-all-start = ((bf16[32,2,6528]{2,1,0:T(2,128)(2,1)}), bf16[32,2,6528]{2,1,0:T(2,128)(2,1)S(1)}, u32[]{:S(2)}, u32[]{:S(2)}) async-start(bf16[32,2,6528]{2,1,0:T(2,128)(2,1)} %pack.1), calls=%async_computation | async-start | bytes 1671168 | tf_op jit(solution)/shard_map/all_to_all | solution.py:330
  20.5 1.3 %copy-start.7 = (f32[512]{0:T(512)S(1)}, f32[512]{0:T(512)}, u32[]{:S(2)}) copy-start(f32[512]{0:T(512)} %param.17) | copy-start | bytes 6148
  20.5 1.3 %copy-start.8 = (f32[512]{0:T(512)S(1)}, f32[512]{0:T(512)}, u32[]{:S(2)}) copy-start(f32[512]{0:T(512)} %param.18) | copy-start | bytes 6148
  20.5 1.3 %copy-start.9 = (f32[512]{0:T(512)S(1)}, f32[512]{0:T(512)}, u32[]{:S(2)}) copy-start(f32[512]{0:T(512)} %param.20) | copy-start | bytes 6148
  20.5 1.3 %copy-start.10 = (f32[512]{0:T(512)S(1)}, f32[512]{0:T(512)}, u32[]{:S(2)}) copy-start(f32[512]{0:T(512)} %param.21) | copy-start | bytes 6148
  20.6 1.3 %copy-start.5 = (bf16[10,512]{1,0:T(8,128)(2,1)S(1)}, bf16[10,512]{1,0:T(8,128)(2,1)}, u32[]{:S(2)}) copy-start(bf16[10,512]{1,0:T(8,128)(2,1)} %param.16) | copy-start | bytes 30724
  22.0 23.0 %copy-start.1 = (s32[2]{0:T(128)S(1)}, s32[2]{0:T(128)}, u32[]{:S(2)}) copy-start(s32[2]{0:T(128)} %source_ref.1) | copy-start | bytes 28
  22.0 11.0 %collective-permute-start.1 = (bf16[384,512]{1,0:T(8,128)(2,1)S(1)}, bf16[384,512]{1,0:T(8,128)(2,1)S(1)}, u32[]{:S(2)}, u32[]{:S(2)}) collective-permute-start(bf16[384,512]{1,0:T(8,128)(2,1)S(1)} %pad_maximum_fusion.1), channel_id=1, source_target_pairs={{0,2},{1,3},{2,0},{3,1},{4,6},{5,7},{6,4},{7,5},{8,10},{9,11},{10,... | collective-permute-start | bytes 1179656 | tf_op jit(solution)/shard_map/ppermute | solution.py:322
  33.1 4.2 %collective-permute-start.2 = (bf16[768,512]{1,0:T(8,128)(2,1)S(1)}, bf16[768,512]{1,0:T(8,128)(2,1)S(1)}, u32[]{:S(2)}, u32[]{:S(2)}) collective-permute-start(bf16[768,512]{1,0:T(8,128)(2,1)S(1)} %pad_maximum_fusion.mine_hbm), channel_id=1, source_target_pairs={{0,4},{4,0},{1,5},{5,1},{2,6},{6,2},{3,7},{7,3},{8,12},{12,8},{9,1... | collective-permute-start | bytes 2359304 | tf_op jit(solution)/shard_map/ppermute | solution.py:322
  37.2 6.8 %copy-start.2 = (bf16[32,2,6528]{2,1,0:T(2,128)(2,1)}, bf16[32,2,6528]{2,1,0:T(2,128)(2,1)S(1)}, u32[]{:S(2)}) copy-start(bf16[32,2,6528]{2,1,0:T(2,128)(2,1)S(1)} %all-to-all-done.own_hbm) | copy-start | bytes 2506756
  37.2 6.8 %collective-permute-start.3 = (bf16[32,2,6528]{2,1,0:T(2,128)(2,1)S(1)}, bf16[32,2,6528]{2,1,0:T(2,128)(2,1)S(1)}, u32[]{:S(2)}, u32[]{:S(2)}) collective-permute-start(bf16[32,2,6528]{2,1,0:T(2,128)(2,1)S(1)} %all-to-all-done.own_hbm), channel_id=1, source_target_pairs={{0,4},{4,0},{1,5},{5,1},{2,6},{6,2},{3,7},{7,3},{8,12},{12,8},{9,1... | collective-permute-start | bytes 2506760 | tf_op jit(solution)/shard_map/ppermute | solution.py:322
  44.0 0.9 copy-start.4
  70.7 2.8 %collective-permute-start.4 = (bf16[16,112,256]{2,1,0:T(8,128)(2,1)}, bf16[16,112,256]{2,1,0:T(8,128)(2,1)S(1)}, u32[]{:S(2)}, u32[]{:S(2)}) collective-permute-start(bf16[16,112,256]{2,1,0:T(8,128)(2,1)} %get-tuple-element.23), channel_id=1, source_target_pairs={{0,4},{4,0},{1,5},{5,1},{2,6},{6,2},{3,7},{7,3},{8,12},{12,8},{9,1... | collective-permute-start | bytes 2752520 | tf_op jit(solution)/shard_map/ppermute | solution.py:322
  76.2 4.2 %copy-start.3 = (bf16[1280,512]{1,0:T(8,128)(2,1)S(1)}, bf16[1280,512]{1,0:T(8,128)(2,1)}, u32[]{:S(2)}) copy-start(bf16[1280,512]{1,0:T(8,128)(2,1)} %get-tuple-element.24) | copy-start | bytes 3932164
  76.2 19.1 %all-to-all-start.1 = ((bf16[16,112,256]{2,1,0:T(8,128)(2,1)}), bf16[16,112,256]{2,1,0:T(8,128)(2,1)S(1)}, u32[]{:S(2)}, u32[]{:S(2)}) async-start(bf16[16,112,256]{2,1,0:T(8,128)(2,1)} %add_convert_fusion), calls=%async_computation.1 | async-start | bytes 1835008 | tf_op jit(solution)/shard_map/all_to_all | solution.py:330
  95.5 7.2 %collective-permute-start.5 = (bf16[112,256]{1,0:T(8,128)(2,1)S(1)}, bf16[112,256]{1,0:T(8,128)(2,1)S(1)}, u32[]{:S(2)}, u32[]{:S(2)}) collective-permute-start(bf16[112,256]{1,0:T(8,128)(2,1)S(1)} %reduce_sum.22), channel_id=1, source_target_pairs={{0,32},{8,40},{16,48},{24,56},{32,0},{40,8},{48,16},{56,24},{1,33}... | collective-permute-start | bytes 172040 | tf_op jit(solution)/shard_map/ppermute | solution.py:326
  98.4 5.3 %collective-permute-start.6 = (bf16[112,256]{1,0:T(8,128)(2,1)S(1)}, bf16[112,256]{1,0:T(8,128)(2,1)S(1)}, u32[]{:S(2)}, u32[]{:S(2)}) collective-permute-start(bf16[112,256]{1,0:T(8,128)(2,1)S(1)} %reduce_sum.22), channel_id=1, source_target_pairs={{0,16},{8,24},{16,32},{24,40},{32,48},{40,56},{48,0},{56,8},{1,17}... | collective-permute-start | bytes 172040 | tf_op jit(solution)/shard_map/ppermute | solution.py:326
  99.4 4.7 %collective-permute-start.7 = (bf16[112,256]{1,0:T(8,128)(2,1)S(1)}, bf16[112,256]{1,0:T(8,128)(2,1)S(1)}, u32[]{:S(2)}, u32[]{:S(2)}) collective-permute-start(bf16[112,256]{1,0:T(8,128)(2,1)S(1)} %reduce_sum.22), channel_id=1, source_target_pairs={{0,48},{8,56},{16,0},{24,8},{32,16},{40,24},{48,32},{56,40},{1,49}... | collective-permute-start | bytes 172040 | tf_op jit(solution)/shard_map/ppermute | solution.py:326
  104.2 4.4 %collective-permute-start.8 = (bf16[112,256]{1,0:T(8,128)(2,1)S(1)}, bf16[112,256]{1,0:T(8,128)(2,1)S(1)}, u32[]{:S(2)}, u32[]{:S(2)}) collective-permute-start(bf16[112,256]{1,0:T(8,128)(2,1)S(1)} %add_convert_fusion.2), channel_id=1, source_target_pairs={{0,8},{8,0},{16,24},{24,16},{32,40},{40,32},{48,56},{56,48},{1,9},... | collective-permute-start | bytes 172040 | tf_op jit(solution)/shard_map/ppermute | solution.py:322
  108.5 4.7 %collective-permute-start.10 = (bf16[112,256]{1,0:T(8,128)(2,1)S(1)}, bf16[112,256]{1,0:T(8,128)(2,1)S(1)}, u32[]{:S(2)}, u32[]{:S(2)}) collective-permute-start(bf16[112,256]{1,0:T(8,128)(2,1)S(1)} %add_convert_fusion.1), channel_id=1, source_target_pairs={{0,128},{64,192},{128,0},{192,64},{1,129},{65,193},{129,1},{193,65... | collective-permute-start | bytes 172040 | tf_op jit(solution)/shard_map/ppermute | solution.py:322
  109.2 4.6 %collective-permute-start.11 = (bf16[112,256]{1,0:T(8,128)(2,1)S(1)}, bf16[112,256]{1,0:T(8,128)(2,1)S(1)}, u32[]{:S(2)}, u32[]{:S(2)}) collective-permute-start(bf16[112,256]{1,0:T(8,128)(2,1)S(1)} %add_convert_fusion.1), channel_id=1, source_target_pairs={{0,192},{64,128},{128,64},{192,0},{1,193},{65,129},{129,65},{193,1... | collective-permute-start | bytes 172040 | tf_op jit(solution)/shard_map/ppermute | solution.py:322
  110.5 3.3 %collective-permute-start.9 = (bf16[112,256]{1,0:T(8,128)(2,1)S(1)}, bf16[112,256]{1,0:T(8,128)(2,1)S(1)}, u32[]{:S(2)}, u32[]{:S(2)}) collective-permute-start(bf16[112,256]{1,0:T(8,128)(2,1)S(1)} %add_convert_fusion.1), channel_id=1, source_target_pairs={{0,64},{64,0},{128,192},{192,128},{1,65},{65,1},{129,193},{193,129... | collective-permute-start | bytes 172040 | tf_op jit(solution)/shard_map/ppermute | solution.py:322
  113.9 5.9 %collective-permute-start.12 = (bf16[384,256]{1,0:T(8,128)(2,1)S(1)}, bf16[384,256]{1,0:T(8,128)(2,1)S(1)}, u32[]{:S(2)}, u32[]{:S(2)}) collective-permute-start(bf16[384,256]{1,0:T(8,128)(2,1)S(1)} %bitcast.24), channel_id=1, source_target_pairs={{0,4},{4,0},{1,5},{5,1},{2,6},{6,2},{3,7},{7,3},{8,12},{12,8},{9,1... | collective-permute-start | bytes 589832 | tf_op jit(solution)/shard_map/ppermute | solution.py:322
